TPU v7x, 256 devices: a whole 4x4x8 slice. The times are simulated.
256 devices in a mesh: rep: 4 (over z_lo, core), ep: 64 (over y, x, z_hi).
Axes of the slice: x: 4, y: 4, z: 8 (z_hi: 4, z_lo: 2; z = z_hi * 2 + z_lo), core: 2. Of those that a mesh axis runs over, the one named last changes fastest.
Arguments:
- deltas: bfloat16 [4, 64, 2048, 768], P('rep', None, 'ep'), may hold values from -3 to 3
- master: float32 [64, 64, 4, 8, 768], P(None, 'ep', 'rep'), may hold values from -6 to 6
- momentum: float32 [64, 64, 4, 8, 768], P(None, 'ep', 'rep'), may hold values from -3 to 3
- hidden: bfloat16 [4, 8192, 2048], P(None, ('rep', 'ep')), may hold values from -6 to 6
- expert_ids: int32 [4, 8192, 8], P(None, ('rep', 'ep')), may hold values from 0 to 63, as said below
- gate_weights: float32 [4, 8192, 8], P(None, ('rep', 'ep')), may hold values from 0.1 to 0.4
Outputs:
- engine_weights: bfloat16 [64, 2048, 768], P('ep')
- momentum_out: float32 [64, 64, 4, 8, 768], P(None, 'ep', 'rep')
- decoded: bfloat16 [4, 8192, 768], P(None, ('rep', 'ep'))
Inputs may be any that keep to these rules, and one draw needn't show every extreme that they name: `expert_ids`: in every step, each row names 8 different experts; among the 32 rows of one device no expert is named by more than 6 rows, and on every device in every step some expert is named by exactly 6 rows.
All inputs are finite; a program needn't handle non-finite values.
Results may differ from a plain program's by a relative error of at most 0.013.
Values may be sent and summed in bfloat16 or wider, within the bound.
No kernel may reach another device: no remote copies, remote signals or barrier semaphores. Data moves between devices by JAX's collectives and lax.ppermute only.
A program may use at most 128 MiB of HBM per device.

v0:
```python
import functools
import math

import jax
import jax.numpy as jnp
from jax import lax
from jax.experimental import pallas as pl
from jax.experimental.layout import Layout, with_layout_constraint
from jax.experimental.pallas import tpu as pltpu
from jax.sharding import Mesh, PartitionSpec as P

outer_momentum = 0.9
outer_rate = 0.7

RING = 4
LANES = 128
CAP = 6
GROUPS = 8
PLUS = [(i, (i + 1) % RING) for i in range(RING)]
MINUS = [(i, (i - 1) % RING) for i in range(RING)]
CHIPS = 8
Z = ("z_lo", "z_hi")
UP = [(i % 2 * RING + i // 2, (i + 1) % CHIPS % 2 * RING + (i + 1) % CHIPS // 2) for i in range(CHIPS)]
DOWN = [(after, before) for before, after in UP]
SWAP = [(0, 1), (1, 0)]


def swap(value, axis):
    return lax.ppermute(value, axis, SWAP)


def later(value, *first):
    return lax.optimization_barrier((value,) + first)[0]


def neighbours(value, axis):
    return lax.ppermute(value, axis, PLUS), lax.ppermute(value, axis, MINUS)


def forward(before, after, axis):
    half = before.shape[0] // 2
    low = lax.ppermute(before[:half], axis, PLUS)
    high = lax.ppermute(after[half:], axis, MINUS)
    return jnp.concatenate([low, high])


def far_sums(before, after, far, axis):
    half = far.shape[0] // 2
    low = lax.ppermute(far[:half].astype(jnp.bfloat16), axis, PLUS)
    high = lax.ppermute(far[half:].astype(jnp.bfloat16), axis, MINUS)
    after = jnp.concatenate([after[:half] + low.astype(jnp.float32), after[half:]])
    before = jnp.concatenate([before[:half], before[half:] + high.astype(jnp.float32)])
    return before.astype(jnp.bfloat16), after.astype(jnp.bfloat16)


def near_sums(own, before, after, axis):
    from_before = lax.ppermute(after, axis, PLUS)
    from_after = lax.ppermute(before, axis, MINUS)
    return own + from_before.astype(jnp.float32) + from_after.astype(jnp.float32)


def by_core(core, mine, other, axis):
    return jnp.where(
        core == 0,
        jnp.concatenate([mine, other], axis=axis),
        jnp.concatenate([other, mine], axis=axis),
    )


def rounded(value):
    return lax.reduce_precision(value, exponent_bits=8, mantissa_bits=7)


def pack_kernel(top, where_ref, row_ref, low_ref, high_ref, spread_ref):
    count, model, slots = row_ref.shape[0], low_ref.shape[2], low_ref.shape[1]
    wide = RING * slots
    routing = row_ref[:, model : model + LANES].astype(jnp.float32)
    place = jnp.where(routing[:, :top] == where_ref[0].astype(jnp.float32), routing[:, top : 2 * top], -wide - 1.0)
    lane = lax.broadcasted_iota(jnp.int32, (count, 2 * wide), 1).astype(jnp.float32)
    spread = jnp.zeros((count, 2 * wide), jnp.float32)
    placed = jnp.zeros((count, wide), jnp.float32)
    for choice in range(top):
        here = place[:, choice : choice + 1]
        high = routing[:, 2 * top + choice : 2 * top + choice + 1]
        rest = routing[:, 3 * top + choice : 3 * top + choice + 1]
        spread = jnp.where(lane == here, high, jnp.where(lane == here + wide, rest, spread))
        placed = jnp.where(lane[:, :wide] == here, 1.0, placed)
    spread_ref[...] = spread.astype(jnp.bfloat16)
    packed = lax.dot_general(
        placed.astype(jnp.bfloat16),
        row_ref[:, :model],
        (((0,), (0,)), ((), ())),
        preferred_element_type=jnp.float32,
    ).astype(jnp.bfloat16)
    for offset in range(RING):
        (low_ref, high_ref)[offset // 2][offset % 2] = packed[offset * slots : (offset + 1) * slots]


def pack(where, plane, model, top, rows):
    count, columns = plane.shape
    tile = GROUPS * rows
    tiles = count // tile
    slots = GROUPS * CAP
    return pl.pallas_call(
        functools.partial(pack_kernel, top),
        grid=(tiles,),
        in_specs=[
            pl.BlockSpec(memory_space=pltpu.SMEM),
            pl.BlockSpec((tile, columns), lambda i: (i, 0)),
        ],
        out_specs=[pl.BlockSpec((2, slots, model), lambda i: (0, i, 0))] * 2
        + [pl.BlockSpec((tile, 2 * RING * slots), lambda i: (i, 0))],
        out_shape=[jax.ShapeDtypeStruct((2, tiles * slots, model), jnp.bfloat16)] * 2
        + [jax.ShapeDtypeStruct((count, 2 * RING * slots), jnp.bfloat16)],
        compiler_params=pltpu.CompilerParams(vmem_limit_bytes=18 * 2**20),
        cost_estimate=pl.CostEstimate(
            flops=2 * count * RING * slots * model,
            bytes_accessed=2 * count * columns + 2 * tiles * slots * RING * model,
            transcendentals=0,
        ),
    )(where, plane)


def answers_kernel(scale, own_ref, other_ref, weight_ref, out_ref):
    count = own_ref.shape[1]
    for side, ref in enumerate((own_ref, other_ref)):
        product = jnp.dot(ref[0], weight_ref[...], preferred_element_type=jnp.float32)
        value = product * scale
        out_ref[0, side * count : (side + 1) * count] = (value + value * jnp.tanh(value)).astype(jnp.bfloat16)


def answers_of(packed, weight, first):
    pairs, count, model = packed[0].shape
    wide = weight.shape[1] // RING
    return pl.pallas_call(
        functools.partial(answers_kernel, 0.5 / math.sqrt(model)),
        grid=(pairs,),
        in_specs=[pl.BlockSpec((1, count, model), lambda i: (i, 0, 0))] * 2
        + [pl.BlockSpec((model, wide), lambda i: (0, first + i))],
        out_specs=pl.BlockSpec((1, 2 * count, wide), lambda i: (i, 0, 0)),
        out_shape=jax.ShapeDtypeStruct((pairs, 2 * count, wide), jnp.bfloat16),
        compiler_params=pltpu.CompilerParams(vmem_limit_bytes=18 * 2**20),
        cost_estimate=pl.CostEstimate(
            flops=4 * pairs * count * model * wide,
            bytes_accessed=4 * pairs * count * (model + wide) + 2 * model * pairs * wide,
            transcendentals=2 * pairs * count * wide,
        ),
    )(*packed, weight)


def unpack_kernel(rows, where_ref, own_ref, other_ref, own_low_ref, own_high_ref, other_low_ref, other_high_ref, out_ref):
    slots = GROUPS * CAP
    tile = GROUPS * rows
    sides = (own_ref, own_low_ref, own_high_ref), (other_ref, other_low_ref, other_high_ref)
    for side, (spread_ref, *answers) in enumerate(sides):
        count = spread_ref.shape[0]
        for part in range(count // tile):
            held = [ref[i, part * slots : (part + 1) * slots] for ref in answers for i in range(2)]
            out = jnp.dot(
                spread_ref[part * tile : (part + 1) * tile],
                jnp.concatenate(held + held),
                preferred_element_type=jnp.float32,
            )
            start = side * count + part * tile
            out_ref[0, start : start + tile] = out.astype(out_ref.dtype)


def unpack(where, spreads, answers, part, rows, dtype):
    blocks = where.shape[0]
    count, wide = spreads[0].shape[0] // RING, spreads[0].shape[1]
    slots, columns = answers[0].shape[1] // (2 * RING), part[1] - part[0]
    column = part[0] // columns
    return pl.pallas_call(
        functools.partial(unpack_kernel, rows),
        grid_spec=pltpu.PrefetchScalarGridSpec(
            num_scalar_prefetch=1,
            grid=(blocks,),
            in_specs=[pl.BlockSpec((count, wide), lambda i, where: (where[i], 0))] * 2
            + [pl.BlockSpec((2, slots, columns), lambda i, where: (0, where[i], column))] * 2
            + [pl.BlockSpec((2, slots, columns), lambda i, where: (0, RING + where[i], column))] * 2,
            out_specs=pl.BlockSpec((1, 2 * count, columns), lambda i, where: (i, 0, 0)),
        ),
        out_shape=jax.ShapeDtypeStruct((blocks, 2 * count, columns), dtype),
        compiler_params=pltpu.CompilerParams(vmem_limit_bytes=18 * 2**20),
        cost_estimate=pl.CostEstimate(
            flops=4 * blocks * count * wide * columns,
            bytes_accessed=4 * blocks * count * (wide + 2 * columns),
            transcendentals=0,
        ),
    )(where, *spreads, *answers, *answers)


def local(deltas, master, momentum, hidden, expert_ids, gate_weights):
    experts, block_rows, width = deltas.shape[1:]
    sub = master.shape[3]
    steps, rows, model = hidden.shape
    top = expert_ids.shape[2]
    z_lo, core = lax.axis_index("z_lo"), lax.axis_index("core")
    y, x, z_hi = lax.axis_index("y"), lax.axis_index("x"), lax.axis_index("z_hi")
    z = z_hi * 2 + z_lo
    taken = steps * rows
    owners = RING * RING
    span = owners * sub
    half_width = width // 2
    cut = 2 * half_width // 3
    parts = [(0, cut), (cut, half_width)]

    pieces = deltas[0].reshape(experts, 2, 2, sub, width)
    kept = lax.dynamic_index_in_dim(pieces, core, axis=2, keepdims=False)
    given = lax.dynamic_index_in_dim(pieces, 1 - core, axis=2, keepdims=False)
    pair = kept.astype(jnp.float32) + swap(given, "core").astype(jnp.float32)
    kept = lax.dynamic_index_in_dim(pair, z_lo, axis=1, keepdims=False)
    given = lax.dynamic_index_in_dim(pair, 1 - z_lo, axis=1, keepdims=False).astype(jnp.bfloat16)
    received = swap(given, "z_lo")
    hidden, expert_ids, gate_weights = [
        later(value, given) for value in (hidden, expert_ids, gate_weights)
    ]

    named = (expert_ids.reshape(taken, top)[:, :, None] == jnp.arange(experts)).astype(jnp.float32)
    row = jnp.arange(taken)
    earlier = (row[:, None] // rows == row // rows) & (row[:, None] > row)
    rank = jnp.dot(
        earlier.astype(jnp.bfloat16),
        jnp.sum(named, axis=1).astype(jnp.bfloat16),
        preferred_element_type=jnp.float32,
    )
    rank = jnp.sum(named * rank[:, None], axis=2).astype(jnp.int32).reshape(expert_ids.shape)
    group = (x % 2) * steps + jnp.arange(steps, dtype=jnp.int32)[:, None, None]
    slot = expert_ids % RING * (GROUPS * CAP) + group * CAP + rank
    gate_high = rounded(gate_weights)
    routing = jnp.concatenate(
        [(expert_ids // RING).astype(jnp.float32), slot.astype(jnp.float32), gate_high, gate_weights - gate_high],
        axis=-1,
    ).astype(jnp.bfloat16)
    routing = jnp.pad(routing.reshape(taken, 4 * top), ((0, 0), (0, LANES - 4 * top)))
    place = jnp.arange(model, dtype=jnp.int32)
    ring_z = (z - 3 + place // (2 * span)) % CHIPS
    source = (place // sub % owners) * RING + ring_z // 2
    source = source * block_rows + (ring_z % 2) * 2 * sub + (place // span % 2) * sub + place % sub
    ordering = (jnp.arange(model, dtype=jnp.int32)[:, None] == source[None, :]).astype(jnp.bfloat16)
    flat = jnp.dot(
        hidden.reshape(taken, model), ordering, preferred_element_type=jnp.float32
    ).astype(jnp.bfloat16)
    flat = jnp.concatenate([flat, routing], axis=1)
    flat = with_layout_constraint(flat, Layout(major_to_minor=(0, 1)))

    plane = lax.all_gather(flat, ("y", "x"), axis=0, tiled=True)
    params = master.reshape(experts, sub, width)
    velocity_old = momentum.reshape(experts, sub, width)
    outer_grad = (kept + received.astype(jnp.float32)) / 4
    velocity = outer_momentum * velocity_old + outer_grad
    piece = (params - outer_rate * (outer_grad + outer_momentum * velocity)).astype(jnp.bfloat16)

    piece = piece.reshape(owners, RING, sub, 2, half_width).transpose(0, 2, 3, 1, 4)
    piece = piece.reshape(owners, sub, 2 * RING * half_width)
    piece = lax.all_to_all(piece, ("y", "x"), split_axis=0, concat_axis=0, tiled=True)
    piece = piece.reshape(span, 2 * RING * half_width)
    mine = lax.dynamic_slice_in_dim(piece, core * RING * half_width, RING * half_width, axis=1)
    other = lax.dynamic_slice_in_dim(piece, (1 - core) * RING * half_width, RING * half_width, axis=1)
    piece = by_core(core, mine, swap(other, "core"), 0)

    def hop(up, down):
        return lax.ppermute(up, Z, UP), lax.ppermute(down, Z, DOWN)

    hops = [(piece, piece)]
    for _ in range(3):
        hops.append(hop(*hops[-1]))
    here = (y * RING + x).reshape(1)
    packed = pack(here, later(plane, *hops[2]), model, top, rows)
    up, down, _ = lax.optimization_barrier((*hops[3], packed[0]))
    low, high = hop(up[:span], down[span:])
    (up1, down1), (up2, down2), (up3, down3) = hops[1:]
    weight = jnp.concatenate([up3, up2, up1, piece, down1, down2, down3, low, high])

    *packed, spread = packed
    packed = [(part, swap(part, "core")) for part in packed]
    spreads = (spread, swap(spread, "core"))

    answers = [answers_of(part, weight, 2 * index) for index, part in enumerate(packed)]
    far_block = ((y + 2) % RING).reshape(1)
    near_blocks = (y + jnp.array([3, 1, 0], jnp.int32)) % RING

    def far_terms(answers, part):
        return unpack(far_block, spreads, answers, part, rows, jnp.bfloat16)[0]

    def near_terms(answers, part):
        return unpack(near_blocks, spreads, answers, part, rows, jnp.float32)

    def to_rows(ringed):
        wide = ringed.shape[1]
        ringed = ringed.reshape(2, RING, taken, wide)
        own, before, after, far = [
            lax.dynamic_index_in_dim(ringed, (x + offset) % RING, axis=1, keepdims=False)
            for offset in (0, 3, 1, 2)
        ]
        received = [
            lax.ppermute(far.astype(jnp.bfloat16), "x", [(i, (i + 2) % RING) for i in range(RING)]),
            lax.ppermute(after.astype(jnp.bfloat16), "x", PLUS),
            lax.ppermute(before.astype(jnp.bfloat16), "x", MINUS),
        ]
        for value in received:
            own = own + value.astype(jnp.float32)
        return own[0], swap(own[1].astype(jnp.bfloat16), "core").astype(jnp.float32)

    far = far_terms(answers, parts[0])
    near = near_terms([answers[0], later(answers[1], far)], parts[0])
    answers = [answers[0], later(answers[1], near)]
    before, after = far_sums(near[0], near[1], far, "y")
    mine_a, other_a = to_rows(near_sums(near[2], before, after, "y"))
    far = far_terms(answers, parts[1])
    near = near_terms([answers[0], later(answers[1], far)], parts[1])
    before, after = far_sums(near[0], near[1], far, "y")
    own = near[2]
    mine_b, other_b = to_rows(near_sums(own, before, after, "y"))

    mine = lax.dynamic_slice_in_dim(weight, z_hi * half_width, half_width, axis=1)
    mine = later(mine, own)
    engine = by_core(core, mine, swap(mine, "core"), 1)
    engine = engine.reshape(CHIPS, 2, owners, sub, width)
    engine = jnp.concatenate([engine, engine])
    engine = lax.dynamic_slice_in_dim(engine, (CHIPS + 3 - z) % CHIPS, CHIPS, axis=0)
    engine = engine.transpose(2, 0, 1, 3, 4).reshape(model, width)

    mine = jnp.concatenate([mine_a, mine_b], axis=1)
    other = jnp.concatenate([other_a, other_b], axis=1)
    decoded = by_core(core, mine, other, 1).reshape(steps, rows, width).astype(jnp.bfloat16)
    return (engine[None], velocity.reshape(momentum.shape), decoded)


def solution(mesh):
    fine = Mesh(
        mesh.devices.reshape(2, 2, RING, RING, RING), ("z_lo", "core", "y", "x", "z_hi")
    )
    rep, ep = ("z_lo", "core"), ("y", "x", "z_hi")
    return jax.shard_map(
        local,
        mesh=fine,
        in_specs=(
            P(rep, None, ep, None),
            P(None, ep, rep, None, None),
            P(None, ep, rep, None, None),
            P(None, rep + ep, None),
            P(None, rep + ep, None),
            P(None, rep + ep, None),
        ),
        out_specs=(
            P(ep, None, None),
            P(None, ep, rep, None, None),
            P(None, rep + ep, None),
        ),
        check_vma=False,
    )
```

profile of v0, /device:TPU:102, one launch (start us, length us, event | category | flops | bytes accessed | tf_op | source)
XLA Modules:
  0.0 230.3 jit_solution(16024084296508409394)
XLA Ops:
  7.2 1.6 dynamic-slice_bitcast_fusion
  9.0 3.4 %collective-permute-done = bf16[64,2,8,768]{3,2,1,0:T(8,128)(2,1)} collective-permute-done((bf16[64,2,8,768]{3,2,1,0:T(8,128)(2,1)S(1)}, bf16[64,2,8,768]{3,2,1,0:T(8,128)(2,1)}, u32[]{:S(2)}, u32[]{:S(2)}) %collective-permute-start) | collective-permute-done | bytes 1572896 | tf_op jit(solution)/shard_map/ppermute | solution.py:29
  12.4 2.3 %convert_add_fusion = f32[64,2,8,768]{3,2,1,0:T(8,128)S(1)} fusion(bf16[64,2,8,768]{3,2,1,0:T(8,128)(2,1)} %collective-permute-done, bf16[64,2,2,8,768]{4,3,2,1,0:T(8,128)(2,1)} %bitcast.176, s32[]{:T(128)S(6)} %select_n.217), kind=kLoop, calls=%fused_computation.8 | loop fusion | flops 2359296 | bytes 6291460 | tf_op jit(solution)/shard_map/add | solution.py:211
  14.8 1.7 copy-done.3
  16.9 0.2 fusion.34
  17.6 3.5 %fusion.4 = bf16[128,2048]{1,0:T(8,128)(2,1)S(1)} fusion(bf16[128,2048]{1,0:T(8,128)(2,1)S(1)} %bitcast.171, s32[2048]{0:T(1024)S(1)} %fusion.62), kind=kOutput, calls=%fused_computation.9 | convolution fusion | flops 1078198272 | bytes 1056768 | tf_op jit(solution)/shard_map/dot_general | solution.py:241
  21.2 0.8 fusion.11
  22.0 0.2 collective-permute-start.1
  22.2 19.6 %collective-permute-done.1 = bf16[64,8,768]{2,1,0:T(8,128)(2,1)} collective-permute-done((bf16[64,8,768]{2,1,0:T(8,128)(2,1)S(1)}, bf16[64,8,768]{2,1,0:T(8,128)(2,1)}, u32[]{:S(2)}, u32[]{:S(2)}) %collective-permute-start.1) | collective-permute-done | bytes 786464 | tf_op jit(solution)/shard_map/ppermute | solution.py:29
  41.8 3.8 %fusion.17 = (f32[64,1,1,8,768]{4,3,2,1,0:T(8,128)}, bf16[64,8,768]{2,1,0:T(8,128)(2,1)S(1)}) fusion(bf16[64,8,768]{2,1,0:T(8,128)(2,1)} %collective-permute-done.1, f32[64,2,8,768]{3,2,1,0:T(8,128)} %copy-done.3, s32[]{:T(128)S(6)} %select_n.219, f32[64,1,1,8,768]{4,3,2,1,0:T(8,128)S(1)} %copy-done.4, f32[64,1,1,8,768]{4,3,2,1,0:T(8,128)} %param.8), kind=kLoop, calls=%fused_computation.38 | loop fusion | flops 3932160 | bytes 7864324
  45.6 1.0 copy.60
  46.6 7.4 %all-to-all-start = ((bf16[16,8,3072]{2,1,0:T(8,128)(2,1)}), bf16[16,8,3072]{2,1,0:T(8,128)(2,1)S(1)}, u32[]{:S(2)}, u32[]{:S(2)}) async-start(bf16[16,8,3072]{2,1,0:T(8,128)(2,1)} %bitcast.10), calls=%async_computation | async-start | bytes 1572864 | tf_op jit(solution)/shard_map/all_to_all | solution.py:256
  54.0 11.2 %all-to-all-done = bf16[16,8,3072]{2,1,0:T(8,128)(2,1)S(1)} async-done(((bf16[16,8,3072]{2,1,0:T(8,128)(2,1)}), bf16[16,8,3072]{2,1,0:T(8,128)(2,1)S(1)}, u32[]{:S(2)}, u32[]{:S(2)}) %all-to-all-start) | async-done | bytes 786464 | tf_op jit(solution)/shard_map/all_to_all | solution.py:256
  65.4 1.7 collective-permute-done.2
  67.1 0.2 maximum_select_fusion.1
  67.2 3.2 %collective-permute-start.3 = (bf16[256,1536]{1,0:T(8,128)(2,1)S(1)}, bf16[256,1536]{1,0:T(8,128)(2,1)}, u32[]{:S(2)}, u32[]{:S(2)}) collective-permute-start(bf16[256,1536]{1,0:T(8,128)(2,1)S(1)} %maximum_select_fusion.1), channel_id=1, source_target_pairs={{0,128},{128,1},{1,129},{129,2},{2,130},{130,3},{3,131},{131,0},{4... | collective-permute-start | bytes 2359304 | tf_op jit(solution)/shard_map/ppermute | solution.py:263
  70.5 17.1 %collective-permute-done.3 = bf16[256,1536]{1,0:T(8,128)(2,1)} collective-permute-done((bf16[256,1536]{1,0:T(8,128)(2,1)S(1)}, bf16[256,1536]{1,0:T(8,128)(2,1)}, u32[]{:S(2)}, u32[]{:S(2)}) %collective-permute-start.3) | collective-permute-done | bytes 786464 | tf_op jit(solution)/shard_map/ppermute | solution.py:263
  87.6 3.8 %collective-permute-start.4 = (bf16[256,1536]{1,0:T(8,128)(2,1)}, bf16[256,1536]{1,0:T(8,128)(2,1)}, u32[]{:S(2)}, u32[]{:S(2)}) collective-permute-start(bf16[256,1536]{1,0:T(8,128)(2,1)} %collective-permute-done.3), channel_id=1, source_target_pairs={{0,128},{128,1},{1,129},{129,2},{2,130},{130,3},{3,131},{131,0},{4... | collective-permute-start | bytes 2359304 | tf_op jit(solution)/shard_map/ppermute | solution.py:263
  91.4 16.6 %collective-permute-done.4 = bf16[256,1536]{1,0:T(8,128)(2,1)} collective-permute-done((bf16[256,1536]{1,0:T(8,128)(2,1)}, bf16[256,1536]{1,0:T(8,128)(2,1)}, u32[]{:S(2)}, u32[]{:S(2)}) %collective-permute-start.4) | collective-permute-done | bytes 786464 | tf_op jit(solution)/shard_map/ppermute | solution.py:263
  107.9 3.7 %collective-permute-start.5 = (bf16[256,1536]{1,0:T(8,128)(2,1)}, bf16[256,1536]{1,0:T(8,128)(2,1)}, u32[]{:S(2)}, u32[]{:S(2)}) collective-permute-start(bf16[256,1536]{1,0:T(8,128)(2,1)} %collective-permute-done.4), channel_id=1, source_target_pairs={{0,128},{128,1},{1,129},{129,2},{2,130},{130,3},{3,131},{131,0},{4... | collective-permute-start | bytes 2359304 | tf_op jit(solution)/shard_map/ppermute | solution.py:263
  111.7 0.9 copy-done.5
  112.6 3.5 %copy-done.2 = bf16[2048,2176]{1,0:T(8,128)(2,1)S(1)} copy-done((bf16[2048,2176]{1,0:T(8,128)(2,1)S(1)}, bf16[2048,2176]{1,0:T(8,128)(2,1)}, u32[]{:S(2)}) %copy-start.2) | copy-done | bytes 8912920
  116.1 11.5 %shard_map.94 = (bf16[2,384,2048]{2,1,0:T(8,128)(2,1)}, bf16[2,384,2048]{2,1,0:T(8,128)(2,1)}, bf16[2048,384]{1,0:T(8,128)(2,1)S(1)}) custom-call(s32[1]{0:T(128)} %bitcast.12.where_ref, bf16[2048,2176]{1,0:T(8,128)(2,1)S(1)} %copy-done.2), custom_call_target="tpu_custom_call" | custom-call | flops 1610612736 | bytes 15204352 | tf_op jit(solution)/shard_map/pallas_call | solution.py:104
  127.6 0.5 collective-permute-start.12
  128.3 1.2 constant_dynamic-update-slice_fusion.8
  129.5 1.2 constant_dynamic-update-slice_fusion.7
  130.7 1.3 constant_dynamic-update-slice_fusion.6
  132.1 17.0 %collective-permute-done.8 = bf16[256,1536]{1,0:T(8,128)(2,1)S(1)} collective-permute-done((bf16[256,1536]{1,0:T(8,128)(2,1)}, bf16[256,1536]{1,0:T(8,128)(2,1)S(1)}, u32[]{:S(2)}, u32[]{:S(2)}) %collective-permute-start.8) | collective-permute-done | bytes 786464 | tf_op jit(solution)/shard_map/ppermute | solution.py:263
  149.1 1.0 slice.114
  150.4 2.0 collective-permute-start.10
  152.5 7.9 %collective-permute-done.9 = bf16[128,1536]{1,0:T(8,128)(2,1)S(1)} collective-permute-done((bf16[128,1536]{1,0:T(8,128)(2,1)S(1)}, bf16[128,1536]{1,0:T(8,128)(2,1)S(1)}, u32[]{:S(2)}, u32[]{:S(2)}) %collective-permute-start.9) | collective-permute-done | bytes 393248 | tf_op jit(solution)/shard_map/ppermute | solution.py:263
  160.4 2.8 %collective-permute-done.10 = bf16[128,1536]{1,0:T(8,128)(2,1)S(1)} collective-permute-done((bf16[128,1536]{1,0:T(8,128)(2,1)S(1)}, bf16[128,1536]{1,0:T(8,128)(2,1)S(1)}, u32[]{:S(2)}, u32[]{:S(2)}) %collective-permute-start.10) | collective-permute-done | bytes 393248 | tf_op jit(solution)/shard_map/ppermute | solution.py:263
  163.3 0.2 constant_dynamic-slice_fusion
  163.5 5.5 %shard_map.96.own_high_ref.other_high_ref = bf16[2,768,384]{2,1,0:T(8,128)(2,1)S(1)} custom-call(bf16[2,384,2048]{2,1,0:T(8,128)(2,1)} %get-tuple-element.22.own_ref, bf16[2,384,2048]{2,1,0:T(8,128)(2,1)} %collective-permute-done.13.other_ref, bf16[2048,1536]{1,0:T(8,128)(2,1)S(1)} %constant_dynamic-update-slice_fusion.weight_ref), custom_call_target="tpu_custom_call" | custom-call | flops 2415919104 | bytes 10616832 | tf_op jit(solution)/shard_map/pallas_call | solution.py:135
  169.1 5.5 %shard_map.95.own_low_ref.other_low_ref = bf16[2,768,384]{2,1,0:T(8,128)(2,1)S(1)} custom-call(bf16[2,384,2048]{2,1,0:T(8,128)(2,1)} %get-tuple-element.18.own_ref, bf16[2,384,2048]{2,1,0:T(8,128)(2,1)} %collective-permute-done.12.other_ref, bf16[2048,1536]{1,0:T(8,128)(2,1)S(1)} %constant_dynamic-update-slice_fusion.weight_ref), custom_call_target="tpu_custom_call" | custom-call | flops 2415919104 | bytes 10616832 | tf_op jit(solution)/shard_map/pallas_call | solution.py:135
  174.6 2.1 shard_map.97
  176.7 0.2 convert.58
  176.9 0.4 shard_map.100
  177.3 0.9 collective-permute-start.22
  178.2 2.4 %collective-permute-start.24 = (bf16[512,128]{1,0:T(8,128)(2,1)S(1)}, bf16[512,128]{1,0:T(8,128)(2,1)S(1)}, u32[]{:S(2)}, u32[]{:S(2)}) collective-permute-start(bf16[512,128]{1,0:T(8,128)(2,1)S(1)} %get-tuple-element.55), channel_id=1, source_target_pairs={{0,48},{16,0},{32,16},{48,32},{1,49},{17,1},{33,17},{49,33},{2,50}... | collective-permute-start | bytes 393224 | tf_op jit(solution)/shard_map/ppermute | solution.py:50
  180.6 1.9 shard_map.98
  182.7 0.4 shard_map.99
  183.2 3.2 %collective-permute-start.17 = (bf16[512,256]{1,0:T(8,128)(2,1)S(1)}, bf16[512,256]{1,0:T(8,128)(2,1)S(1)}, u32[]{:S(2)}, u32[]{:S(2)}) collective-permute-start(bf16[512,256]{1,0:T(8,128)(2,1)S(1)} %get-tuple-element.50), channel_id=1, source_target_pairs={{0,48},{16,0},{32,16},{48,32},{1,49},{17,1},{33,17},{49,33},{2,50}... | collective-permute-start | bytes 786440 | tf_op jit(solution)/shard_map/ppermute | solution.py:50
  186.6 1.0 collective-permute-start.25
  187.6 1.2 collective-permute-start.23
  188.8 4.8 %collective-permute-done.15 = bf16[512,256]{1,0:T(8,128)(2,1)S(1)} collective-permute-done((bf16[512,256]{1,0:T(8,128)(2,1)S(1)}, bf16[512,256]{1,0:T(8,128)(2,1)S(1)}, u32[]{:S(2)}, u32[]{:S(2)}) %collective-permute-start.15) | collective-permute-done | bytes 262176 | tf_op jit(solution)/shard_map/ppermute | solution.py:49
  193.8 3.3 %collective-permute-start.18 = (bf16[1024,256]{1,0:T(8,128)(2,1)S(1)}, bf16[1024,256]{1,0:T(8,128)(2,1)S(1)}, u32[]{:S(2)}, u32[]{:S(2)}) collective-permute-start(bf16[1024,256]{1,0:T(8,128)(2,1)S(1)} %pad_maximum_fusion.1), channel_id=1, source_target_pairs={{0,48},{16,0},{32,16},{48,32},{1,49},{17,1},{33,17},{49,33},{2,50}... | collective-permute-start | bytes 1572872 | tf_op jit(solution)/shard_map/ppermute | solution.py:58
  197.3 1.5 collective-permute-done.25
  198.9 0.9 collective-permute-start.28
  199.9 2.4 %collective-permute-start.27 = (bf16[2,128,128]{2,1,0:T(8,128)(2,1)S(1)}, bf16[2,128,128]{2,1,0:T(8,128)(2,1)S(1)}, u32[]{:S(2)}, u32[]{:S(2)}) collective-permute-start(bf16[2,128,128]{2,1,0:T(8,128)(2,1)S(1)} %get-tuple-element.53), channel_id=1, source_target_pairs={{0,4},{4,8},{8,12},{12,0},{1,5},{5,9},{9,13},{13,1},{2,6},{6,10},{... | collective-permute-start | bytes 196616 | tf_op jit(solution)/shard_map/ppermute | solution.py:298
  202.3 1.6 collective-permute-start.26
  203.9 0.9 maximum_select_fusion
  204.7 0.5 collective-permute-done.28
  205.2 2.8 %collective-permute-done.26 = bf16[2,128,128]{2,1,0:T(8,128)(2,1)S(1)} collective-permute-done((bf16[2,128,128]{2,1,0:T(8,128)(2,1)S(1)}, bf16[2,128,128]{2,1,0:T(8,128)(2,1)S(1)}, u32[]{:S(2)}, u32[]{:S(2)}) %collective-permute-start.26) | collective-permute-done | bytes 65568 | tf_op jit(solution)/shard_map/ppermute | solution.py:297
  208.1 0.6 collective-permute-done.18
  208.7 0.7 collective-permute-done.16
  209.6 0.9 collective-permute-start.21
  210.5 2.4 %collective-permute-start.20 = (bf16[2,128,256]{2,1,0:T(8,128)(2,1)S(1)}, bf16[2,128,256]{2,1,0:T(8,128)(2,1)S(1)}, u32[]{:S(2)}, u32[]{:S(2)}) collective-permute-start(bf16[2,128,256]{2,1,0:T(8,128)(2,1)S(1)} %get-tuple-element.44), channel_id=1, source_target_pairs={{0,4},{4,8},{8,12},{12,0},{1,5},{5,9},{9,13},{13,1},{2,6},{6,10},{... | collective-permute-start | bytes 393224 | tf_op jit(solution)/shard_map/ppermute | solution.py:298
  212.9 1.6 collective-permute-start.19
  214.5 2.7 %collective-permute-done.21 = bf16[2,128,256]{2,1,0:T(8,128)(2,1)S(1)} collective-permute-done((bf16[2,128,256]{2,1,0:T(8,128)(2,1)S(1)}, bf16[2,128,256]{2,1,0:T(8,128)(2,1)S(1)}, u32[]{:S(2)}, u32[]{:S(2)}) %collective-permute-start.21) | collective-permute-done | bytes 131104 | tf_op jit(solution)/shard_map/ppermute | solution.py:299
  217.3 2.1 collective-permute-done.19
  219.6 1.1 fusion.3
  220.7 2.0 copy.69
  222.7 0.7 fusion.16
  (100 shorter events, 3.2 us)
Async XLA Ops:
  7.2 10.5 %copy-start = (bf16[4,32,2048]{2,1,0:T(8,128)(2,1)S(1)}, bf16[4,32,2048]{2,1,0:T(8,128)(2,1)}, u32[]{:S(2)}) copy-start(bf16[4,32,2048]{2,1,0:T(8,128)(2,1)} %param.10) | copy-start | bytes 1572868
  7.2 104.5 %all-gather.2.cloned.1.call-start = ((), (), s32[]{:S(2)}) async-start(), calls=%async_computation.1 | async-start | bytes 9469952 | tf_op jit(solution)/shard_map/all_gather | solution.py:247
  8.8 3.6 %collective-permute-start = (bf16[64,2,8,768]{3,2,1,0:T(8,128)(2,1)S(1)}, bf16[64,2,8,768]{3,2,1,0:T(8,128)(2,1)}, u32[]{:S(2)}, u32[]{:S(2)}) collective-permute-start(bf16[64,2,8,768]{3,2,1,0:T(8,128)(2,1)S(1)} %dynamic-slice_bitcast_fusion), channel_id=1, source_target_pairs={{0,64},{64,0},{1,65},{65,1},{2,66},{66,2},{3,67},{67,3},{4,68},{68... | collective-permute-start | bytes 4718600 | tf_op jit(solution)/shard_map/ppermute | solution.py:29
  9.0 7.6 %copy-start.10 = (f32[4,32,8]{1,2,0:T(8,128)S(1)}, f32[4,32,8]{1,2,0:T(8,128)}, u32[]{:S(2)}) copy-start(f32[4,32,8]{1,2,0:T(8,128)} %param.12) | copy-start | bytes 12292
  9.0 7.8 %copy-start.9 = (s32[4,32,8]{1,2,0:T(8,128)S(1)}, s32[4,32,8]{1,2,0:T(8,128)}, u32[]{:S(2)}) copy-start(s32[4,32,8]{1,2,0:T(8,128)} %param.11) | copy-start | bytes 12292
  14.8 1.7 copy-start.3
  17.6 24.2 %copy-start.4 = (f32[64,1,1,8,768]{4,3,2,1,0:T(8,128)S(1)}, f32[64,1,1,8,768]{4,3,2,1,0:T(8,128)}, u32[]{:S(2)}) copy-start(f32[64,1,1,8,768]{4,3,2,1,0:T(8,128)} %param.9) | copy-start | bytes 4718596
  22.0 19.8 %collective-permute-start.1 = (bf16[64,8,768]{2,1,0:T(8,128)(2,1)S(1)}, bf16[64,8,768]{2,1,0:T(8,128)(2,1)}, u32[]{:S(2)}, u32[]{:S(2)}) collective-permute-start(bf16[64,8,768]{2,1,0:T(8,128)(2,1)S(1)} %fusion.10), channel_id=1, source_target_pairs={{0,128},{128,0},{1,129},{129,1},{2,130},{130,2},{3,131},{131,3},{4... | collective-permute-start | bytes 2359304 | tf_op jit(solution)/shard_map/ppermute | solution.py:29
  46.6 18.6 %all-to-all-start = ((bf16[16,8,3072]{2,1,0:T(8,128)(2,1)}), bf16[16,8,3072]{2,1,0:T(8,128)(2,1)S(1)}, u32[]{:S(2)}, u32[]{:S(2)}) async-start(bf16[16,8,3072]{2,1,0:T(8,128)(2,1)} %bitcast.10), calls=%async_computation | async-start | bytes 1572864 | tf_op jit(solution)/shard_map/all_to_all | solution.py:256
  65.3 1.8 collective-permute-start.2
  67.2 20.3 %collective-permute-start.3 = (bf16[256,1536]{1,0:T(8,128)(2,1)S(1)}, bf16[256,1536]{1,0:T(8,128)(2,1)}, u32[]{:S(2)}, u32[]{:S(2)}) collective-permute-start(bf16[256,1536]{1,0:T(8,128)(2,1)S(1)} %maximum_select_fusion.1), channel_id=1, source_target_pairs={{0,128},{128,1},{1,129},{129,2},{2,130},{130,3},{3,131},{131,0},{4... | collective-permute-start | bytes 2359304 | tf_op jit(solution)/shard_map/ppermute | solution.py:263
  70.5 20.9 %collective-permute-start.6 = (bf16[256,1536]{1,0:T(8,128)(2,1)S(1)}, bf16[256,1536]{1,0:T(8,128)(2,1)S(1)}, u32[]{:S(2)}, u32[]{:S(2)}) collective-permute-start(bf16[256,1536]{1,0:T(8,128)(2,1)S(1)} %maximum_select_fusion.1), channel_id=1, source_target_pairs={{128,0},{1,128},{129,1},{2,129},{130,2},{3,130},{131,3},{0,131},{1... | collective-permute-start | bytes 2359304 | tf_op jit(solution)/shard_map/ppermute | solution.py:263
  87.6 20.4 %collective-permute-start.4 = (bf16[256,1536]{1,0:T(8,128)(2,1)}, bf16[256,1536]{1,0:T(8,128)(2,1)}, u32[]{:S(2)}, u32[]{:S(2)}) collective-permute-start(bf16[256,1536]{1,0:T(8,128)(2,1)} %collective-permute-done.3), channel_id=1, source_target_pairs={{0,128},{128,1},{1,129},{129,2},{2,130},{130,3},{3,131},{131,0},{4... | collective-permute-start | bytes 2359304 | tf_op jit(solution)/shard_map/ppermute | solution.py:263
  91.4 20.3 %copy-start.7 = (bf16[256,1536]{1,0:T(8,128)(2,1)}, bf16[256,1536]{1,0:T(8,128)(2,1)S(1)}, u32[]{:S(2)}) copy-start(bf16[256,1536]{1,0:T(8,128)(2,1)S(1)} %collective-permute-done.6) | copy-start | bytes 2359300
  91.4 20.3 %collective-permute-start.7 = (bf16[256,1536]{1,0:T(8,128)(2,1)S(1)}, bf16[256,1536]{1,0:T(8,128)(2,1)S(1)}, u32[]{:S(2)}, u32[]{:S(2)}) collective-permute-start(bf16[256,1536]{1,0:T(8,128)(2,1)S(1)} %collective-permute-done.6), channel_id=1, source_target_pairs={{128,0},{1,128},{129,1},{2,129},{130,2},{3,130},{131,3},{0,131},{1... | collective-permute-start | bytes 2359304 | tf_op jit(solution)/shard_map/ppermute | solution.py:263
  107.9 20.3 %collective-permute-start.5 = (bf16[256,1536]{1,0:T(8,128)(2,1)}, bf16[256,1536]{1,0:T(8,128)(2,1)}, u32[]{:S(2)}, u32[]{:S(2)}) collective-permute-start(bf16[256,1536]{1,0:T(8,128)(2,1)} %collective-permute-done.4), channel_id=1, source_target_pairs={{0,128},{128,1},{1,129},{129,2},{2,130},{130,3},{3,131},{131,0},{4... | collective-permute-start | bytes 2359304 | tf_op jit(solution)/shard_map/ppermute | solution.py:263
  111.6 0.9 copy-start.5
  112.6 3.5 %copy-start.2 = (bf16[2048,2176]{1,0:T(8,128)(2,1)S(1)}, bf16[2048,2176]{1,0:T(8,128)(2,1)}, u32[]{:S(2)}) copy-start(bf16[2048,2176]{1,0:T(8,128)(2,1)} %all-gather.2.cloned.1.call-done.row_ref) | copy-start | bytes 26738692
  116.1 12.0 %copy-start.11 = (s32[3]{0:T(128)S(1)}, s32[3]{0:T(128)}, u32[]{:S(2)}) copy-start(s32[3]{0:T(128)} %constant.283.clone) | copy-start | bytes 40
  127.6 35.9 %collective-permute-start.13 = (bf16[2,384,2048]{2,1,0:T(8,128)(2,1)}, bf16[2,384,2048]{2,1,0:T(8,128)(2,1)}, u32[]{:S(2)}, u32[]{:S(2)}) collective-permute-start(bf16[2,384,2048]{2,1,0:T(8,128)(2,1)} %get-tuple-element.22.own_ref), channel_id=1, source_target_pairs={{0,64},{64,0},{1,65},{65,1},{2,66},{66,2},{3,67},{67,3},{4,68},{68... | collective-permute-start | bytes 9437192 | tf_op jit(solution)/shard_map/ppermute | solution.py:29
  127.6 41.5 %collective-permute-start.12 = (bf16[2,384,2048]{2,1,0:T(8,128)(2,1)}, bf16[2,384,2048]{2,1,0:T(8,128)(2,1)}, u32[]{:S(2)}, u32[]{:S(2)}) collective-permute-start(bf16[2,384,2048]{2,1,0:T(8,128)(2,1)} %get-tuple-element.18.own_ref), channel_id=1, source_target_pairs={{0,64},{64,0},{1,65},{65,1},{2,66},{66,2},{3,67},{67,3},{4,68},{68... | collective-permute-start | bytes 9437192 | tf_op jit(solution)/shard_map/ppermute | solution.py:29
  128.2 3.9 %copy-start.8 = (bf16[256,1536]{1,0:T(8,128)(2,1)S(1)}, bf16[256,1536]{1,0:T(8,128)(2,1)}, u32[]{:S(2)}) copy-start(bf16[256,1536]{1,0:T(8,128)(2,1)} %copy-done.7) | copy-start | bytes 2359300
  128.2 20.9 %collective-permute-start.8 = (bf16[256,1536]{1,0:T(8,128)(2,1)}, bf16[256,1536]{1,0:T(8,128)(2,1)S(1)}, u32[]{:S(2)}, u32[]{:S(2)}) collective-permute-start(bf16[256,1536]{1,0:T(8,128)(2,1)} %copy-done.5), channel_id=1, source_target_pairs={{128,0},{1,128},{129,1},{2,129},{130,2},{3,130},{131,3},{0,131},{1... | collective-permute-start | bytes 2359304 | tf_op jit(solution)/shard_map/ppermute | solution.py:263
  130.7 19.6 %copy-start.6 = (bf16[256,1536]{1,0:T(8,128)(2,1)S(1)}, bf16[256,1536]{1,0:T(8,128)(2,1)}, u32[]{:S(2)}) copy-start(bf16[256,1536]{1,0:T(8,128)(2,1)} %copy-done.5) | copy-start | bytes 2359300
  150.1 10.2 %collective-permute-start.9 = (bf16[128,1536]{1,0:T(8,128)(2,1)S(1)}, bf16[128,1536]{1,0:T(8,128)(2,1)S(1)}, u32[]{:S(2)}, u32[]{:S(2)}) collective-permute-start(bf16[128,1536]{1,0:T(8,128)(2,1)S(1)} %slice.114), channel_id=1, source_target_pairs={{0,128},{128,1},{1,129},{129,2},{2,130},{130,3},{3,131},{131,0},{4... | collective-permute-start | bytes 1179656 | tf_op jit(solution)/shard_map/ppermute | solution.py:263
  150.2 24.4 %collective-permute-start.11 = (bf16[2048,384]{1,0:T(8,128)(2,1)S(1)}, bf16[2048,384]{1,0:T(8,128)(2,1)S(1)}, u32[]{:S(2)}, u32[]{:S(2)}) collective-permute-start(bf16[2048,384]{1,0:T(8,128)(2,1)S(1)} %get-tuple-element.21.own_ref), channel_id=1, source_target_pairs={{0,64},{64,0},{1,65},{65,1},{2,66},{66,2},{3,67},{67,3},{4,68},{68... | collective-permute-start | bytes 4718600 | tf_op jit(solution)/shard_map/ppermute | solution.py:29
  150.4 12.8 %collective-permute-start.10 = (bf16[128,1536]{1,0:T(8,128)(2,1)S(1)}, bf16[128,1536]{1,0:T(8,128)(2,1)S(1)}, u32[]{:S(2)}, u32[]{:S(2)}) collective-permute-start(bf16[128,1536]{1,0:T(8,128)(2,1)S(1)} %slice.115), channel_id=1, source_target_pairs={{128,0},{1,128},{129,1},{2,129},{130,2},{3,130},{131,3},{0,131},{1... | collective-permute-start | bytes 1179656 | tf_op jit(solution)/shard_map/ppermute | solution.py:263
  163.4 38.8 %collective-permute-start.14 = (bf16[2048,384]{1,0:T(8,128)(2,1)S(1)}, bf16[2048,384]{1,0:T(8,128)(2,1)S(1)}, u32[]{:S(2)}, u32[]{:S(2)}) collective-permute-start(bf16[2048,384]{1,0:T(8,128)(2,1)S(1)} %constant_dynamic-slice_fusion), channel_id=1, source_target_pairs={{0,64},{64,0},{1,65},{65,1},{2,66},{66,2},{3,67},{67,3},{4,68},{68... | collective-permute-start | bytes 4718600 | tf_op jit(solution)/shard_map/ppermute | solution.py:29
  177.3 9.2 %collective-permute-start.22 = (bf16[512,128]{1,0:T(8,128)(2,1)S(1)}, bf16[512,128]{1,0:T(8,128)(2,1)S(1)}, u32[]{:S(2)}, u32[]{:S(2)}) collective-permute-start(bf16[512,128]{1,0:T(8,128)(2,1)S(1)} %get-tuple-element.54), channel_id=1, source_target_pairs={{0,16},{16,32},{32,48},{48,0},{1,17},{17,33},{33,49},{49,1},{2,18}... | collective-permute-start | bytes 393224 | tf_op jit(solution)/shard_map/ppermute | solution.py:49
  178.2 8.3 %collective-permute-start.24 = (bf16[512,128]{1,0:T(8,128)(2,1)S(1)}, bf16[512,128]{1,0:T(8,128)(2,1)S(1)}, u32[]{:S(2)}, u32[]{:S(2)}) collective-permute-start(bf16[512,128]{1,0:T(8,128)(2,1)S(1)} %get-tuple-element.55), channel_id=1, source_target_pairs={{0,48},{16,0},{32,16},{48,32},{1,49},{17,1},{33,17},{49,33},{2,50}... | collective-permute-start | bytes 393224 | tf_op jit(solution)/shard_map/ppermute | solution.py:50
  183.1 10.5 %collective-permute-start.15 = (bf16[512,256]{1,0:T(8,128)(2,1)S(1)}, bf16[512,256]{1,0:T(8,128)(2,1)S(1)}, u32[]{:S(2)}, u32[]{:S(2)}) collective-permute-start(bf16[512,256]{1,0:T(8,128)(2,1)S(1)} %get-tuple-element.49), channel_id=1, source_target_pairs={{0,16},{16,32},{32,48},{48,0},{1,17},{17,33},{33,49},{49,1},{2,18}... | collective-permute-start | bytes 786440 | tf_op jit(solution)/shard_map/ppermute | solution.py:49
  183.2 10.4 %collective-permute-start.17 = (bf16[512,256]{1,0:T(8,128)(2,1)S(1)}, bf16[512,256]{1,0:T(8,128)(2,1)S(1)}, u32[]{:S(2)}, u32[]{:S(2)}) collective-permute-start(bf16[512,256]{1,0:T(8,128)(2,1)S(1)} %get-tuple-element.50), channel_id=1, source_target_pairs={{0,48},{16,0},{32,16},{48,32},{1,49},{17,1},{33,17},{49,33},{2,50}... | collective-permute-start | bytes 786440 | tf_op jit(solution)/shard_map/ppermute | solution.py:50
  186.6 12.2 %collective-permute-start.25 = (bf16[1024,128]{1,0:T(8,128)(2,1)S(1)}, bf16[1024,128]{1,0:T(8,128)(2,1)S(1)}, u32[]{:S(2)}, u32[]{:S(2)}) collective-permute-start(bf16[1024,128]{1,0:T(8,128)(2,1)S(1)} %pad_maximum_fusion.3), channel_id=1, source_target_pairs={{0,48},{16,0},{32,16},{48,32},{1,49},{17,1},{33,17},{49,33},{2,50}... | collective-permute-start | bytes 786440 | tf_op jit(solution)/shard_map/ppermute | solution.py:58
  187.6 11.2 %collective-permute-start.23 = (bf16[1024,128]{1,0:T(8,128)(2,1)S(1)}, bf16[1024,128]{1,0:T(8,128)(2,1)S(1)}, u32[]{:S(2)}, u32[]{:S(2)}) collective-permute-start(bf16[1024,128]{1,0:T(8,128)(2,1)S(1)} %pad_maximum_fusion.2), channel_id=1, source_target_pairs={{0,16},{16,32},{32,48},{48,0},{1,17},{17,33},{33,49},{49,1},{2,18}... | collective-permute-start | bytes 786440 | tf_op jit(solution)/shard_map/ppermute | solution.py:57
  193.8 14.9 %collective-permute-start.18 = (bf16[1024,256]{1,0:T(8,128)(2,1)S(1)}, bf16[1024,256]{1,0:T(8,128)(2,1)S(1)}, u32[]{:S(2)}, u32[]{:S(2)}) collective-permute-start(bf16[1024,256]{1,0:T(8,128)(2,1)S(1)} %pad_maximum_fusion.1), channel_id=1, source_target_pairs={{0,48},{16,0},{32,16},{48,32},{1,49},{17,1},{33,17},{49,33},{2,50}... | collective-permute-start | bytes 1572872 | tf_op jit(solution)/shard_map/ppermute | solution.py:58
  197.2 12.2 %collective-permute-start.16 = (bf16[1024,256]{1,0:T(8,128)(2,1)S(1)}, bf16[1024,256]{1,0:T(8,128)(2,1)S(1)}, u32[]{:S(2)}, u32[]{:S(2)}) collective-permute-start(bf16[1024,256]{1,0:T(8,128)(2,1)S(1)} %pad_maximum_fusion), channel_id=1, source_target_pairs={{0,16},{16,32},{32,48},{48,0},{1,17},{17,33},{33,49},{49,1},{2,18}... | collective-permute-start | bytes 1572872 | tf_op jit(solution)/shard_map/ppermute | solution.py:57
  198.9 6.3 %collective-permute-start.28 = (bf16[2,128,128]{2,1,0:T(8,128)(2,1)S(1)}, bf16[2,128,128]{2,1,0:T(8,128)(2,1)S(1)}, u32[]{:S(2)}, u32[]{:S(2)}) collective-permute-start(bf16[2,128,128]{2,1,0:T(8,128)(2,1)S(1)} %get-tuple-element.52), channel_id=1, source_target_pairs={{0,12},{4,0},{8,4},{12,8},{1,13},{5,1},{9,5},{13,9},{2,14},{6,2},{... | collective-permute-start | bytes 196616 | tf_op jit(solution)/shard_map/ppermute | solution.py:299
  199.9 5.3 %collective-permute-start.27 = (bf16[2,128,128]{2,1,0:T(8,128)(2,1)S(1)}, bf16[2,128,128]{2,1,0:T(8,128)(2,1)S(1)}, u32[]{:S(2)}, u32[]{:S(2)}) collective-permute-start(bf16[2,128,128]{2,1,0:T(8,128)(2,1)S(1)} %get-tuple-element.53), channel_id=1, source_target_pairs={{0,4},{4,8},{8,12},{12,0},{1,5},{5,9},{9,13},{13,1},{2,6},{6,10},{... | collective-permute-start | bytes 196616 | tf_op jit(solution)/shard_map/ppermute | solution.py:298
  202.3 5.8 %collective-permute-start.26 = (bf16[2,128,128]{2,1,0:T(8,128)(2,1)S(1)}, bf16[2,128,128]{2,1,0:T(8,128)(2,1)S(1)}, u32[]{:S(2)}, u32[]{:S(2)}) collective-permute-start(bf16[2,128,128]{2,1,0:T(8,128)(2,1)S(1)} %get-tuple-element.51), channel_id=1, source_target_pairs={{0,8},{4,12},{8,0},{12,4},{1,9},{5,13},{9,1},{13,5},{2,10},{6,14},... | collective-permute-start | bytes 196616 | tf_op jit(solution)/shard_map/ppermute | solution.py:297
  209.6 7.7 %collective-permute-start.21 = (bf16[2,128,256]{2,1,0:T(8,128)(2,1)S(1)}, bf16[2,128,256]{2,1,0:T(8,128)(2,1)S(1)}, u32[]{:S(2)}, u32[]{:S(2)}) collective-permute-start(bf16[2,128,256]{2,1,0:T(8,128)(2,1)S(1)} %get-tuple-element.43), channel_id=1, source_target_pairs={{0,12},{4,0},{8,4},{12,8},{1,13},{5,1},{9,5},{13,9},{2,14},{6,2},{... | collective-permute-start | bytes 393224 | tf_op jit(solution)/shard_map/ppermute | solution.py:299
  210.5 6.7 %collective-permute-start.20 = (bf16[2,128,256]{2,1,0:T(8,128)(2,1)S(1)}, bf16[2,128,256]{2,1,0:T(8,128)(2,1)S(1)}, u32[]{:S(2)}, u32[]{:S(2)}) collective-permute-start(bf16[2,128,256]{2,1,0:T(8,128)(2,1)S(1)} %get-tuple-element.44), channel_id=1, source_target_pairs={{0,4},{4,8},{8,12},{12,0},{1,5},{5,9},{9,13},{13,1},{2,6},{6,10},{... | collective-permute-start | bytes 393224 | tf_op jit(solution)/shard_map/ppermute | solution.py:298
  212.9 6.5 %collective-permute-start.19 = (bf16[2,128,256]{2,1,0:T(8,128)(2,1)S(1)}, bf16[2,128,256]{2,1,0:T(8,128)(2,1)S(1)}, u32[]{:S(2)}, u32[]{:S(2)}) collective-permute-start(bf16[2,128,256]{2,1,0:T(8,128)(2,1)S(1)} %get-tuple-element.42), channel_id=1, source_target_pairs={{0,8},{4,12},{8,0},{12,4},{1,9},{5,13},{9,1},{13,5},{2,10},{6,14},... | collective-permute-start | bytes 393224 | tf_op jit(solution)/shard_map/ppermute | solution.py:297
  214.5 8.2 %collective-permute-start.30 = (bf16[128,128]{1,0:T(8,128)(2,1)S(1)}, bf16[128,128]{1,0:T(8,128)(2,1)S(1)}, u32[]{:S(2)}, u32[]{:S(2)}) collective-permute-start(bf16[128,128]{1,0:T(8,128)(2,1)S(1)} %get-tuple-element.59), channel_id=1, source_target_pairs={{0,64},{64,0},{1,65},{65,1},{2,66},{66,2},{3,67},{67,3},{4,68},{68... | collective-permute-start | bytes 98312 | tf_op jit(solution)/shard_map/ppermute | solution.py:29
  219.5 3.2 %collective-permute-start.29 = (bf16[128,256]{1,0:T(8,128)(2,1)S(1)}, bf16[128,256]{1,0:T(8,128)(2,1)S(1)}, u32[]{:S(2)}, u32[]{:S(2)}) collective-permute-start(bf16[128,256]{1,0:T(8,128)(2,1)S(1)} %get-tuple-element.57), channel_id=1, source_target_pairs={{0,64},{64,0},{1,65},{65,1},{2,66},{66,2},{3,67},{67,3},{4,68},{68... | collective-permute-start | bytes 196616 | tf_op jit(solution)/shard_map/ppermute | solution.py:29
  219.6 3.9 %copy-start.1 = (bf16[4,32,2048]{2,1,0:T(8,128)(2,1)S(1)}, bf16[4,32,2048]{2,1,0:T(8,128)(2,1)}, u32[]{:S(2)}) copy-start(bf16[4,32,2048]{2,1,0:T(8,128)(2,1)} %param.10) | copy-start | bytes 1572868
Sparse Core Ops, SparseCore 0:
  22.2 79.9 all-gather.1
where the time goes:
time: 234 us; the launch traced here: 230 us
  waiting for transfers between devices  113 us (48%)
  starting transfers between devices  43.6 us (19%)
  Pallas kernels  27.4 us (12%)
  local copies, waits for them, and re-layouts  16.9 us (7%)
  between operations  14.6 us (6%)
  other arithmetic  11 us (5%)
  matrix products  3.73 us (2%)
    ppermute x8, waiting for transfers between devices, hop(): return (lax.ppermute(up, Z, UP), lax.ppermute(down, Z, DOWN))  61.4 us
    ppermute x9, waiting for transfers between devices, swap(): return lax.ppermute(value, axis, SWAP)  24.7 us
    ppermute x8, starting transfers between devices, hop(): return (lax.ppermute(up, Z, UP), lax.ppermute(down, Z, DOWN))  12.9 us
    pallas_call x1, Pallas kernels, pack(): pl.pallas_call(functools.partial(pack_kernel, top), grid=(tiles,), in_spe...  11.5 us
    all_to_all x1, waiting for transfers between devices, local(): lax.all_to_all(piece, ('y', 'x'), split_axis=0, concat_axis=0, tiled=True)  11.2 us
    pallas_call x2, Pallas kernels, answers_of(): pl.pallas_call(functools.partial(answers_kernel, 0.5 / math.sqrt(model)),...  11.1 us
    unnamed x32, local copies, waits for them, and re-layouts  10.1 us
    all_to_all x1, starting transfers between devices, local(): lax.all_to_all(piece, ('y', 'x'), split_axis=0, concat_axis=0, tiled=True)  7.45 us
  transfers between devices with their start and end apart: 33, of which 17 were waited for; matrix products, arithmetic and copies ran while one was open for 7% of the time, Pallas kernels for 12%

commit v1 on v0

v1 whole, which is shorter than its diff:
```python
import functools
import math

import jax
import jax.numpy as jnp
from jax import lax
from jax.experimental import pallas as pl
from jax.experimental.layout import Layout, with_layout_constraint
from jax.experimental.pallas import tpu as pltpu
from jax.sharding import Mesh, PartitionSpec as P

outer_momentum = 0.9
outer_rate = 0.7

RING = 4
LANES = 128
CAP = 6
GROUPS = 8
PLUS = [(i, (i + 1) % RING) for i in range(RING)]
MINUS = [(i, (i - 1) % RING) for i in range(RING)]
CHIPS = 8
Z = ("z_lo", "z_hi")
UP = [(i % 2 * RING + i // 2, (i + 1) % CHIPS % 2 * RING + (i + 1) % CHIPS // 2) for i in range(CHIPS)]
DOWN = [(after, before) for before, after in UP]
SWAP = [(0, 1), (1, 0)]


def swap(value, axis):
    return lax.ppermute(value, axis, SWAP)


def later(value, *first):
    return lax.optimization_barrier((value,) + first)[0]


def neighbours(value, axis):
    return lax.ppermute(value, axis, PLUS), lax.ppermute(value, axis, MINUS)


def forward(before, after, axis):
    half = before.shape[0] // 2
    low = lax.ppermute(before[:half], axis, PLUS)
    high = lax.ppermute(after[half:], axis, MINUS)
    return jnp.concatenate([low, high])


def far_sums(before, after, far, axis):
    half = far.shape[0] // 2
    low = lax.ppermute(far[:half].astype(jnp.bfloat16), axis, PLUS)
    high = lax.ppermute(far[half:].astype(jnp.bfloat16), axis, MINUS)
    after = jnp.concatenate([after[:half] + low.astype(jnp.float32), after[half:]])
    before = jnp.concatenate([before[:half], before[half:] + high.astype(jnp.float32)])
    return before.astype(jnp.bfloat16), after.astype(jnp.bfloat16)


def near_sums(own, before, after, axis):
    from_before = lax.ppermute(after, axis, PLUS)
    from_after = lax.ppermute(before, axis, MINUS)
    return own + from_before.astype(jnp.float32) + from_after.astype(jnp.float32)


def by_core(core, mine, other, axis):
    return jnp.where(
        core == 0,
        jnp.concatenate([mine, other], axis=axis),
        jnp.concatenate([other, mine], axis=axis),
    )


def rounded(value):
    return lax.reduce_precision(value, exponent_bits=8, mantissa_bits=7)


def pack_kernel(top, where_ref, row_ref, packed_ref, spread_ref):
    count, model, slots = row_ref.shape[0], packed_ref.shape[2], packed_ref.shape[1]
    wide = RING * slots
    routing = row_ref[:, model : model + LANES].astype(jnp.float32)
    place = jnp.where(routing[:, :top] == where_ref[0].astype(jnp.float32), routing[:, top : 2 * top], -wide - 1.0)
    lane = lax.broadcasted_iota(jnp.int32, (count, 2 * wide), 1).astype(jnp.float32)
    spread = jnp.zeros((count, 2 * wide), jnp.float32)
    placed = jnp.zeros((count, wide), jnp.float32)
    for choice in range(top):
        here = place[:, choice : choice + 1]
        high = routing[:, 2 * top + choice : 2 * top + choice + 1]
        rest = routing[:, 3 * top + choice : 3 * top + choice + 1]
        spread = jnp.where(lane == here, high, jnp.where(lane == here + wide, rest, spread))
        placed = jnp.where(lane[:, :wide] == here, 1.0, placed)
    spread_ref[...] = spread.astype(jnp.bfloat16)
    packed = lax.dot_general(
        placed.astype(jnp.bfloat16),
        row_ref[:, :model],
        (((0,), (0,)), ((), ())),
        preferred_element_type=jnp.float32,
    ).astype(jnp.bfloat16)
    for offset in range(RING):
        packed_ref[offset] = packed[offset * slots : (offset + 1) * slots]


def pack(where, plane, model, top, rows):
    count, columns = plane.shape
    tile = GROUPS * rows
    tiles = count // tile
    slots = GROUPS * CAP
    return pl.pallas_call(
        functools.partial(pack_kernel, top),
        grid=(tiles,),
        in_specs=[
            pl.BlockSpec(memory_space=pltpu.SMEM),
            pl.BlockSpec((tile, columns), lambda i: (i, 0)),
        ],
        out_specs=[
            pl.BlockSpec((RING, slots, model), lambda i: (0, i, 0)),
            pl.BlockSpec((tile, 2 * RING * slots), lambda i: (i, 0)),
        ],
        out_shape=[
            jax.ShapeDtypeStruct((RING, tiles * slots, model), jnp.bfloat16),
            jax.ShapeDtypeStruct((count, 2 * RING * slots), jnp.bfloat16),
        ],
        compiler_params=pltpu.CompilerParams(vmem_limit_bytes=48 * 2**20),
        cost_estimate=pl.CostEstimate(
            flops=2 * count * RING * slots * model,
            bytes_accessed=2 * count * columns + 2 * tiles * slots * RING * model,
            transcendentals=0,
        ),
    )(where, plane)


def passed_on(values, first):
    anywhere = pl.BlockSpec(memory_space=pl.ANY)
    count = len(values)
    return pl.pallas_call(
        lambda *refs: None,
        in_specs=[anywhere] * (count + 1),
        out_specs=[anywhere] * count,
        out_shape=[jax.ShapeDtypeStruct(value.shape, value.dtype) for value in values],
        input_output_aliases={index: index for index in range(count)},
        compiler_params=pltpu.CompilerParams(vmem_limit_bytes=2**20),
    )(*values, first)


def answers_kernel(scale, which_ref, packed_ref, *refs):
    *pieces, out_ref, served_ref, weight_ref = refs
    start = 0
    for piece in pieces:
        weight_ref[start : start + piece.shape[0]] = piece[...]
        start += piece.shape[0]
    product = jnp.dot(packed_ref[0], weight_ref[...], preferred_element_type=jnp.float32)
    value = product * scale
    out_ref[0] = (value + value * jnp.tanh(value)).astype(jnp.bfloat16)

    @pl.when(pl.program_id(0) == which_ref[0])
    def _():
        served_ref[...] = weight_ref[...]


def answers_of(which, packed, pieces):
    _, count, model = packed.shape
    wide = pieces[0].shape[1] // RING
    return pl.pallas_call(
        functools.partial(answers_kernel, 0.5 / math.sqrt(model)),
        grid=(RING,),
        in_specs=[
            pl.BlockSpec(memory_space=pltpu.SMEM),
            pl.BlockSpec((1, count, model), lambda i: (i, 0, 0)),
        ]
        + [pl.BlockSpec((piece.shape[0], wide), lambda i: (0, i)) for piece in pieces],
        out_specs=[
            pl.BlockSpec((1, count, wide), lambda i: (i, 0, 0)),
            pl.BlockSpec((model, wide), lambda i: (0, 0)),
        ],
        out_shape=[
            jax.ShapeDtypeStruct((RING, count, wide), jnp.bfloat16),
            jax.ShapeDtypeStruct((model, wide), jnp.bfloat16),
        ],
        scratch_shapes=[pltpu.VMEM((model, wide), jnp.bfloat16)],
        compiler_params=pltpu.CompilerParams(vmem_limit_bytes=32 * 2**20),
        cost_estimate=pl.CostEstimate(
            flops=2 * RING * count * model * wide,
            bytes_accessed=2 * RING * (count * (model + wide) + model * wide),
            transcendentals=RING * count * wide,
        ),
    )(which, packed, *pieces)


def unpack_kernel(rows, where_ref, spread_ref, answers_ref, first_ref, out_ref):
    slots = GROUPS * CAP
    tile = GROUPS * rows
    for start in range(0, spread_ref.shape[0], tile):
        part = start // tile * slots
        held = [answers_ref[i, part : part + slots] for i in range(RING)]
        out = jnp.dot(
            spread_ref[start : start + tile],
            jnp.concatenate(held + held),
            preferred_element_type=jnp.float32,
        )
        out_ref[0, start : start + tile] = out.astype(out_ref.dtype)


def unpack(where, spread, answers, part, rows, dtype, first):
    blocks = where.shape[0]
    count, wide = spread.shape[0] // RING, spread.shape[1]
    slots, columns = answers.shape[1] // RING, part[1] - part[0]
    column = part[0] // columns
    return pl.pallas_call(
        functools.partial(unpack_kernel, rows),
        grid_spec=pltpu.PrefetchScalarGridSpec(
            num_scalar_prefetch=1,
            grid=(blocks,),
            in_specs=[
                pl.BlockSpec((count, wide), lambda i, where: (where[i], 0)),
                pl.BlockSpec((RING, slots, columns), lambda i, where: (0, where[i], column)),
                pl.BlockSpec(memory_space=pl.ANY),
            ],
            out_specs=pl.BlockSpec((1, count, columns), lambda i, where: (i, 0, 0)),
        ),
        out_shape=jax.ShapeDtypeStruct((blocks, count, columns), dtype),
        compiler_params=pltpu.CompilerParams(vmem_limit_bytes=18 * 2**20),
        cost_estimate=pl.CostEstimate(
            flops=2 * blocks * count * wide * columns,
            bytes_accessed=2 * blocks * count * (wide + 2 * columns),
            transcendentals=0,
        ),
    )(where, spread, answers, first)


def local(deltas, master, momentum, hidden, expert_ids, gate_weights):
    experts, block_rows, width = deltas.shape[1:]
    sub = master.shape[3]
    steps, rows, model = hidden.shape
    top = expert_ids.shape[2]
    z_lo, core = lax.axis_index("z_lo"), lax.axis_index("core")
    y, x, z_hi = lax.axis_index("y"), lax.axis_index("x"), lax.axis_index("z_hi")
    z = z_hi * 2 + z_lo
    taken = steps * rows
    owners = RING * RING
    span = owners * sub
    cut = 2 * width // 3
    parts = [(0, cut), (cut, width)]

    pieces = deltas[0].reshape(experts, 2, 2, sub, width)
    kept = lax.dynamic_index_in_dim(pieces, core, axis=2, keepdims=False)
    given = lax.dynamic_index_in_dim(pieces, 1 - core, axis=2, keepdims=False)
    other = swap(given, "core")

    def pair(index):
        both = [lax.dynamic_index_in_dim(value, index, axis=1, keepdims=False) for value in (kept, other)]
        return both[0].astype(jnp.float32) + both[1].astype(jnp.float32)

    given = pair(1 - z_lo).astype(jnp.bfloat16)
    received = swap(given, "z_lo")
    hidden, expert_ids, gate_weights = [
        later(value, given) for value in (hidden, expert_ids, gate_weights)
    ]

    named = (expert_ids.reshape(taken, top)[:, :, None] == jnp.arange(experts)).astype(jnp.float32)
    row = jnp.arange(taken)
    earlier = (row[:, None] // rows == row // rows) & (row[:, None] > row)
    rank = jnp.dot(
        earlier.astype(jnp.bfloat16),
        jnp.sum(named, axis=1).astype(jnp.bfloat16),
        preferred_element_type=jnp.float32,
    )
    rank = jnp.sum(named * rank[:, None], axis=2).astype(jnp.int32).reshape(expert_ids.shape)
    group = (x % 2) * steps + jnp.arange(steps, dtype=jnp.int32)[:, None, None]
    slot = expert_ids % RING * (GROUPS * CAP) + group * CAP + rank
    gate_high = rounded(gate_weights)
    routing = jnp.concatenate(
        [(expert_ids // RING).astype(jnp.float32), slot.astype(jnp.float32), gate_high, gate_weights - gate_high],
        axis=-1,
    ).astype(jnp.bfloat16)
    routing = jnp.pad(routing.reshape(taken, 4 * top), ((0, 0), (0, LANES - 4 * top)))
    place = jnp.arange(model, dtype=jnp.int32)
    turn = place // span % CHIPS
    ring_z = z + jnp.where(turn < 3, turn - 1, jnp.where(turn % 2 == 1, -1, 1) * (turn // 2 + turn % 2))
    ring_z = (z + jnp.where(turn == 7, 4, ring_z - z)) % CHIPS
    ring_core = (core + place // (CHIPS * span)) % 2
    source = (place // sub % owners) * RING + ring_z // 2
    source = source * block_rows + (ring_z % 2) * 2 * sub + ring_core * sub + place % sub
    ordering = (jnp.arange(model, dtype=jnp.int32)[:, None] == source[None, :]).astype(jnp.bfloat16)
    flat = jnp.dot(
        hidden.reshape(taken, model), ordering, preferred_element_type=jnp.float32
    ).astype(jnp.bfloat16)
    flat = jnp.concatenate([flat, routing], axis=1)
    flat = with_layout_constraint(flat, Layout(major_to_minor=(0, 1)))

    plane = lax.all_gather(flat, ("y", "x"), axis=0, tiled=True)
    params = master.reshape(experts, sub, width)
    velocity_old = momentum.reshape(experts, sub, width)
    outer_grad = (pair(z_lo) + received.astype(jnp.float32)) / 4
    velocity = outer_momentum * velocity_old + outer_grad
    piece = (params - outer_rate * (outer_grad + outer_momentum * velocity)).astype(jnp.bfloat16)

    piece = piece.reshape(owners, RING, sub, width).transpose(0, 2, 1, 3).reshape(owners, sub, RING * width)
    piece = lax.all_to_all(piece, ("y", "x"), split_axis=0, concat_axis=0, tiled=True)
    piece = piece.reshape(span, RING * width)

    def hop(up, down):
        return lax.ppermute(up, Z, UP), lax.ppermute(down, Z, DOWN)

    hops = [(piece, piece)]
    for _ in range(3):
        hops.append(hop(*hops[-1]))
    here = (y * RING + x).reshape(1)
    packed, spread = pack(here, plane, model, top, rows)
    up, down = passed_on(hops[3], spread)
    low, high = hop(up[: span // 2], down[span // 2 :])
    (up1, down1), (up2, down2) = hops[1:3]
    first = [up1, piece, down1]
    rest = [up2, down2, up, down, low, high]
    pieces = first + rest + [swap(jnp.concatenate(first), "core")] + [swap(part, "core") for part in rest]
    answers, engine = answers_of(z_hi.reshape(1), packed, pieces)
    far_block = ((y + 2) % RING).reshape(1)
    near_blocks = (y + jnp.array([3, 1, 0], jnp.int32)) % RING

    def to_rows(ringed):
        ringed = ringed.reshape(RING, taken, -1)
        own, before, after, far = [
            lax.dynamic_index_in_dim(ringed, (x + offset) % RING, axis=0, keepdims=False)
            for offset in (0, 3, 1, 2)
        ]
        received = [
            lax.ppermute(far.astype(jnp.bfloat16), "x", [(i, (i + 2) % RING) for i in range(RING)]),
            lax.ppermute(after.astype(jnp.bfloat16), "x", PLUS),
            lax.ppermute(before.astype(jnp.bfloat16), "x", MINUS),
        ]
        for value in received:
            own = own + value.astype(jnp.float32)
        return own

    first = spread
    decoded = []
    for part in parts:
        far = first = unpack(far_block, spread, answers, part, rows, jnp.bfloat16, first)
        near = first = unpack(near_blocks, spread, answers, part, rows, jnp.float32, first)
        before, after = far_sums(near[0], near[1], far[0], "y")
        decoded.append(to_rows(near_sums(near[2], before, after, "y")))
    decoded = jnp.concatenate(decoded, axis=1).reshape(steps, rows, width).astype(jnp.bfloat16)

    engine = later(engine, near).reshape(2, CHIPS, owners, sub, width)
    engine = by_core(core, engine[:1], engine[1:], 0)
    engine = jnp.concatenate([engine[:, i : i + 1] for i in (5, 3, 0, 1, 2, 4, 6, 7)] * 2, axis=1)
    engine = lax.dynamic_slice_in_dim(engine, (CHIPS + 3 - z) % CHIPS, CHIPS, axis=1)
    engine = engine.transpose(2, 1, 0, 3, 4).reshape(model, width)
    return (engine[None], velocity.reshape(momentum.shape), decoded)


def solution(mesh):
    fine = Mesh(
        mesh.devices.reshape(2, 2, RING, RING, RING), ("z_lo", "core", "y", "x", "z_hi")
    )
    rep, ep = ("z_lo", "core"), ("y", "x", "z_hi")
    return jax.shard_map(
        local,
        mesh=fine,
        in_specs=(
            P(rep, None, ep, None),
            P(None, ep, rep, None, None),
            P(None, ep, rep, None, None),
            P(None, rep + ep, None),
            P(None, rep + ep, None),
            P(None, rep + ep, None),
        ),
        out_specs=(
            P(ep, None, None),
            P(None, ep, rep, None, None),
            P(None, rep + ep, None),
        ),
        check_vma=False,
    )
```

time: 234 us -> 203 us (0.87); the launches traced: 230 us -> 202 us
  waiting for transfers between devices: 113 us -> 80.9 us
  blocking collectives: 0 us -> 18.7 us
  local copies, waits for them, and re-layouts: 16.9 us -> 9.79 us
  starting transfers between devices: 43.6 us -> 36.6 us
    ppermute x8, waiting for transfers between devices: 61.4 us -> 40.6 us  [hop(): return (lax.ppermute(up, Z, UP), lax.ppermute(down, Z, DOWN))]
    all_to_all x0 -> x1, blocking collectives: none -> 18.7 us  [local(): lax.all_to_all(piece, ('y', 'x'), split_axis=0, concat_axis=0, tiled=True)]
    all_to_all x1 -> x0, waiting for transfers between devices: 11.2 us -> none  [local(): lax.all_to_all(piece, ('y', 'x'), split_axis=0, concat_axis=0, tiled=True)]
    all_to_all x1 -> x0, starting transfers between devices: 7.45 us -> none  [local(): lax.all_to_all(piece, ('y', 'x'), split_axis=0, concat_axis=0, tiled=True)]
    unnamed x32 -> x27, local copies, waits for them, and re-layouts: 10.1 us -> 2.68 us
    ppermute x2, waiting for transfers between devices: 0.74 us -> 6.01 us  [near_sums(): from_before = lax.ppermute(after, axis, PLUS)]
    ppermute x2, starting transfers between devices: 4.76 us -> 1.31 us  [to_rows(): lax.ppermute(after.astype(jnp.bfloat16), 'x', PLUS)]
    ppermute x2, waiting for transfers between devices: 4.95 us -> 2.34 us  [to_rows(): lax.ppermute(far.astype(jnp.bfloat16), 'x', [(i, (i + 2) % RING) for i in...]
  transfers between devices with their start and end apart: 33 -> 32, of which waited for: 17 -> 14; matrix products, arithmetic and copies ran while one was open for 7% -> 5% of each run, Pallas kernels for 12% -> 7%
where the time goes in v1:
time: 203 us; the launch traced here: 202 us
  waiting for transfers between devices  80.9 us (40%)
  starting transfers between devices  36.6 us (18%)
  Pallas kernels  26.5 us (13%)
  blocking collectives  18.7 us (9%)
  between operations  14.5 us (7%)
  other arithmetic  11.1 us (5%)
  local copies, waits for them, and re-layouts  9.79 us (5%)
  matrix products  3.73 us (2%)
    ppermute x8, waiting for transfers between devices, hop(): return (lax.ppermute(up, Z, UP), lax.ppermute(down, Z, DOWN))  40.6 us
    ppermute x9, waiting for transfers between devices, swap(): return lax.ppermute(value, axis, SWAP)  25.3 us
    all_to_all x1, blocking collectives, local(): lax.all_to_all(piece, ('y', 'x'), split_axis=0, concat_axis=0, tiled=True)  18.7 us
    pallas_call x1, Pallas kernels, pack(): pl.pallas_call(functools.partial(pack_kernel, top), grid=(tiles,), in_spe...  13.5 us
    ppermute x8, starting transfers between devices, hop(): return (lax.ppermute(up, Z, UP), lax.ppermute(down, Z, DOWN))  12.8 us
    pallas_call x1, Pallas kernels, answers_of(): pl.pallas_call(functools.partial(answers_kernel, 0.5 / math.sqrt(model)),...  8.72 us
    ppermute x2, starting transfers between devices, near_sums(): from_after = lax.ppermute(before, axis, MINUS)  6.42 us
    ppermute x2, waiting for transfers between devices, near_sums(): from_before = lax.ppermute(after, axis, PLUS)  6.01 us
  transfers between devices with their start and end apart: 32, of which 14 were waited for; matrix products, arithmetic and copies ran while one was open for 5% of the time, Pallas kernels for 7%

profile of v1, /device:TPU:102, one launch (start us, length us, event | category | flops | bytes accessed | tf_op | source)
XLA Modules:
  0.0 201.9 jit_solution(6798582510102498519)
XLA Ops:
  7.3 2.7 %copy_bitcast_fusion = bf16[64,2,8,768]{3,2,0,1:T(8,128)(2,1)} fusion(bf16[64,2,2,8,768]{4,3,2,1,0:T(8,128)(2,1)} %bitcast.162, s32[]{:T(128)S(6)} %select_n.249), kind=kLoop, calls=%fused_computation.16 | loop fusion | bytes 3145732 | tf_op jit(solution)/shard_map/jit(dynamic_index_in_dim)/squeeze | solution.py:242
  10.0 3.6 %collective-permute-done = bf16[64,2,8,768]{3,2,0,1:T(8,128)(2,1)S(1)} collective-permute-done((bf16[64,2,8,768]{3,2,0,1:T(8,128)(2,1)}, bf16[64,2,8,768]{3,2,0,1:T(8,128)(2,1)S(1)}, u32[]{:S(2)}, u32[]{:S(2)}) %collective-permute-start) | collective-permute-done | bytes 1572896 | tf_op jit(solution)/shard_map/ppermute | solution.py:29
  13.6 2.2 %fusion.5 = bf16[64,8,768]{2,1,0:T(8,128)(2,1)} fusion(bf16[64,2,8,768]{3,2,0,1:T(8,128)(2,1)S(1)} %collective-permute-done, s32[]{:T(128)S(6)} %select_n.245, bf16[64,2,2,8,768]{4,3,2,1,0:T(8,128)(2,1)} %bitcast.163, s32[]{:T(128)S(6)} %select_n.246, s32[]{:T(128)S(6)} %select_n.248), kind=kLoop, calls=%fused_computation.11 | loop fusion | flops 1572864 | bytes 2359308 | tf_op jit(solution)/shard_map/convert_element_type | solution.py:249
  15.9 0.2 fusion.35
  16.3 0.1 concatenate.49
  16.5 0.1 concatenate.51
  16.6 0.1 concatenate.52
  16.7 0.1 copy.59
  16.9 3.5 %fusion.2 = bf16[128,2048]{1,0:T(8,128)(2,1)S(1)} fusion(bf16[128,2048]{1,0:T(8,128)(2,1)S(1)} %bitcast.153, s32[2048]{0:T(1024)S(1)} %fusion.62), kind=kOutput, calls=%fused_computation.5 | convolution fusion | flops 1078198272 | bytes 1056768 | tf_op jit(solution)/shard_map/dot_general | solution.py:280
  20.4 0.9 fusion.11
  21.3 0.2 collective-permute-start.1
  21.5 19.7 %collective-permute-done.1 = bf16[64,8,768]{2,1,0:T(8,128)(2,1)S(1)} collective-permute-done((bf16[64,8,768]{2,1,0:T(8,128)(2,1)}, bf16[64,8,768]{2,1,0:T(8,128)(2,1)S(1)}, u32[]{:S(2)}, u32[]{:S(2)}) %collective-permute-start.1) | collective-permute-done | bytes 786464 | tf_op jit(solution)/shard_map/ppermute | solution.py:29
  41.2 4.0 %fusion.10 = (f32[64,1,1,8,768]{4,3,2,1,0:T(8,128)}, bf16[64,8,768]{2,1,0:T(8,128)(2,1)S(1)}) fusion(bf16[64,8,768]{2,1,0:T(8,128)(2,1)S(1)} %collective-permute-done.1, f32[64,1,1,8,768]{4,3,2,1,0:T(8,128)} %param.9, bf16[64,2,8,768]{3,2,0,1:T(8,128)(2,1)S(1)} %collective-permute-done, s32[]{:T(128)S(6)} %select_n.269, ...), kind=kLoop, calls=%fused_computation.24 | loop fusion | flops 5111808 | bytes 7864332
  45.1 18.7 %all_to_all.5 = bf16[16,8,3072]{2,1,0:T(8,128)(2,1)S(1)} all-to-all(bf16[16,8,3072]{2,1,0:T(8,128)(2,1)S(1)} %bitcast.160), channel_id=1, replica_groups=mesh['z_lo'=2,'core'=2,'y'=4,'x'=4,'z_hi'=4] {'y','x'}, dimensions={0} | all-to-all | bytes 1572864 | tf_op jit(solution)/shard_map/all_to_all | solution.py:294
  63.9 3.1 %collective-permute-start.2 = (bf16[128,3072]{1,0:T(8,128)(2,1)S(1)}, bf16[128,3072]{1,0:T(8,128)(2,1)S(1)}, u32[]{:S(2)}, u32[]{:S(2)}) collective-permute-start(bf16[128,3072]{1,0:T(8,128)(2,1)S(1)} %bitcast.154), channel_id=1, source_target_pairs={{0,128},{128,1},{1,129},{129,2},{2,130},{130,3},{3,131},{131,0},{4... | collective-permute-start | bytes 2359304 | tf_op jit(solution)/shard_map/ppermute | solution.py:298
  67.0 15.1 %collective-permute-done.2.refs_0_ = bf16[128,3072]{1,0:T(8,128)(2,1)S(1)} collective-permute-done((bf16[128,3072]{1,0:T(8,128)(2,1)S(1)}, bf16[128,3072]{1,0:T(8,128)(2,1)S(1)}, u32[]{:S(2)}, u32[]{:S(2)}) %collective-permute-start.2) | collective-permute-done | bytes 786464 | tf_op jit(solution)/shard_map/ppermute | solution.py:298
  82.2 3.7 %collective-permute-start.4 = (bf16[128,3072]{1,0:T(8,128)(2,1)S(1)}, bf16[128,3072]{1,0:T(8,128)(2,1)}, u32[]{:S(2)}, u32[]{:S(2)}) collective-permute-start(bf16[128,3072]{1,0:T(8,128)(2,1)S(1)} %collective-permute-done.2.refs_0_), channel_id=1, source_target_pairs={{0,128},{128,1},{1,129},{129,2},{2,130},{130,3},{3,131},{131,0},{4... | collective-permute-start | bytes 2359304 | tf_op jit(solution)/shard_map/ppermute | solution.py:298
  85.9 1.7 pad_maximum_fusion
  87.5 12.7 %collective-permute-done.4.refs_3_ = bf16[128,3072]{1,0:T(8,128)(2,1)} collective-permute-done((bf16[128,3072]{1,0:T(8,128)(2,1)S(1)}, bf16[128,3072]{1,0:T(8,128)(2,1)}, u32[]{:S(2)}, u32[]{:S(2)}) %collective-permute-start.4) | collective-permute-done | bytes 786464 | tf_op jit(solution)/shard_map/ppermute | solution.py:298
  100.2 3.8 %collective-permute-start.6 = (bf16[128,3072]{1,0:T(8,128)(2,1)}, bf16[128,3072]{1,0:T(8,128)(2,1)S(1)}, u32[]{:S(2)}, u32[]{:S(2)}) collective-permute-start(bf16[128,3072]{1,0:T(8,128)(2,1)} %collective-permute-done.4.refs_3_), channel_id=1, source_target_pairs={{0,128},{128,1},{1,129},{129,2},{2,130},{130,3},{3,131},{131,0},{4... | collective-permute-start | bytes 2359304 | tf_op jit(solution)/shard_map/ppermute | solution.py:298
  104.0 0.5 collective-permute-start.12
  104.5 13.5 %shard_map.94 = (bf16[4,384,2048]{2,1,0:T(8,128)(2,1)}, bf16[2048,384]{1,0:T(8,128)(2,1)S(1)}) custom-call(s32[1]{0:T(128)} %bitcast.1.where_ref, bf16[2048,2176]{1,0:T(8,128)(2,1)} %all-gather.2.cloned.1.call-done.row_ref), custom_call_target="tpu_custom_call" | custom-call | flops 1610612736 | bytes 15204352 | tf_op jit(solution)/shard_map/pallas_call | solution.py:104
  118.0 3.2 %collective-permute-done.7.refs_1_ = bf16[128,3072]{1,0:T(8,128)(2,1)} collective-permute-done((bf16[128,3072]{1,0:T(8,128)(2,1)}, bf16[128,3072]{1,0:T(8,128)(2,1)}, u32[]{:S(2)}, u32[]{:S(2)}) %collective-permute-start.7) | collective-permute-done | bytes 786464 | tf_op jit(solution)/shard_map/ppermute | solution.py:298
  121.2 0.3 collective-permute-start.8
  121.4 1.0 slice.135
  122.4 1.9 collective-permute-start.9
  124.4 0.5 collective-permute-start.14
  124.9 5.0 %collective-permute-done.8.refs_7_ = bf16[64,3072]{1,0:T(8,128)(2,1)S(1)} collective-permute-done((bf16[64,3072]{1,0:T(8,128)(2,1)S(1)}, bf16[64,3072]{1,0:T(8,128)(2,1)S(1)}, u32[]{:S(2)}, u32[]{:S(2)}) %collective-permute-start.8) | collective-permute-done | bytes 393248 | tf_op jit(solution)/shard_map/ppermute | solution.py:298
  129.9 4.6 %collective-permute-done.9.refs_8_ = bf16[64,3072]{1,0:T(8,128)(2,1)} collective-permute-done((bf16[64,3072]{1,0:T(8,128)(2,1)S(1)}, bf16[64,3072]{1,0:T(8,128)(2,1)}, u32[]{:S(2)}, u32[]{:S(2)}) %collective-permute-start.9) | collective-permute-done | bytes 393248 | tf_op jit(solution)/shard_map/ppermute | solution.py:298
  134.5 2.0 %collective-permute-done.16.refs_15_ = bf16[64,3072]{1,0:T(8,128)(2,1)} collective-permute-done((bf16[64,3072]{1,0:T(8,128)(2,1)}, bf16[64,3072]{1,0:T(8,128)(2,1)}, u32[]{:S(2)}, u32[]{:S(2)}) %collective-permute-start.16) | collective-permute-done | bytes 393248 | tf_op jit(solution)/shard_map/ppermute | solution.py:29
  136.6 1.1 copy-done.3
  137.7 1.1 copy-done.5
  138.8 8.7 %shard_map.96 = (bf16[4,384,768]{2,1,0:T(8,128)(2,1)S(1)}, bf16[2048,768]{1,0:T(8,128)(2,1)S(1)}) custom-call(s32[1]{0:T(128)} %bitcast.which_ref, bf16[4,384,2048]{2,1,0:T(8,128)(2,1)} %get-tuple-element.16.packed_ref, bf16[128,3072]{1,0:T(8,128)(2,1)S(1)} %copy-done.3, bf16[128,3072]{1,0:T(8,128)(2,1)S(1)} %bitcast.157, bf16[128,3072]{1,0:T(8,128)(2,1)S(1)} %copy-done.5, ...), custom_call_target="tpu_custom_call" | custom-call | flops 4831838208 | bytes 21233664 | tf_op jit(solution)/shard_map/pallas_call | solution.py:159
  147.6 0.4 shard_map.97.first_ref
  148.1 2.0 shard_map.98.first_ref
  150.1 0.2 convert.59
  150.3 0.3 shard_map.99.first_ref
  150.6 1.5 shard_map.100
  152.2 1.4 collective-permute-start.17
  153.6 1.9 collective-permute-start.19
  155.5 0.2 collective-permute-start.24
  155.7 3.1 %collective-permute-start.26 = (bf16[256,256]{1,0:T(8,128)(2,1)S(1)}, bf16[256,256]{1,0:T(8,128)(2,1)S(1)}, u32[]{:S(2)}, u32[]{:S(2)}) collective-permute-start(bf16[256,256]{1,0:T(8,128)(2,1)S(1)} %get-tuple-element.53), channel_id=1, source_target_pairs={{0,48},{16,0},{32,16},{48,32},{1,49},{17,1},{33,17},{49,33},{2,50}... | collective-permute-start | bytes 393224 | tf_op jit(solution)/shard_map/ppermute | solution.py:50
  158.9 0.2 fusion.86
  159.1 0.5 maximum_select_fusion
  160.2 4.4 %collective-permute-done.24 = bf16[256,256]{1,0:T(8,128)(2,1)S(1)} collective-permute-done((bf16[256,256]{1,0:T(8,128)(2,1)S(1)}, bf16[256,256]{1,0:T(8,128)(2,1)S(1)}, u32[]{:S(2)}, u32[]{:S(2)}) %collective-permute-start.24) | collective-permute-done | bytes 131104 | tf_op jit(solution)/shard_map/ppermute | solution.py:49
  164.7 0.3 collective-permute-start.25
  165.0 3.1 %collective-permute-start.27 = (bf16[512,256]{1,0:T(8,128)(2,1)S(1)}, bf16[512,256]{1,0:T(8,128)(2,1)S(1)}, u32[]{:S(2)}, u32[]{:S(2)}) collective-permute-start(bf16[512,256]{1,0:T(8,128)(2,1)S(1)} %pad_maximum_fusion.4), channel_id=1, source_target_pairs={{0,48},{16,0},{32,16},{48,32},{1,49},{17,1},{33,17},{49,33},{2,50}... | collective-permute-start | bytes 786440 | tf_op jit(solution)/shard_map/ppermute | solution.py:58
  168.1 0.2 fusion.17
  168.5 3.3 %collective-permute-start.20 = (bf16[512,512]{1,0:T(8,128)(2,1)S(1)}, bf16[512,512]{1,0:T(8,128)(2,1)S(1)}, u32[]{:S(2)}, u32[]{:S(2)}) collective-permute-start(bf16[512,512]{1,0:T(8,128)(2,1)S(1)} %pad_maximum_fusion.2), channel_id=1, source_target_pairs={{0,48},{16,0},{32,16},{48,32},{1,49},{17,1},{33,17},{49,33},{2,50}... | collective-permute-start | bytes 1572872 | tf_op jit(solution)/shard_map/ppermute | solution.py:58
  171.8 0.3 dynamic-slice_bitcast_fusion
  172.0 2.0 copy.61
  174.0 1.2 collective-permute-done.25
  175.3 2.5 %collective-permute-start.28 = (bf16[128,256]{1,0:T(8,128)(2,1)S(1)}, bf16[128,256]{1,0:T(8,128)(2,1)S(1)}, u32[]{:S(2)}, u32[]{:S(2)}) collective-permute-start(bf16[128,256]{1,0:T(8,128)(2,1)S(1)} %get-tuple-element.49), channel_id=1, source_target_pairs={{0,8},{4,12},{8,0},{12,4},{1,9},{5,13},{9,1},{13,5},{2,10},{6,14},... | collective-permute-start | bytes 196616 | tf_op jit(solution)/shard_map/ppermute | solution.py:322
  177.9 0.8 collective-permute-start.29
  178.7 1.2 collective-permute-start.30
  179.9 4.8 %collective-permute-done.18 = bf16[512,512]{1,0:T(8,128)(2,1)S(1)} collective-permute-done((bf16[512,512]{1,0:T(8,128)(2,1)S(1)}, bf16[512,512]{1,0:T(8,128)(2,1)S(1)}, u32[]{:S(2)}, u32[]{:S(2)}) %collective-permute-start.18) | collective-permute-done | bytes 524320 | tf_op jit(solution)/shard_map/ppermute | solution.py:57
  184.7 0.2 fusion.9
  185.0 2.5 %collective-permute-start.21 = (bf16[128,512]{1,0:T(8,128)(2,1)S(1)}, bf16[128,512]{1,0:T(8,128)(2,1)S(1)}, u32[]{:S(2)}, u32[]{:S(2)}) collective-permute-start(bf16[128,512]{1,0:T(8,128)(2,1)S(1)} %get-tuple-element.42), channel_id=1, source_target_pairs={{0,8},{4,12},{8,0},{12,4},{1,9},{5,13},{9,1},{13,5},{2,10},{6,14},... | collective-permute-start | bytes 393224 | tf_op jit(solution)/shard_map/ppermute | solution.py:322
  187.6 0.5 collective-permute-start.22
  188.1 1.5 collective-permute-start.23
  189.7 2.3 %collective-permute-done.21 = bf16[128,512]{1,0:T(8,128)(2,1)S(1)} collective-permute-done((bf16[128,512]{1,0:T(8,128)(2,1)S(1)}, bf16[128,512]{1,0:T(8,128)(2,1)S(1)}, u32[]{:S(2)}, u32[]{:S(2)}) %collective-permute-start.21) | collective-permute-done | bytes 131104 | tf_op jit(solution)/shard_map/ppermute | solution.py:322
  192.0 0.6 collective-permute-done.22
  192.6 1.6 collective-permute-done.23
  194.3 0.7 pad_maximum_fusion.5
  (89 shorter events, 1.8 us)
Async XLA Ops:
  7.2 9.7 %copy-start = (bf16[4,32,2048]{2,1,0:T(8,128)(2,1)S(1)}, bf16[4,32,2048]{2,1,0:T(8,128)(2,1)}, u32[]{:S(2)}) copy-start(bf16[4,32,2048]{2,1,0:T(8,128)(2,1)} %param.10) | copy-start | bytes 1572868
  7.2 8.6 %copy-start.6 = (s32[4,32,8]{1,2,0:T(8,128)S(1)}, s32[4,32,8]{1,2,0:T(8,128)}, u32[]{:S(2)}) copy-start(s32[4,32,8]{1,2,0:T(8,128)} %param.11) | copy-start | bytes 12292
  7.2 9.3 %copy-start.7 = (f32[4,32,8]{1,2,0:T(8,128)S(1)}, f32[4,32,8]{1,2,0:T(8,128)}, u32[]{:S(2)}) copy-start(f32[4,32,8]{1,2,0:T(8,128)} %param.12) | copy-start | bytes 12292
  7.2 97.3 %all-gather.2.cloned.1.call-start = ((), (), s32[]{:S(2)}) async-start(), calls=%async_computation.1 | async-start | bytes 9469952 | tf_op jit(solution)/shard_map/all_gather | solution.py:286
  10.0 3.6 %collective-permute-start = (bf16[64,2,8,768]{3,2,0,1:T(8,128)(2,1)}, bf16[64,2,8,768]{3,2,0,1:T(8,128)(2,1)S(1)}, u32[]{:S(2)}, u32[]{:S(2)}) collective-permute-start(bf16[64,2,8,768]{3,2,0,1:T(8,128)(2,1)} %copy_bitcast_fusion), channel_id=1, source_target_pairs={{0,64},{64,0},{1,65},{65,1},{2,66},{66,2},{3,67},{67,3},{4,68},{68... | collective-permute-start | bytes 4718600 | tf_op jit(solution)/shard_map/ppermute | solution.py:29
  21.3 19.9 %collective-permute-start.1 = (bf16[64,8,768]{2,1,0:T(8,128)(2,1)}, bf16[64,8,768]{2,1,0:T(8,128)(2,1)S(1)}, u32[]{:S(2)}, u32[]{:S(2)}) collective-permute-start(bf16[64,8,768]{2,1,0:T(8,128)(2,1)} %fusion.5), channel_id=1, source_target_pairs={{0,128},{128,0},{1,129},{129,1},{2,130},{130,2},{3,131},{131,3},{4... | collective-permute-start | bytes 2359304 | tf_op jit(solution)/shard_map/ppermute | solution.py:29
  63.9 18.3 %collective-permute-start.2 = (bf16[128,3072]{1,0:T(8,128)(2,1)S(1)}, bf16[128,3072]{1,0:T(8,128)(2,1)S(1)}, u32[]{:S(2)}, u32[]{:S(2)}) collective-permute-start(bf16[128,3072]{1,0:T(8,128)(2,1)S(1)} %bitcast.154), channel_id=1, source_target_pairs={{0,128},{128,1},{1,129},{129,2},{2,130},{130,3},{3,131},{131,0},{4... | collective-permute-start | bytes 2359304 | tf_op jit(solution)/shard_map/ppermute | solution.py:298
  67.0 18.8 %collective-permute-start.3 = (bf16[128,3072]{1,0:T(8,128)(2,1)S(1)}, bf16[128,3072]{1,0:T(8,128)(2,1)S(1)}, u32[]{:S(2)}, u32[]{:S(2)}) collective-permute-start(bf16[128,3072]{1,0:T(8,128)(2,1)S(1)} %bitcast.155), channel_id=1, source_target_pairs={{128,0},{1,128},{129,1},{2,129},{130,2},{3,130},{131,3},{0,131},{1... | collective-permute-start | bytes 2359304 | tf_op jit(solution)/shard_map/ppermute | solution.py:298
  82.2 5.4 %copy-start.2 = (bf16[128,3072]{1,0:T(8,128)(2,1)}, bf16[128,3072]{1,0:T(8,128)(2,1)S(1)}, u32[]{:S(2)}) copy-start(bf16[128,3072]{1,0:T(8,128)(2,1)S(1)} %collective-permute-done.2.refs_0_) | copy-start | bytes 2359300
  82.2 18.0 %collective-permute-start.4 = (bf16[128,3072]{1,0:T(8,128)(2,1)S(1)}, bf16[128,3072]{1,0:T(8,128)(2,1)}, u32[]{:S(2)}, u32[]{:S(2)}) collective-permute-start(bf16[128,3072]{1,0:T(8,128)(2,1)S(1)} %collective-permute-done.2.refs_0_), channel_id=1, source_target_pairs={{0,128},{128,1},{1,129},{129,2},{2,130},{130,3},{3,131},{131,0},{4... | collective-permute-start | bytes 2359304 | tf_op jit(solution)/shard_map/ppermute | solution.py:298
  85.9 14.3 %copy-start.4 = (bf16[128,3072]{1,0:T(8,128)(2,1)}, bf16[128,3072]{1,0:T(8,128)(2,1)S(1)}, u32[]{:S(2)}) copy-start(bf16[128,3072]{1,0:T(8,128)(2,1)S(1)} %collective-permute-done.3.refs_2_) | copy-start | bytes 2359300
  85.9 18.1 %collective-permute-start.5 = (bf16[128,3072]{1,0:T(8,128)(2,1)S(1)}, bf16[128,3072]{1,0:T(8,128)(2,1)}, u32[]{:S(2)}, u32[]{:S(2)}) collective-permute-start(bf16[128,3072]{1,0:T(8,128)(2,1)S(1)} %collective-permute-done.3.refs_2_), channel_id=1, source_target_pairs={{128,0},{1,128},{129,1},{2,129},{130,2},{3,130},{131,3},{0,131},{1... | collective-permute-start | bytes 2359304 | tf_op jit(solution)/shard_map/ppermute | solution.py:298
  87.5 47.0 %collective-permute-start.10 = (bf16[384,3072]{1,0:T(8,128)(2,1)}, bf16[384,3072]{1,0:T(8,128)(2,1)}, u32[]{:S(2)}, u32[]{:S(2)}) collective-permute-start(bf16[384,3072]{1,0:T(8,128)(2,1)} %pad_maximum_fusion), channel_id=1, source_target_pairs={{0,64},{64,0},{1,65},{65,1},{2,66},{66,2},{3,67},{67,3},{4,68},{68... | collective-permute-start | bytes 7077896 | tf_op jit(solution)/shard_map/ppermute | solution.py:29
  100.2 17.8 %collective-permute-start.6 = (bf16[128,3072]{1,0:T(8,128)(2,1)}, bf16[128,3072]{1,0:T(8,128)(2,1)S(1)}, u32[]{:S(2)}, u32[]{:S(2)}) collective-permute-start(bf16[128,3072]{1,0:T(8,128)(2,1)} %collective-permute-done.4.refs_3_), channel_id=1, source_target_pairs={{0,128},{128,1},{1,129},{129,2},{2,130},{130,3},{3,131},{131,0},{4... | collective-permute-start | bytes 2359304 | tf_op jit(solution)/shard_map/ppermute | solution.py:298
  104.0 17.1 %collective-permute-start.7 = (bf16[128,3072]{1,0:T(8,128)(2,1)}, bf16[128,3072]{1,0:T(8,128)(2,1)}, u32[]{:S(2)}, u32[]{:S(2)}) collective-permute-start(bf16[128,3072]{1,0:T(8,128)(2,1)} %collective-permute-done.5.refs_4_), channel_id=1, source_target_pairs={{128,0},{1,128},{129,1},{2,129},{130,2},{3,130},{131,3},{0,131},{1... | collective-permute-start | bytes 2359304 | tf_op jit(solution)/shard_map/ppermute | solution.py:298
  104.0 20.4 %collective-permute-start.11 = (bf16[128,3072]{1,0:T(8,128)(2,1)}, bf16[128,3072]{1,0:T(8,128)(2,1)}, u32[]{:S(2)}, u32[]{:S(2)}) collective-permute-start(bf16[128,3072]{1,0:T(8,128)(2,1)} %collective-permute-done.4.refs_3_), channel_id=1, source_target_pairs={{0,64},{64,0},{1,65},{65,1},{2,66},{66,2},{3,67},{67,3},{4,68},{68... | collective-permute-start | bytes 2359304 | tf_op jit(solution)/shard_map/ppermute | solution.py:29
  104.0 20.4 %collective-permute-start.12 = (bf16[128,3072]{1,0:T(8,128)(2,1)}, bf16[128,3072]{1,0:T(8,128)(2,1)}, u32[]{:S(2)}, u32[]{:S(2)}) collective-permute-start(bf16[128,3072]{1,0:T(8,128)(2,1)} %collective-permute-done.5.refs_4_), channel_id=1, source_target_pairs={{0,64},{64,0},{1,65},{65,1},{2,66},{66,2},{3,67},{67,3},{4,68},{68... | collective-permute-start | bytes 2359304 | tf_op jit(solution)/shard_map/ppermute | solution.py:29
  118.0 16.5 %copy-start.8 = (s32[3]{0:T(128)S(1)}, s32[3]{0:T(128)}, u32[]{:S(2)}) copy-start(s32[3]{0:T(128)} %constant.351.clone) | copy-start | bytes 40
  121.2 8.7 %collective-permute-start.8 = (bf16[64,3072]{1,0:T(8,128)(2,1)S(1)}, bf16[64,3072]{1,0:T(8,128)(2,1)S(1)}, u32[]{:S(2)}, u32[]{:S(2)}) collective-permute-start(bf16[64,3072]{1,0:T(8,128)(2,1)S(1)} %slice.134), channel_id=1, source_target_pairs={{0,128},{128,1},{1,129},{129,2},{2,130},{130,3},{3,131},{131,0},{4... | collective-permute-start | bytes 1179656 | tf_op jit(solution)/shard_map/ppermute | solution.py:298
  122.4 12.1 %collective-permute-start.9 = (bf16[64,3072]{1,0:T(8,128)(2,1)S(1)}, bf16[64,3072]{1,0:T(8,128)(2,1)}, u32[]{:S(2)}, u32[]{:S(2)}) collective-permute-start(bf16[64,3072]{1,0:T(8,128)(2,1)S(1)} %slice.135), channel_id=1, source_target_pairs={{128,0},{1,128},{129,1},{2,129},{130,2},{3,130},{131,3},{0,131},{1... | collective-permute-start | bytes 1179656 | tf_op jit(solution)/shard_map/ppermute | solution.py:298
  124.4 12.2 %collective-permute-start.13 = (bf16[128,3072]{1,0:T(8,128)(2,1)S(1)}, bf16[128,3072]{1,0:T(8,128)(2,1)}, u32[]{:S(2)}, u32[]{:S(2)}) collective-permute-start(bf16[128,3072]{1,0:T(8,128)(2,1)S(1)} %get-tuple-element.18.refs_5_), channel_id=1, source_target_pairs={{0,64},{64,0},{1,65},{65,1},{2,66},{66,2},{3,67},{67,3},{4,68},{68... | collective-permute-start | bytes 2359304 | tf_op jit(solution)/shard_map/ppermute | solution.py:29
  124.4 12.2 %collective-permute-start.14 = (bf16[128,3072]{1,0:T(8,128)(2,1)}, bf16[128,3072]{1,0:T(8,128)(2,1)}, u32[]{:S(2)}, u32[]{:S(2)}) collective-permute-start(bf16[128,3072]{1,0:T(8,128)(2,1)} %get-tuple-element.19.refs_6_), channel_id=1, source_target_pairs={{0,64},{64,0},{1,65},{65,1},{2,66},{66,2},{3,67},{67,3},{4,68},{68... | collective-permute-start | bytes 2359304 | tf_op jit(solution)/shard_map/ppermute | solution.py:29
  129.9 4.6 %collective-permute-start.15 = (bf16[64,3072]{1,0:T(8,128)(2,1)S(1)}, bf16[64,3072]{1,0:T(8,128)(2,1)}, u32[]{:S(2)}, u32[]{:S(2)}) collective-permute-start(bf16[64,3072]{1,0:T(8,128)(2,1)S(1)} %collective-permute-done.8.refs_7_), channel_id=1, source_target_pairs={{0,64},{64,0},{1,65},{65,1},{2,66},{66,2},{3,67},{67,3},{4,68},{68... | collective-permute-start | bytes 1179656 | tf_op jit(solution)/shard_map/ppermute | solution.py:29
  134.5 2.1 %collective-permute-start.16 = (bf16[64,3072]{1,0:T(8,128)(2,1)}, bf16[64,3072]{1,0:T(8,128)(2,1)}, u32[]{:S(2)}, u32[]{:S(2)}) collective-permute-start(bf16[64,3072]{1,0:T(8,128)(2,1)} %collective-permute-done.9.refs_8_), channel_id=1, source_target_pairs={{0,64},{64,0},{1,65},{65,1},{2,66},{66,2},{3,67},{67,3},{4,68},{68... | collective-permute-start | bytes 1179656 | tf_op jit(solution)/shard_map/ppermute | solution.py:29
  136.6 1.1 copy-start.3
  137.7 1.1 copy-start.5
  152.2 16.0 %collective-permute-start.17 = (bf16[256,512]{1,0:T(8,128)(2,1)S(1)}, bf16[256,512]{1,0:T(8,128)(2,1)S(1)}, u32[]{:S(2)}, u32[]{:S(2)}) collective-permute-start(bf16[256,512]{1,0:T(8,128)(2,1)S(1)} %get-tuple-element.47), channel_id=1, source_target_pairs={{0,16},{16,32},{32,48},{48,0},{1,17},{17,33},{33,49},{49,1},{2,18}... | collective-permute-start | bytes 786440 | tf_op jit(solution)/shard_map/ppermute | solution.py:49
  153.6 14.6 %collective-permute-start.19 = (bf16[256,512]{1,0:T(8,128)(2,1)S(1)}, bf16[256,512]{1,0:T(8,128)(2,1)S(1)}, u32[]{:S(2)}, u32[]{:S(2)}) collective-permute-start(bf16[256,512]{1,0:T(8,128)(2,1)S(1)} %get-tuple-element.48), channel_id=1, source_target_pairs={{0,48},{16,0},{32,16},{48,32},{1,49},{17,1},{33,17},{49,33},{2,50}... | collective-permute-start | bytes 786440 | tf_op jit(solution)/shard_map/ppermute | solution.py:50
  155.5 9.1 %collective-permute-start.24 = (bf16[256,256]{1,0:T(8,128)(2,1)S(1)}, bf16[256,256]{1,0:T(8,128)(2,1)S(1)}, u32[]{:S(2)}, u32[]{:S(2)}) collective-permute-start(bf16[256,256]{1,0:T(8,128)(2,1)S(1)} %get-tuple-element.52), channel_id=1, source_target_pairs={{0,16},{16,32},{32,48},{48,0},{1,17},{17,33},{33,49},{49,1},{2,18}... | collective-permute-start | bytes 393224 | tf_op jit(solution)/shard_map/ppermute | solution.py:49
  155.7 8.9 %collective-permute-start.26 = (bf16[256,256]{1,0:T(8,128)(2,1)S(1)}, bf16[256,256]{1,0:T(8,128)(2,1)S(1)}, u32[]{:S(2)}, u32[]{:S(2)}) collective-permute-start(bf16[256,256]{1,0:T(8,128)(2,1)S(1)} %get-tuple-element.53), channel_id=1, source_target_pairs={{0,48},{16,0},{32,16},{48,32},{1,49},{17,1},{33,17},{49,33},{2,50}... | collective-permute-start | bytes 393224 | tf_op jit(solution)/shard_map/ppermute | solution.py:50
  164.7 10.5 %collective-permute-start.25 = (bf16[512,256]{1,0:T(8,128)(2,1)S(1)}, bf16[512,256]{1,0:T(8,128)(2,1)S(1)}, u32[]{:S(2)}, u32[]{:S(2)}) collective-permute-start(bf16[512,256]{1,0:T(8,128)(2,1)S(1)} %pad_maximum_fusion.3), channel_id=1, source_target_pairs={{0,16},{16,32},{32,48},{48,0},{1,17},{17,33},{33,49},{49,1},{2,18}... | collective-permute-start | bytes 786440 | tf_op jit(solution)/shard_map/ppermute | solution.py:57
  165.0 10.3 %collective-permute-start.27 = (bf16[512,256]{1,0:T(8,128)(2,1)S(1)}, bf16[512,256]{1,0:T(8,128)(2,1)S(1)}, u32[]{:S(2)}, u32[]{:S(2)}) collective-permute-start(bf16[512,256]{1,0:T(8,128)(2,1)S(1)} %pad_maximum_fusion.4), channel_id=1, source_target_pairs={{0,48},{16,0},{32,16},{48,32},{1,49},{17,1},{33,17},{49,33},{2,50}... | collective-permute-start | bytes 786440 | tf_op jit(solution)/shard_map/ppermute | solution.py:58
  168.3 16.4 %collective-permute-start.18 = (bf16[512,512]{1,0:T(8,128)(2,1)S(1)}, bf16[512,512]{1,0:T(8,128)(2,1)S(1)}, u32[]{:S(2)}, u32[]{:S(2)}) collective-permute-start(bf16[512,512]{1,0:T(8,128)(2,1)S(1)} %pad_maximum_fusion.1), channel_id=1, source_target_pairs={{0,16},{16,32},{32,48},{48,0},{1,17},{17,33},{33,49},{49,1},{2,18}... | collective-permute-start | bytes 1572872 | tf_op jit(solution)/shard_map/ppermute | solution.py:57
  168.5 16.3 %collective-permute-start.20 = (bf16[512,512]{1,0:T(8,128)(2,1)S(1)}, bf16[512,512]{1,0:T(8,128)(2,1)S(1)}, u32[]{:S(2)}, u32[]{:S(2)}) collective-permute-start(bf16[512,512]{1,0:T(8,128)(2,1)S(1)} %pad_maximum_fusion.2), channel_id=1, source_target_pairs={{0,48},{16,0},{32,16},{48,32},{1,49},{17,1},{33,17},{49,33},{2,50}... | collective-permute-start | bytes 1572872 | tf_op jit(solution)/shard_map/ppermute | solution.py:58
  175.2 19.8 %copy-start.1 = (bf16[4,32,2048]{2,1,0:T(8,128)(2,1)S(1)}, bf16[4,32,2048]{2,1,0:T(8,128)(2,1)}, u32[]{:S(2)}) copy-start(bf16[4,32,2048]{2,1,0:T(8,128)(2,1)} %param.10) | copy-start | bytes 1572868
  175.3 12.7 %collective-permute-start.28 = (bf16[128,256]{1,0:T(8,128)(2,1)S(1)}, bf16[128,256]{1,0:T(8,128)(2,1)S(1)}, u32[]{:S(2)}, u32[]{:S(2)}) collective-permute-start(bf16[128,256]{1,0:T(8,128)(2,1)S(1)} %get-tuple-element.49), channel_id=1, source_target_pairs={{0,8},{4,12},{8,0},{12,4},{1,9},{5,13},{9,1},{13,5},{2,10},{6,14},... | collective-permute-start | bytes 196616 | tf_op jit(solution)/shard_map/ppermute | solution.py:322
  177.9 11.7 %collective-permute-start.29 = (bf16[128,256]{1,0:T(8,128)(2,1)S(1)}, bf16[128,256]{1,0:T(8,128)(2,1)S(1)}, u32[]{:S(2)}, u32[]{:S(2)}) collective-permute-start(bf16[128,256]{1,0:T(8,128)(2,1)S(1)} %get-tuple-element.51), channel_id=1, source_target_pairs={{0,4},{4,8},{8,12},{12,0},{1,5},{5,9},{9,13},{13,1},{2,6},{6,10},{... | collective-permute-start | bytes 196616 | tf_op jit(solution)/shard_map/ppermute | solution.py:323
  178.7 10.9 %collective-permute-start.30 = (bf16[128,256]{1,0:T(8,128)(2,1)S(1)}, bf16[128,256]{1,0:T(8,128)(2,1)S(1)}, u32[]{:S(2)}, u32[]{:S(2)}) collective-permute-start(bf16[128,256]{1,0:T(8,128)(2,1)S(1)} %get-tuple-element.50), channel_id=1, source_target_pairs={{0,12},{4,0},{8,4},{12,8},{1,13},{5,1},{9,5},{13,9},{2,14},{6,2},{... | collective-permute-start | bytes 196616 | tf_op jit(solution)/shard_map/ppermute | solution.py:324
  185.0 7.0 %collective-permute-start.21 = (bf16[128,512]{1,0:T(8,128)(2,1)S(1)}, bf16[128,512]{1,0:T(8,128)(2,1)S(1)}, u32[]{:S(2)}, u32[]{:S(2)}) collective-permute-start(bf16[128,512]{1,0:T(8,128)(2,1)S(1)} %get-tuple-element.42), channel_id=1, source_target_pairs={{0,8},{4,12},{8,0},{12,4},{1,9},{5,13},{9,1},{13,5},{2,10},{6,14},... | collective-permute-start | bytes 393224 | tf_op jit(solution)/shard_map/ppermute | solution.py:322
  187.6 5.0 %collective-permute-start.22 = (bf16[128,512]{1,0:T(8,128)(2,1)S(1)}, bf16[128,512]{1,0:T(8,128)(2,1)S(1)}, u32[]{:S(2)}, u32[]{:S(2)}) collective-permute-start(bf16[128,512]{1,0:T(8,128)(2,1)S(1)} %get-tuple-element.44), channel_id=1, source_target_pairs={{0,4},{4,8},{8,12},{12,0},{1,5},{5,9},{9,13},{13,1},{2,6},{6,10},{... | collective-permute-start | bytes 393224 | tf_op jit(solution)/shard_map/ppermute | solution.py:323
  188.1 6.2 %collective-permute-start.23 = (bf16[128,512]{1,0:T(8,128)(2,1)S(1)}, bf16[128,512]{1,0:T(8,128)(2,1)S(1)}, u32[]{:S(2)}, u32[]{:S(2)}) collective-permute-start(bf16[128,512]{1,0:T(8,128)(2,1)S(1)} %get-tuple-element.43), channel_id=1, source_target_pairs={{0,12},{4,0},{8,4},{12,8},{1,13},{5,1},{9,5},{13,9},{2,14},{6,2},{... | collective-permute-start | bytes 393224 | tf_op jit(solution)/shard_map/ppermute | solution.py:324
Sparse Core Ops, SparseCore 0:
  21.4 79.9 all-gather.1

commit v2 on v1

--- a/solution.py
+++ b/solution.py
@@ -184,7 +184,7 @@
 
 def unpack_kernel(rows, where_ref, spread_ref, answers_ref, first_ref, out_ref):
     slots = GROUPS * CAP
-    tile = GROUPS * rows
+    tile = min(GROUPS * rows, spread_ref.shape[0])
     for start in range(0, spread_ref.shape[0], tile):
         part = start // tile * slots
         held = [answers_ref[i, part : part + slots] for i in range(RING)]
@@ -196,22 +196,30 @@
         out_ref[0, start : start + tile] = out.astype(out_ref.dtype)
 
 
-def unpack(where, spread, answers, part, rows, dtype, first):
+def unpack(where, spread, answers, part, axis, rows, dtype, first):
     blocks = where.shape[0]
     count, wide = spread.shape[0] // RING, spread.shape[1]
     slots, columns = answers.shape[1] // RING, part[1] - part[0]
     column = part[0] // columns
+    if axis == "y":
+        grid = (blocks, 1)
+        spread_spec = pl.BlockSpec((count, wide), lambda i, j, where: (where[i], 0))
+        answers_spec = pl.BlockSpec((RING, slots, columns), lambda i, j, where: (0, where[i], column))
+        out_spec = pl.BlockSpec((1, count, columns), lambda i, j, where: (i, 0, 0))
+    else:
+        grid = (blocks, RING)
+        spread_spec = pl.BlockSpec((count // RING, wide), lambda i, j, where: (j * RING + where[i], 0))
+        answers_spec = pl.BlockSpec(
+            (RING, slots // 2, columns), lambda i, j, where: (0, j * 2 + where[i] // 2, column)
+        )
+        out_spec = pl.BlockSpec((1, count // RING, columns), lambda i, j, where: (i, j, 0))
     return pl.pallas_call(
         functools.partial(unpack_kernel, rows),
         grid_spec=pltpu.PrefetchScalarGridSpec(
             num_scalar_prefetch=1,
-            grid=(blocks,),
-            in_specs=[
-                pl.BlockSpec((count, wide), lambda i, where: (where[i], 0)),
-                pl.BlockSpec((RING, slots, columns), lambda i, where: (0, where[i], column)),
-                pl.BlockSpec(memory_space=pl.ANY),
-            ],
-            out_specs=pl.BlockSpec((1, count, columns), lambda i, where: (i, 0, 0)),
+            grid=grid,
+            in_specs=[spread_spec, answers_spec, pl.BlockSpec(memory_space=pl.ANY)],
+            out_specs=out_spec,
         ),
         out_shape=jax.ShapeDtypeStruct((blocks, count, columns), dtype),
         compiler_params=pltpu.CompilerParams(vmem_limit_bytes=18 * 2**20),
@@ -234,8 +242,7 @@
     taken = steps * rows
     owners = RING * RING
     span = owners * sub
-    cut = 2 * width // 3
-    parts = [(0, cut), (cut, width)]
+    cut = width // 2
 
     pieces = deltas[0].reshape(experts, 2, 2, sub, width)
     kept = lax.dynamic_index_in_dim(pieces, core, axis=2, keepdims=False)
@@ -309,34 +316,40 @@
     rest = [up2, down2, up, down, low, high]
     pieces = first + rest + [swap(jnp.concatenate(first), "core")] + [swap(part, "core") for part in rest]
     answers, engine = answers_of(z_hi.reshape(1), packed, pieces)
-    far_block = ((y + 2) % RING).reshape(1)
-    near_blocks = (y + jnp.array([3, 1, 0], jnp.int32)) % RING
-
-    def to_rows(ringed):
-        ringed = ringed.reshape(RING, taken, -1)
+
+    def last_ring(summed, axis, at):
+        summed = summed.reshape(RING, taken, -1)
         own, before, after, far = [
-            lax.dynamic_index_in_dim(ringed, (x + offset) % RING, axis=0, keepdims=False)
+            lax.dynamic_index_in_dim(summed, (at + offset) % RING, axis=0, keepdims=False)
             for offset in (0, 3, 1, 2)
         ]
         received = [
-            lax.ppermute(far.astype(jnp.bfloat16), "x", [(i, (i + 2) % RING) for i in range(RING)]),
-            lax.ppermute(after.astype(jnp.bfloat16), "x", PLUS),
-            lax.ppermute(before.astype(jnp.bfloat16), "x", MINUS),
+            lax.ppermute(far.astype(jnp.bfloat16), axis, [(i, (i + 2) % RING) for i in range(RING)]),
+            lax.ppermute(after.astype(jnp.bfloat16), axis, PLUS),
+            lax.ppermute(before.astype(jnp.bfloat16), axis, MINUS),
         ]
         for value in received:
             own = own + value.astype(jnp.float32)
         return own
 
+    ways = [((0, cut), "y", y, "x", x), ((cut, width), "x", x, "y", y)]
     first = spread
-    decoded = []
-    for part in parts:
-        far = first = unpack(far_block, spread, answers, part, rows, jnp.bfloat16, first)
-        near = first = unpack(near_blocks, spread, answers, part, rows, jnp.float32, first)
-        before, after = far_sums(near[0], near[1], far[0], "y")
-        decoded.append(to_rows(near_sums(near[2], before, after, "y")))
+    fars, nears, decoded = [], [], []
+    for part, axis, at, _, _ in ways:
+        block = ((at + 2) % RING).reshape(1)
+        first = unpack(block, spread, answers, part, axis, rows, jnp.bfloat16, first)
+        fars.append(first)
+    for part, axis, at, _, _ in ways:
+        near_blocks = (at + jnp.array([3, 1, 0], jnp.int32)) % RING
+        first = unpack(near_blocks, spread, answers, part, axis, rows, jnp.float32, first)
+        nears.append(first)
+    for far, terms, (_, axis, _, second, at) in zip(fars, nears, ways):
+        before, after = far_sums(terms[0], terms[1], far[0], axis)
+        decoded.append(last_ring(near_sums(terms[2], before, after, axis), second, at))
+    (engine,) = passed_on([engine], before)
     decoded = jnp.concatenate(decoded, axis=1).reshape(steps, rows, width).astype(jnp.bfloat16)
 
-    engine = later(engine, near).reshape(2, CHIPS, owners, sub, width)
+    engine = engine.reshape(2, CHIPS, owners, sub, width)
     engine = by_core(core, engine[:1], engine[1:], 0)
     engine = jnp.concatenate([engine[:, i : i + 1] for i in (5, 3, 0, 1, 2, 4, 6, 7)] * 2, axis=1)
     engine = lax.dynamic_slice_in_dim(engine, (CHIPS + 3 - z) % CHIPS, CHIPS, axis=1)

time: 203 us -> 199 us (0.980)
  waiting for transfers between devices: 80.9 us -> 75.8 us
  Pallas kernels: 26.5 us -> 29.4 us
    ppermute x2, waiting for transfers between devices: 4.41 us -> 0.01 us  [far_sums(): low = lax.ppermute(far[:half].astype(jnp.bfloat16), axis, PLUS)]
    ppermute x2, waiting for transfers between devices: 0.01 us -> 3.5 us  [near_sums(): from_after = lax.ppermute(before, axis, MINUS)]
    ppermute x2, waiting for transfers between devices: 6.01 us -> 2.75 us  [near_sums(): from_before = lax.ppermute(after, axis, PLUS)]
    ppermute x2, starting transfers between devices: 6.42 us -> 3.3 us  [near_sums(): from_after = lax.ppermute(before, axis, MINUS)]
    ppermute x2, starting transfers between devices: 0.34 us -> 3.42 us  [near_sums(): from_before = lax.ppermute(after, axis, PLUS)]
    pallas_call x4, Pallas kernels: 4.27 us -> 7.08 us  [unpack(): pl.pallas_call(functools.partial(unpack_kernel, rows), grid_spec=pltpu.Pr...]
    ppermute x2, starting transfers between devices: 5.05 us -> 2.27 us  [far_sums(): high = lax.ppermute(far[half:].astype(jnp.bfloat16), axis, MINUS)]
    ppermute x2, starting transfers between devices: 1.58 us -> 4.36 us  [far_sums(): low = lax.ppermute(far[:half].astype(jnp.bfloat16), axis, PLUS)]
  transfers between devices with their start and end apart: 32 -> 32, of which waited for: 14 -> 14; matrix products, arithmetic and copies ran while one was open for 5% -> 6% of each run, Pallas kernels for 7% -> 9%
where the time goes in v2:
time: 199 us; the launch traced here: 198 us
  waiting for transfers between devices  75.8 us (38%)
  starting transfers between devices  35 us (18%)
  Pallas kernels  29.4 us (15%)
  blocking collectives  18.7 us (9%)
  between operations  14.5 us (7%)
  other arithmetic  11.1 us (6%)
  local copies, waits for them, and re-layouts  9.79 us (5%)
  matrix products  3.73 us (2%)
    ppermute x8, waiting for transfers between devices, hop(): return (lax.ppermute(up, Z, UP), lax.ppermute(down, Z, DOWN))  40.6 us
    ppermute x9, waiting for transfers between devices, swap(): return lax.ppermute(value, axis, SWAP)  25.3 us
    all_to_all x1, blocking collectives, local(): lax.all_to_all(piece, ('y', 'x'), split_axis=0, concat_axis=0, tiled=True)  18.7 us
    pallas_call x1, Pallas kernels, pack(): pl.pallas_call(functools.partial(pack_kernel, top), grid=(tiles,), in_spe...  13.5 us
    ppermute x8, starting transfers between devices, hop(): return (lax.ppermute(up, Z, UP), lax.ppermute(down, Z, DOWN))  12.8 us
    pallas_call x1, Pallas kernels, answers_of(): pl.pallas_call(functools.partial(answers_kernel, 0.5 / math.sqrt(model)),...  8.86 us
    pallas_call x4, Pallas kernels, unpack(): pl.pallas_call(functools.partial(unpack_kernel, rows), grid_spec=pltpu.Pr...  7.08 us
    ppermute x2, starting transfers between devices, far_sums(): low = lax.ppermute(far[:half].astype(jnp.bfloat16), axis, PLUS)  4.36 us
  transfers between devices with their start and end apart: 32, of which 14 were waited for; matrix products, arithmetic and copies ran while one was open for 6% of the time, Pallas kernels for 9%

profile of v2, /device:TPU:102, one launch (start us, length us, event | category | flops | bytes accessed | tf_op | source)
XLA Modules:
  0.0 198.0 jit_solution(14015981018171467608)
XLA Ops:
  7.3 2.7 %copy_bitcast_fusion = bf16[64,2,8,768]{3,2,0,1:T(8,128)(2,1)} fusion(bf16[64,2,2,8,768]{4,3,2,1,0:T(8,128)(2,1)} %bitcast.163, s32[]{:T(128)S(6)} %select_n.268), kind=kLoop, calls=%fused_computation.16 | loop fusion | bytes 3145732 | tf_op jit(solution)/shard_map/jit(dynamic_index_in_dim)/squeeze | solution.py:249
  10.0 3.6 %collective-permute-done = bf16[64,2,8,768]{3,2,0,1:T(8,128)(2,1)S(1)} collective-permute-done((bf16[64,2,8,768]{3,2,0,1:T(8,128)(2,1)}, bf16[64,2,8,768]{3,2,0,1:T(8,128)(2,1)S(1)}, u32[]{:S(2)}, u32[]{:S(2)}) %collective-permute-start) | collective-permute-done | bytes 1572896 | tf_op jit(solution)/shard_map/ppermute | solution.py:29
  13.6 2.2 %fusion.5 = bf16[64,8,768]{2,1,0:T(8,128)(2,1)} fusion(bf16[64,2,8,768]{3,2,0,1:T(8,128)(2,1)S(1)} %collective-permute-done, s32[]{:T(128)S(6)} %select_n.264, bf16[64,2,2,8,768]{4,3,2,1,0:T(8,128)(2,1)} %bitcast.164, s32[]{:T(128)S(6)} %select_n.265, s32[]{:T(128)S(6)} %select_n.267), kind=kLoop, calls=%fused_computation.11 | loop fusion | flops 1572864 | bytes 2359308 | tf_op jit(solution)/shard_map/convert_element_type | solution.py:256
  15.9 0.2 fusion.35
  16.5 0.1 concatenate.51
  16.6 0.1 concatenate.52
  16.7 0.1 copy.61
  16.9 3.5 %fusion.2 = bf16[128,2048]{1,0:T(8,128)(2,1)S(1)} fusion(bf16[128,2048]{1,0:T(8,128)(2,1)S(1)} %bitcast.154, s32[2048]{0:T(1024)S(1)} %fusion.62), kind=kOutput, calls=%fused_computation.5 | convolution fusion | flops 1078198272 | bytes 1056768 | tf_op jit(solution)/shard_map/dot_general | solution.py:287
  20.4 0.9 fusion.13
  21.3 0.2 collective-permute-start.1
  21.5 19.7 %collective-permute-done.1 = bf16[64,8,768]{2,1,0:T(8,128)(2,1)S(1)} collective-permute-done((bf16[64,8,768]{2,1,0:T(8,128)(2,1)}, bf16[64,8,768]{2,1,0:T(8,128)(2,1)S(1)}, u32[]{:S(2)}, u32[]{:S(2)}) %collective-permute-start.1) | collective-permute-done | bytes 786464 | tf_op jit(solution)/shard_map/ppermute | solution.py:29
  41.1 4.0 %fusion.8 = (f32[64,1,1,8,768]{4,3,2,1,0:T(8,128)}, bf16[64,8,768]{2,1,0:T(8,128)(2,1)S(1)}) fusion(bf16[64,8,768]{2,1,0:T(8,128)(2,1)S(1)} %collective-permute-done.1, f32[64,1,1,8,768]{4,3,2,1,0:T(8,128)} %param.10, bf16[64,2,8,768]{3,2,0,1:T(8,128)(2,1)S(1)} %collective-permute-done, s32[]{:T(128)S(6)} %select_n.288, ...), kind=kLoop, calls=%fused_computation.21 | loop fusion | flops 5111808 | bytes 7864332
  45.1 18.7 %all_to_all.5 = bf16[16,8,3072]{2,1,0:T(8,128)(2,1)S(1)} all-to-all(bf16[16,8,3072]{2,1,0:T(8,128)(2,1)S(1)} %bitcast.161), channel_id=1, replica_groups=mesh['z_lo'=2,'core'=2,'y'=4,'x'=4,'z_hi'=4] {'y','x'}, dimensions={0} | all-to-all | bytes 1572864 | tf_op jit(solution)/shard_map/all_to_all | solution.py:301
  63.9 3.1 %collective-permute-start.2 = (bf16[128,3072]{1,0:T(8,128)(2,1)S(1)}, bf16[128,3072]{1,0:T(8,128)(2,1)S(1)}, u32[]{:S(2)}, u32[]{:S(2)}) collective-permute-start(bf16[128,3072]{1,0:T(8,128)(2,1)S(1)} %bitcast.155), channel_id=1, source_target_pairs={{0,128},{128,1},{1,129},{129,2},{2,130},{130,3},{3,131},{131,0},{4... | collective-permute-start | bytes 2359304 | tf_op jit(solution)/shard_map/ppermute | solution.py:305
  67.0 15.1 %collective-permute-done.2.refs_0_ = bf16[128,3072]{1,0:T(8,128)(2,1)S(1)} collective-permute-done((bf16[128,3072]{1,0:T(8,128)(2,1)S(1)}, bf16[128,3072]{1,0:T(8,128)(2,1)S(1)}, u32[]{:S(2)}, u32[]{:S(2)}) %collective-permute-start.2) | collective-permute-done | bytes 786464 | tf_op jit(solution)/shard_map/ppermute | solution.py:305
  82.2 3.7 %collective-permute-start.4 = (bf16[128,3072]{1,0:T(8,128)(2,1)S(1)}, bf16[128,3072]{1,0:T(8,128)(2,1)}, u32[]{:S(2)}, u32[]{:S(2)}) collective-permute-start(bf16[128,3072]{1,0:T(8,128)(2,1)S(1)} %collective-permute-done.2.refs_0_), channel_id=1, source_target_pairs={{0,128},{128,1},{1,129},{129,2},{2,130},{130,3},{3,131},{131,0},{4... | collective-permute-start | bytes 2359304 | tf_op jit(solution)/shard_map/ppermute | solution.py:305
  85.9 1.7 pad_maximum_fusion
  87.5 12.7 %collective-permute-done.4.refs_3_ = bf16[128,3072]{1,0:T(8,128)(2,1)} collective-permute-done((bf16[128,3072]{1,0:T(8,128)(2,1)S(1)}, bf16[128,3072]{1,0:T(8,128)(2,1)}, u32[]{:S(2)}, u32[]{:S(2)}) %collective-permute-start.4) | collective-permute-done | bytes 786464 | tf_op jit(solution)/shard_map/ppermute | solution.py:305
  100.2 3.8 %collective-permute-start.6 = (bf16[128,3072]{1,0:T(8,128)(2,1)}, bf16[128,3072]{1,0:T(8,128)(2,1)S(1)}, u32[]{:S(2)}, u32[]{:S(2)}) collective-permute-start(bf16[128,3072]{1,0:T(8,128)(2,1)} %collective-permute-done.4.refs_3_), channel_id=1, source_target_pairs={{0,128},{128,1},{1,129},{129,2},{2,130},{130,3},{3,131},{131,0},{4... | collective-permute-start | bytes 2359304 | tf_op jit(solution)/shard_map/ppermute | solution.py:305
  104.0 0.5 collective-permute-start.12
  104.5 13.5 %shard_map.103 = (bf16[4,384,2048]{2,1,0:T(8,128)(2,1)}, bf16[2048,384]{1,0:T(8,128)(2,1)S(1)}) custom-call(s32[1]{0:T(128)} %bitcast.1.where_ref, bf16[2048,2176]{1,0:T(8,128)(2,1)} %all-gather.2.cloned.1.call-done.row_ref), custom_call_target="tpu_custom_call" | custom-call | flops 1610612736 | bytes 15204352 | tf_op jit(solution)/shard_map/pallas_call | solution.py:104
  118.0 3.2 %collective-permute-done.7.refs_1_ = bf16[128,3072]{1,0:T(8,128)(2,1)} collective-permute-done((bf16[128,3072]{1,0:T(8,128)(2,1)}, bf16[128,3072]{1,0:T(8,128)(2,1)}, u32[]{:S(2)}, u32[]{:S(2)}) %collective-permute-start.7) | collective-permute-done | bytes 786464 | tf_op jit(solution)/shard_map/ppermute | solution.py:305
  121.2 0.3 collective-permute-start.8
  121.4 1.0 slice.135
  122.4 1.9 collective-permute-start.9
  124.4 0.5 collective-permute-start.14
  124.9 5.0 %collective-permute-done.8.refs_7_ = bf16[64,3072]{1,0:T(8,128)(2,1)S(1)} collective-permute-done((bf16[64,3072]{1,0:T(8,128)(2,1)S(1)}, bf16[64,3072]{1,0:T(8,128)(2,1)S(1)}, u32[]{:S(2)}, u32[]{:S(2)}) %collective-permute-start.8) | collective-permute-done | bytes 393248 | tf_op jit(solution)/shard_map/ppermute | solution.py:305
  129.9 4.6 %collective-permute-done.9.refs_8_ = bf16[64,3072]{1,0:T(8,128)(2,1)} collective-permute-done((bf16[64,3072]{1,0:T(8,128)(2,1)S(1)}, bf16[64,3072]{1,0:T(8,128)(2,1)}, u32[]{:S(2)}, u32[]{:S(2)}) %collective-permute-start.9) | collective-permute-done | bytes 393248 | tf_op jit(solution)/shard_map/ppermute | solution.py:305
  134.5 2.0 %collective-permute-done.16.refs_15_ = bf16[64,3072]{1,0:T(8,128)(2,1)} collective-permute-done((bf16[64,3072]{1,0:T(8,128)(2,1)}, bf16[64,3072]{1,0:T(8,128)(2,1)}, u32[]{:S(2)}, u32[]{:S(2)}) %collective-permute-start.16) | collective-permute-done | bytes 393248 | tf_op jit(solution)/shard_map/ppermute | solution.py:29
  136.6 1.1 copy-done.3
  137.7 1.1 copy-done.5
  138.8 8.9 %shard_map.105 = (bf16[4,384,768]{2,1,0:T(8,128)(2,1)S(1)}, bf16[2048,768]{1,0:T(8,128)(2,1)S(1)}) custom-call(s32[1]{0:T(128)} %bitcast.which_ref, bf16[4,384,2048]{2,1,0:T(8,128)(2,1)} %get-tuple-element.15.packed_ref, bf16[128,3072]{1,0:T(8,128)(2,1)S(1)} %copy-done.3, bf16[128,3072]{1,0:T(8,128)(2,1)S(1)} %bitcast.158, bf16[128,3072]{1,0:T(8,128)(2,1)S(1)} %copy-done.5, ...), custom_call_target="tpu_custom_call" | custom-call | flops 4831838208 | bytes 21233664 | tf_op jit(solution)/shard_map/pallas_call | solution.py:159
  147.7 0.4 shard_map.106.first_ref
  148.2 1.1 shard_map.107.first_ref
  149.3 1.9 shard_map.108.first_ref
  151.2 1.4 collective-permute-start.18
  152.6 1.9 collective-permute-start.20
  154.5 0.1 convert.61
  154.7 3.7 %shard_map.109 = f32[3,512,384]{2,1,0:T(8,128)S(1)} custom-call(s32[3]{0:T(128)S(1)} %get-tuple-element.57.where_ref, bf16[2048,384]{1,0:T(8,128)(2,1)S(1)} %get-tuple-element.16.refs_2_.spread_ref.first_ref, bf16[4,384,768]{2,1,0:T(8,128)(2,1)S(1)} %get-tuple-element.20.answers_ref, f32[3,512,384]{2,1,0:T(8,128)S(1)} %shard_map.108.first_ref), custom_call_target="tpu_custom_call" | custom-call | flops 452984832 | bytes 3538944 | tf_op jit(solution)/shard_map/pallas_call | solution.py:216
  158.4 0.1 convert.58
  158.6 0.3 collective-permute-start.17
  158.9 3.0 %collective-permute-start.25 = (bf16[256,384]{1,0:T(8,128)(2,1)S(1)}, bf16[256,384]{1,0:T(8,128)(2,1)S(1)}, u32[]{:S(2)}, u32[]{:S(2)}) collective-permute-start(bf16[256,384]{1,0:T(8,128)(2,1)S(1)} %get-tuple-element.50), channel_id=1, source_target_pairs={{0,4},{4,8},{8,12},{12,0},{1,5},{5,9},{9,13},{13,1},{2,6},{6,10},{... | collective-permute-start | bytes 589832 | tf_op jit(solution)/shard_map/ppermute | solution.py:49
  161.9 0.1 fusion.19
  162.1 0.4 collective-permute-start.19
  162.5 3.2 %collective-permute-start.21 = (bf16[512,384]{1,0:T(8,128)(2,1)S(1)}, bf16[512,384]{1,0:T(8,128)(2,1)S(1)}, u32[]{:S(2)}, u32[]{:S(2)}) collective-permute-start(bf16[512,384]{1,0:T(8,128)(2,1)S(1)} %pad_maximum_fusion.3), channel_id=1, source_target_pairs={{0,48},{16,0},{32,16},{48,32},{1,49},{17,1},{33,17},{49,33},{2,50}... | collective-permute-start | bytes 1179656 | tf_op jit(solution)/shard_map/ppermute | solution.py:58
  165.7 0.5 collective-permute-done.17
  166.4 3.0 %collective-permute-start.26 = (bf16[512,384]{1,0:T(8,128)(2,1)S(1)}, bf16[512,384]{1,0:T(8,128)(2,1)S(1)}, u32[]{:S(2)}, u32[]{:S(2)}) collective-permute-start(bf16[512,384]{1,0:T(8,128)(2,1)S(1)} %pad_maximum_fusion.4), channel_id=1, source_target_pairs={{0,4},{4,8},{8,12},{12,0},{1,5},{5,9},{9,13},{13,1},{2,6},{6,10},{... | collective-permute-start | bytes 1179656 | tf_op jit(solution)/shard_map/ppermute | solution.py:57
  169.5 0.2 fusion.87
  169.7 0.5 maximum_select_fusion
  170.8 0.2 dynamic-slice_bitcast_fusion
  171.0 2.0 %copy.63 = bf16[16,8,2,8,768]{4,3,2,1,0:T(8,128)(2,1)} copy(bf16[16,8,2,8,768]{4,3,0,1,2:T(8,128)(2,1)S(1)} %dynamic-slice_bitcast_fusion) | data formatting | bytes 6291456 | tf_op jit(solution)/shard_map/transpose | solution.py:356
  173.0 0.6 collective-permute-done.19
  173.6 0.1 fusion.12
  173.8 1.3 collective-permute-start.22
  175.2 1.4 collective-permute-start.23
  176.6 0.8 collective-permute-start.24
  177.4 2.1 %collective-permute-done.26 = bf16[512,384]{1,0:T(8,128)(2,1)S(1)} collective-permute-done((bf16[512,384]{1,0:T(8,128)(2,1)S(1)}, bf16[512,384]{1,0:T(8,128)(2,1)S(1)}, u32[]{:S(2)}, u32[]{:S(2)}) %collective-permute-start.26) | collective-permute-done | bytes 393248 | tf_op jit(solution)/shard_map/ppermute | solution.py:57
  179.5 3.5 %collective-permute-done.27 = bf16[512,384]{1,0:T(8,128)(2,1)S(1)} collective-permute-done((bf16[512,384]{1,0:T(8,128)(2,1)S(1)}, bf16[512,384]{1,0:T(8,128)(2,1)S(1)}, u32[]{:S(2)}, u32[]{:S(2)}) %collective-permute-start.27) | collective-permute-done | bytes 393248 | tf_op jit(solution)/shard_map/ppermute | solution.py:58
  183.0 0.1 fusion.10
  183.2 0.8 collective-permute-start.28
  184.0 3.2 %collective-permute-start.30 = (bf16[128,384]{1,0:T(8,128)(2,1)S(1)}, bf16[128,384]{1,0:T(8,128)(2,1)S(1)}, u32[]{:S(2)}, u32[]{:S(2)}) collective-permute-start(bf16[128,384]{1,0:T(8,128)(2,1)S(1)} %get-tuple-element.46), channel_id=1, source_target_pairs={{0,48},{16,0},{32,16},{48,32},{1,49},{17,1},{33,17},{49,33},{2,50}... | collective-permute-start | bytes 294920 | tf_op jit(solution)/shard_map/ppermute | solution.py:329
  187.3 2.2 %collective-permute-done.28 = bf16[128,384]{1,0:T(8,128)(2,1)S(1)} collective-permute-done((bf16[128,384]{1,0:T(8,128)(2,1)S(1)}, bf16[128,384]{1,0:T(8,128)(2,1)S(1)}, u32[]{:S(2)}, u32[]{:S(2)}) %collective-permute-start.28) | collective-permute-done | bytes 98336 | tf_op jit(solution)/shard_map/ppermute | solution.py:327
  189.4 1.0 collective-permute-done.29
  190.5 0.7 pad_maximum_fusion.5
  (90 shorter events, 1.9 us)
Async XLA Ops:
  7.2 9.7 %copy-start = (bf16[4,32,2048]{2,1,0:T(8,128)(2,1)S(1)}, bf16[4,32,2048]{2,1,0:T(8,128)(2,1)}, u32[]{:S(2)}) copy-start(bf16[4,32,2048]{2,1,0:T(8,128)(2,1)} %param.11) | copy-start | bytes 1572868
  7.2 8.6 %copy-start.6 = (s32[4,32,8]{1,2,0:T(8,128)S(1)}, s32[4,32,8]{1,2,0:T(8,128)}, u32[]{:S(2)}) copy-start(s32[4,32,8]{1,2,0:T(8,128)} %param.12) | copy-start | bytes 12292
  7.2 9.3 %copy-start.7 = (f32[4,32,8]{1,2,0:T(8,128)S(1)}, f32[4,32,8]{1,2,0:T(8,128)}, u32[]{:S(2)}) copy-start(f32[4,32,8]{1,2,0:T(8,128)} %param.13) | copy-start | bytes 12292
  7.2 97.3 %all-gather.2.cloned.1.call-start = ((), (), s32[]{:S(2)}) async-start(), calls=%async_computation.1 | async-start | bytes 9469952 | tf_op jit(solution)/shard_map/all_gather | solution.py:293
  10.0 3.6 %collective-permute-start = (bf16[64,2,8,768]{3,2,0,1:T(8,128)(2,1)}, bf16[64,2,8,768]{3,2,0,1:T(8,128)(2,1)S(1)}, u32[]{:S(2)}, u32[]{:S(2)}) collective-permute-start(bf16[64,2,8,768]{3,2,0,1:T(8,128)(2,1)} %copy_bitcast_fusion), channel_id=1, source_target_pairs={{0,64},{64,0},{1,65},{65,1},{2,66},{66,2},{3,67},{67,3},{4,68},{68... | collective-permute-start | bytes 4718600 | tf_op jit(solution)/shard_map/ppermute | solution.py:29
  21.3 19.9 %collective-permute-start.1 = (bf16[64,8,768]{2,1,0:T(8,128)(2,1)}, bf16[64,8,768]{2,1,0:T(8,128)(2,1)S(1)}, u32[]{:S(2)}, u32[]{:S(2)}) collective-permute-start(bf16[64,8,768]{2,1,0:T(8,128)(2,1)} %fusion.5), channel_id=1, source_target_pairs={{0,128},{128,0},{1,129},{129,1},{2,130},{130,2},{3,131},{131,3},{4... | collective-permute-start | bytes 2359304 | tf_op jit(solution)/shard_map/ppermute | solution.py:29
  63.9 18.3 %collective-permute-start.2 = (bf16[128,3072]{1,0:T(8,128)(2,1)S(1)}, bf16[128,3072]{1,0:T(8,128)(2,1)S(1)}, u32[]{:S(2)}, u32[]{:S(2)}) collective-permute-start(bf16[128,3072]{1,0:T(8,128)(2,1)S(1)} %bitcast.155), channel_id=1, source_target_pairs={{0,128},{128,1},{1,129},{129,2},{2,130},{130,3},{3,131},{131,0},{4... | collective-permute-start | bytes 2359304 | tf_op jit(solution)/shard_map/ppermute | solution.py:305
  67.0 18.8 %collective-permute-start.3 = (bf16[128,3072]{1,0:T(8,128)(2,1)S(1)}, bf16[128,3072]{1,0:T(8,128)(2,1)S(1)}, u32[]{:S(2)}, u32[]{:S(2)}) collective-permute-start(bf16[128,3072]{1,0:T(8,128)(2,1)S(1)} %bitcast.156), channel_id=1, source_target_pairs={{128,0},{1,128},{129,1},{2,129},{130,2},{3,130},{131,3},{0,131},{1... | collective-permute-start | bytes 2359304 | tf_op jit(solution)/shard_map/ppermute | solution.py:305
  82.2 5.4 %copy-start.2 = (bf16[128,3072]{1,0:T(8,128)(2,1)}, bf16[128,3072]{1,0:T(8,128)(2,1)S(1)}, u32[]{:S(2)}) copy-start(bf16[128,3072]{1,0:T(8,128)(2,1)S(1)} %collective-permute-done.2.refs_0_) | copy-start | bytes 2359300
  82.2 18.0 %collective-permute-start.4 = (bf16[128,3072]{1,0:T(8,128)(2,1)S(1)}, bf16[128,3072]{1,0:T(8,128)(2,1)}, u32[]{:S(2)}, u32[]{:S(2)}) collective-permute-start(bf16[128,3072]{1,0:T(8,128)(2,1)S(1)} %collective-permute-done.2.refs_0_), channel_id=1, source_target_pairs={{0,128},{128,1},{1,129},{129,2},{2,130},{130,3},{3,131},{131,0},{4... | collective-permute-start | bytes 2359304 | tf_op jit(solution)/shard_map/ppermute | solution.py:305
  85.9 14.3 %copy-start.4 = (bf16[128,3072]{1,0:T(8,128)(2,1)}, bf16[128,3072]{1,0:T(8,128)(2,1)S(1)}, u32[]{:S(2)}) copy-start(bf16[128,3072]{1,0:T(8,128)(2,1)S(1)} %collective-permute-done.3.refs_2_) | copy-start | bytes 2359300
  85.9 18.1 %collective-permute-start.5 = (bf16[128,3072]{1,0:T(8,128)(2,1)S(1)}, bf16[128,3072]{1,0:T(8,128)(2,1)}, u32[]{:S(2)}, u32[]{:S(2)}) collective-permute-start(bf16[128,3072]{1,0:T(8,128)(2,1)S(1)} %collective-permute-done.3.refs_2_), channel_id=1, source_target_pairs={{128,0},{1,128},{129,1},{2,129},{130,2},{3,130},{131,3},{0,131},{1... | collective-permute-start | bytes 2359304 | tf_op jit(solution)/shard_map/ppermute | solution.py:305
  87.5 47.0 %collective-permute-start.10 = (bf16[384,3072]{1,0:T(8,128)(2,1)}, bf16[384,3072]{1,0:T(8,128)(2,1)}, u32[]{:S(2)}, u32[]{:S(2)}) collective-permute-start(bf16[384,3072]{1,0:T(8,128)(2,1)} %pad_maximum_fusion), channel_id=1, source_target_pairs={{0,64},{64,0},{1,65},{65,1},{2,66},{66,2},{3,67},{67,3},{4,68},{68... | collective-permute-start | bytes 7077896 | tf_op jit(solution)/shard_map/ppermute | solution.py:29
  100.2 17.8 %collective-permute-start.6 = (bf16[128,3072]{1,0:T(8,128)(2,1)}, bf16[128,3072]{1,0:T(8,128)(2,1)S(1)}, u32[]{:S(2)}, u32[]{:S(2)}) collective-permute-start(bf16[128,3072]{1,0:T(8,128)(2,1)} %collective-permute-done.4.refs_3_), channel_id=1, source_target_pairs={{0,128},{128,1},{1,129},{129,2},{2,130},{130,3},{3,131},{131,0},{4... | collective-permute-start | bytes 2359304 | tf_op jit(solution)/shard_map/ppermute | solution.py:305
  104.0 17.1 %collective-permute-start.7 = (bf16[128,3072]{1,0:T(8,128)(2,1)}, bf16[128,3072]{1,0:T(8,128)(2,1)}, u32[]{:S(2)}, u32[]{:S(2)}) collective-permute-start(bf16[128,3072]{1,0:T(8,128)(2,1)} %collective-permute-done.5.refs_4_), channel_id=1, source_target_pairs={{128,0},{1,128},{129,1},{2,129},{130,2},{3,130},{131,3},{0,131},{1... | collective-permute-start | bytes 2359304 | tf_op jit(solution)/shard_map/ppermute | solution.py:305
  104.0 20.4 %collective-permute-start.11 = (bf16[128,3072]{1,0:T(8,128)(2,1)}, bf16[128,3072]{1,0:T(8,128)(2,1)}, u32[]{:S(2)}, u32[]{:S(2)}) collective-permute-start(bf16[128,3072]{1,0:T(8,128)(2,1)} %collective-permute-done.4.refs_3_), channel_id=1, source_target_pairs={{0,64},{64,0},{1,65},{65,1},{2,66},{66,2},{3,67},{67,3},{4,68},{68... | collective-permute-start | bytes 2359304 | tf_op jit(solution)/shard_map/ppermute | solution.py:29
  104.0 20.4 %collective-permute-start.12 = (bf16[128,3072]{1,0:T(8,128)(2,1)}, bf16[128,3072]{1,0:T(8,128)(2,1)}, u32[]{:S(2)}, u32[]{:S(2)}) collective-permute-start(bf16[128,3072]{1,0:T(8,128)(2,1)} %collective-permute-done.5.refs_4_), channel_id=1, source_target_pairs={{0,64},{64,0},{1,65},{65,1},{2,66},{66,2},{3,67},{67,3},{4,68},{68... | collective-permute-start | bytes 2359304 | tf_op jit(solution)/shard_map/ppermute | solution.py:29
  118.0 16.5 %copy-start.8 = (s32[3]{0:T(128)S(1)}, s32[3]{0:T(128)}, u32[]{:S(2)}) copy-start(s32[3]{0:T(128)} %constant.362.clone) | copy-start | bytes 40
  121.2 8.7 %collective-permute-start.8 = (bf16[64,3072]{1,0:T(8,128)(2,1)S(1)}, bf16[64,3072]{1,0:T(8,128)(2,1)S(1)}, u32[]{:S(2)}, u32[]{:S(2)}) collective-permute-start(bf16[64,3072]{1,0:T(8,128)(2,1)S(1)} %slice.134), channel_id=1, source_target_pairs={{0,128},{128,1},{1,129},{129,2},{2,130},{130,3},{3,131},{131,0},{4... | collective-permute-start | bytes 1179656 | tf_op jit(solution)/shard_map/ppermute | solution.py:305
  122.4 12.1 %collective-permute-start.9 = (bf16[64,3072]{1,0:T(8,128)(2,1)S(1)}, bf16[64,3072]{1,0:T(8,128)(2,1)}, u32[]{:S(2)}, u32[]{:S(2)}) collective-permute-start(bf16[64,3072]{1,0:T(8,128)(2,1)S(1)} %slice.135), channel_id=1, source_target_pairs={{128,0},{1,128},{129,1},{2,129},{130,2},{3,130},{131,3},{0,131},{1... | collective-permute-start | bytes 1179656 | tf_op jit(solution)/shard_map/ppermute | solution.py:305
  124.4 12.2 %collective-permute-start.13 = (bf16[128,3072]{1,0:T(8,128)(2,1)S(1)}, bf16[128,3072]{1,0:T(8,128)(2,1)}, u32[]{:S(2)}, u32[]{:S(2)}) collective-permute-start(bf16[128,3072]{1,0:T(8,128)(2,1)S(1)} %get-tuple-element.17.refs_5_), channel_id=1, source_target_pairs={{0,64},{64,0},{1,65},{65,1},{2,66},{66,2},{3,67},{67,3},{4,68},{68... | collective-permute-start | bytes 2359304 | tf_op jit(solution)/shard_map/ppermute | solution.py:29
  124.4 12.2 %collective-permute-start.14 = (bf16[128,3072]{1,0:T(8,128)(2,1)}, bf16[128,3072]{1,0:T(8,128)(2,1)}, u32[]{:S(2)}, u32[]{:S(2)}) collective-permute-start(bf16[128,3072]{1,0:T(8,128)(2,1)} %get-tuple-element.18.refs_6_), channel_id=1, source_target_pairs={{0,64},{64,0},{1,65},{65,1},{2,66},{66,2},{3,67},{67,3},{4,68},{68... | collective-permute-start | bytes 2359304 | tf_op jit(solution)/shard_map/ppermute | solution.py:29
  129.9 4.6 %collective-permute-start.15 = (bf16[64,3072]{1,0:T(8,128)(2,1)S(1)}, bf16[64,3072]{1,0:T(8,128)(2,1)}, u32[]{:S(2)}, u32[]{:S(2)}) collective-permute-start(bf16[64,3072]{1,0:T(8,128)(2,1)S(1)} %collective-permute-done.8.refs_7_), channel_id=1, source_target_pairs={{0,64},{64,0},{1,65},{65,1},{2,66},{66,2},{3,67},{67,3},{4,68},{68... | collective-permute-start | bytes 1179656 | tf_op jit(solution)/shard_map/ppermute | solution.py:29
  134.5 2.1 %collective-permute-start.16 = (bf16[64,3072]{1,0:T(8,128)(2,1)}, bf16[64,3072]{1,0:T(8,128)(2,1)}, u32[]{:S(2)}, u32[]{:S(2)}) collective-permute-start(bf16[64,3072]{1,0:T(8,128)(2,1)} %collective-permute-done.9.refs_8_), channel_id=1, source_target_pairs={{0,64},{64,0},{1,65},{65,1},{2,66},{66,2},{3,67},{67,3},{4,68},{68... | collective-permute-start | bytes 1179656 | tf_op jit(solution)/shard_map/ppermute | solution.py:29
  136.6 1.1 copy-start.3
  137.7 1.1 copy-start.5
  151.2 10.7 %collective-permute-start.18 = (bf16[256,384]{1,0:T(8,128)(2,1)S(1)}, bf16[256,384]{1,0:T(8,128)(2,1)S(1)}, u32[]{:S(2)}, u32[]{:S(2)}) collective-permute-start(bf16[256,384]{1,0:T(8,128)(2,1)S(1)} %get-tuple-element.48), channel_id=1, source_target_pairs={{0,16},{16,32},{32,48},{48,0},{1,17},{17,33},{33,49},{49,1},{2,18}... | collective-permute-start | bytes 589832 | tf_op jit(solution)/shard_map/ppermute | solution.py:49
  152.6 9.4 %collective-permute-start.20 = (bf16[256,384]{1,0:T(8,128)(2,1)S(1)}, bf16[256,384]{1,0:T(8,128)(2,1)S(1)}, u32[]{:S(2)}, u32[]{:S(2)}) collective-permute-start(bf16[256,384]{1,0:T(8,128)(2,1)S(1)} %get-tuple-element.49), channel_id=1, source_target_pairs={{0,48},{16,0},{32,16},{48,32},{1,49},{17,1},{33,17},{49,33},{2,50}... | collective-permute-start | bytes 589832 | tf_op jit(solution)/shard_map/ppermute | solution.py:50
  158.6 7.7 %collective-permute-start.17 = (bf16[256,384]{1,0:T(8,128)(2,1)S(1)}, bf16[256,384]{1,0:T(8,128)(2,1)S(1)}, u32[]{:S(2)}, u32[]{:S(2)}) collective-permute-start(bf16[256,384]{1,0:T(8,128)(2,1)S(1)} %get-tuple-element.51), channel_id=1, source_target_pairs={{0,12},{4,0},{8,4},{12,8},{1,13},{5,1},{9,5},{13,9},{2,14},{6,2},{... | collective-permute-start | bytes 589832 | tf_op jit(solution)/shard_map/ppermute | solution.py:50
  158.9 7.3 %collective-permute-start.25 = (bf16[256,384]{1,0:T(8,128)(2,1)S(1)}, bf16[256,384]{1,0:T(8,128)(2,1)S(1)}, u32[]{:S(2)}, u32[]{:S(2)}) collective-permute-start(bf16[256,384]{1,0:T(8,128)(2,1)S(1)} %get-tuple-element.50), channel_id=1, source_target_pairs={{0,4},{4,8},{8,12},{12,0},{1,5},{5,9},{9,13},{13,1},{2,6},{6,10},{... | collective-permute-start | bytes 589832 | tf_op jit(solution)/shard_map/ppermute | solution.py:49
  162.1 11.5 %collective-permute-start.19 = (bf16[512,384]{1,0:T(8,128)(2,1)S(1)}, bf16[512,384]{1,0:T(8,128)(2,1)S(1)}, u32[]{:S(2)}, u32[]{:S(2)}) collective-permute-start(bf16[512,384]{1,0:T(8,128)(2,1)S(1)} %pad_maximum_fusion.2), channel_id=1, source_target_pairs={{0,16},{16,32},{32,48},{48,0},{1,17},{17,33},{33,49},{49,1},{2,18}... | collective-permute-start | bytes 1179656 | tf_op jit(solution)/shard_map/ppermute | solution.py:57
  162.5 11.1 %collective-permute-start.21 = (bf16[512,384]{1,0:T(8,128)(2,1)S(1)}, bf16[512,384]{1,0:T(8,128)(2,1)S(1)}, u32[]{:S(2)}, u32[]{:S(2)}) collective-permute-start(bf16[512,384]{1,0:T(8,128)(2,1)S(1)} %pad_maximum_fusion.3), channel_id=1, source_target_pairs={{0,48},{16,0},{32,16},{48,32},{1,49},{17,1},{33,17},{49,33},{2,50}... | collective-permute-start | bytes 1179656 | tf_op jit(solution)/shard_map/ppermute | solution.py:58
  166.4 13.1 %collective-permute-start.26 = (bf16[512,384]{1,0:T(8,128)(2,1)S(1)}, bf16[512,384]{1,0:T(8,128)(2,1)S(1)}, u32[]{:S(2)}, u32[]{:S(2)}) collective-permute-start(bf16[512,384]{1,0:T(8,128)(2,1)S(1)} %pad_maximum_fusion.4), channel_id=1, source_target_pairs={{0,4},{4,8},{8,12},{12,0},{1,5},{5,9},{9,13},{13,1},{2,6},{6,10},{... | collective-permute-start | bytes 1179656 | tf_op jit(solution)/shard_map/ppermute | solution.py:57
  169.4 13.6 %collective-permute-start.27 = (bf16[512,384]{1,0:T(8,128)(2,1)S(1)}, bf16[512,384]{1,0:T(8,128)(2,1)S(1)}, u32[]{:S(2)}, u32[]{:S(2)}) collective-permute-start(bf16[512,384]{1,0:T(8,128)(2,1)S(1)} %pad_maximum_fusion.1.refs_1_), channel_id=1, source_target_pairs={{0,12},{4,0},{8,4},{12,8},{1,13},{5,1},{9,5},{13,9},{2,14},{6,2},{... | collective-permute-start | bytes 1179656 | tf_op jit(solution)/shard_map/ppermute | solution.py:58
  173.6 17.5 %copy-start.1 = (bf16[4,32,2048]{2,1,0:T(8,128)(2,1)S(1)}, bf16[4,32,2048]{2,1,0:T(8,128)(2,1)}, u32[]{:S(2)}) copy-start(bf16[4,32,2048]{2,1,0:T(8,128)(2,1)} %param.11) | copy-start | bytes 1572868
  173.8 10.1 %collective-permute-start.22 = (bf16[128,384]{1,0:T(8,128)(2,1)S(1)}, bf16[128,384]{1,0:T(8,128)(2,1)S(1)}, u32[]{:S(2)}, u32[]{:S(2)}) collective-permute-start(bf16[128,384]{1,0:T(8,128)(2,1)S(1)} %get-tuple-element.42), channel_id=1, source_target_pairs={{0,8},{4,12},{8,0},{12,4},{1,9},{5,13},{9,1},{13,5},{2,10},{6,14},... | collective-permute-start | bytes 294920 | tf_op jit(solution)/shard_map/ppermute | solution.py:327
  175.2 12.0 %collective-permute-start.23 = (bf16[128,384]{1,0:T(8,128)(2,1)S(1)}, bf16[128,384]{1,0:T(8,128)(2,1)S(1)}, u32[]{:S(2)}, u32[]{:S(2)}) collective-permute-start(bf16[128,384]{1,0:T(8,128)(2,1)S(1)} %get-tuple-element.44), channel_id=1, source_target_pairs={{0,4},{4,8},{8,12},{12,0},{1,5},{5,9},{9,13},{13,1},{2,6},{6,10},{... | collective-permute-start | bytes 294920 | tf_op jit(solution)/shard_map/ppermute | solution.py:328
  176.6 10.6 %collective-permute-start.24 = (bf16[128,384]{1,0:T(8,128)(2,1)S(1)}, bf16[128,384]{1,0:T(8,128)(2,1)S(1)}, u32[]{:S(2)}, u32[]{:S(2)}) collective-permute-start(bf16[128,384]{1,0:T(8,128)(2,1)S(1)} %get-tuple-element.43), channel_id=1, source_target_pairs={{0,12},{4,0},{8,4},{12,8},{1,13},{5,1},{9,5},{13,9},{2,14},{6,2},{... | collective-permute-start | bytes 294920 | tf_op jit(solution)/shard_map/ppermute | solution.py:329
  183.2 6.3 %collective-permute-start.28 = (bf16[128,384]{1,0:T(8,128)(2,1)S(1)}, bf16[128,384]{1,0:T(8,128)(2,1)S(1)}, u32[]{:S(2)}, u32[]{:S(2)}) collective-permute-start(bf16[128,384]{1,0:T(8,128)(2,1)S(1)} %get-tuple-element.45), channel_id=1, source_target_pairs={{0,32},{16,48},{32,0},{48,16},{1,33},{17,49},{33,1},{49,17},{2,34}... | collective-permute-start | bytes 294920 | tf_op jit(solution)/shard_map/ppermute | solution.py:327
  183.9 6.5 %collective-permute-start.29 = (bf16[128,384]{1,0:T(8,128)(2,1)S(1)}, bf16[128,384]{1,0:T(8,128)(2,1)S(1)}, u32[]{:S(2)}, u32[]{:S(2)}) collective-permute-start(bf16[128,384]{1,0:T(8,128)(2,1)S(1)} %get-tuple-element.47), channel_id=1, source_target_pairs={{0,16},{16,32},{32,48},{48,0},{1,17},{17,33},{33,49},{49,1},{2,18}... | collective-permute-start | bytes 294920 | tf_op jit(solution)/shard_map/ppermute | solution.py:328
  184.0 6.5 %collective-permute-start.30 = (bf16[128,384]{1,0:T(8,128)(2,1)S(1)}, bf16[128,384]{1,0:T(8,128)(2,1)S(1)}, u32[]{:S(2)}, u32[]{:S(2)}) collective-permute-start(bf16[128,384]{1,0:T(8,128)(2,1)S(1)} %get-tuple-element.46), channel_id=1, source_target_pairs={{0,48},{16,0},{32,16},{48,32},{1,49},{17,1},{33,17},{49,33},{2,50}... | collective-permute-start | bytes 294920 | tf_op jit(solution)/shard_map/ppermute | solution.py:329
Sparse Core Ops, SparseCore 0:
  21.4 79.9 all-gather.1

commit v3 on v2

--- a/solution.py
+++ b/solution.py
@@ -184,7 +184,7 @@
 
 def unpack_kernel(rows, where_ref, spread_ref, answers_ref, first_ref, out_ref):
     slots = GROUPS * CAP
-    tile = min(GROUPS * rows, spread_ref.shape[0])
+    tile = GROUPS * rows
     for start in range(0, spread_ref.shape[0], tile):
         part = start // tile * slots
         held = [answers_ref[i, part : part + slots] for i in range(RING)]
@@ -196,30 +196,40 @@
         out_ref[0, start : start + tile] = out.astype(out_ref.dtype)
 
 
+def unpack_across_kernel(rows, where_ref, spread_ref, answers_ref, first_ref, out_ref):
+    tile = spread_ref.shape[2]
+    for block in range(RING):
+        held = [answers_ref[i, block, 0] for i in range(RING)]
+        out = jnp.dot(
+            spread_ref[block, 0], jnp.concatenate(held + held), preferred_element_type=jnp.float32
+        )
+        out_ref[0, block * tile : (block + 1) * tile] = out.astype(out_ref.dtype)
+
+
 def unpack(where, spread, answers, part, axis, rows, dtype, first):
     blocks = where.shape[0]
     count, wide = spread.shape[0] // RING, spread.shape[1]
     slots, columns = answers.shape[1] // RING, part[1] - part[0]
     column = part[0] // columns
     if axis == "y":
-        grid = (blocks, 1)
-        spread_spec = pl.BlockSpec((count, wide), lambda i, j, where: (where[i], 0))
-        answers_spec = pl.BlockSpec((RING, slots, columns), lambda i, j, where: (0, where[i], column))
-        out_spec = pl.BlockSpec((1, count, columns), lambda i, j, where: (i, 0, 0))
+        kernel = unpack_kernel
+        spread_spec = pl.BlockSpec((count, wide), lambda i, where: (where[i], 0))
+        answers_spec = pl.BlockSpec((RING, slots, columns), lambda i, where: (0, where[i], column))
     else:
-        grid = (blocks, RING)
-        spread_spec = pl.BlockSpec((count // RING, wide), lambda i, j, where: (j * RING + where[i], 0))
+        kernel = unpack_across_kernel
+        spread = spread.reshape(RING, RING, count // RING, wide)
+        answers = answers.reshape(RING, RING, 2, slots // 2, answers.shape[2])
+        spread_spec = pl.BlockSpec((RING, 1, count // RING, wide), lambda i, where: (0, where[i], 0, 0))
         answers_spec = pl.BlockSpec(
-            (RING, slots // 2, columns), lambda i, j, where: (0, j * 2 + where[i] // 2, column)
+            (RING, RING, 1, slots // 2, columns), lambda i, where: (0, 0, where[i] // 2, 0, column)
         )
-        out_spec = pl.BlockSpec((1, count // RING, columns), lambda i, j, where: (i, j, 0))
     return pl.pallas_call(
-        functools.partial(unpack_kernel, rows),
+        functools.partial(kernel, rows),
         grid_spec=pltpu.PrefetchScalarGridSpec(
             num_scalar_prefetch=1,
-            grid=grid,
+            grid=(blocks,),
             in_specs=[spread_spec, answers_spec, pl.BlockSpec(memory_space=pl.ANY)],
-            out_specs=out_spec,
+            out_specs=pl.BlockSpec((1, count, columns), lambda i, where: (i, 0, 0)),
         ),
         out_shape=jax.ShapeDtypeStruct((blocks, count, columns), dtype),
         compiler_params=pltpu.CompilerParams(vmem_limit_bytes=18 * 2**20),

time: 199 us -> 196 us (0.985)
  Pallas kernels: 29.4 us -> 27.3 us
    pallas_call x4, Pallas kernels: 7.08 us -> 4.99 us  [unpack(): pl.pallas_call(functools.partial(kernel, rows), grid_spec=pltpu.PrefetchS...]
  transfers between devices with their start and end apart: 32 -> 32, of which waited for: 14 -> 14; matrix products, arithmetic and copies ran while one was open for 6% -> 6% of each run, Pallas kernels for 9% -> 8%
where the time goes in v3:
time: 196 us
  waiting for transfers between devices  75.7 us (39%)
  starting transfers between devices  35 us (18%)
  Pallas kernels  27.3 us (14%)
  blocking collectives  18.7 us (10%)
  between operations  14.5 us (7%)
  other arithmetic  11.1 us (6%)
  local copies, waits for them, and re-layouts  9.79 us (5%)
  matrix products  3.73 us (2%)
    ppermute x8, waiting for transfers between devices, hop(): return (lax.ppermute(up, Z, UP), lax.ppermute(down, Z, DOWN))  40.6 us
    ppermute x9, waiting for transfers between devices, swap(): return lax.ppermute(value, axis, SWAP)  25.3 us
    all_to_all x1, blocking collectives, local(): lax.all_to_all(piece, ('y', 'x'), split_axis=0, concat_axis=0, tiled=True)  18.7 us
    pallas_call x1, Pallas kernels, pack(): pl.pallas_call(functools.partial(pack_kernel, top), grid=(tiles,), in_spe...  13.5 us
    ppermute x8, starting transfers between devices, hop(): return (lax.ppermute(up, Z, UP), lax.ppermute(down, Z, DOWN))  12.8 us
    pallas_call x1, Pallas kernels, answers_of(): pl.pallas_call(functools.partial(answers_kernel, 0.5 / math.sqrt(model)),...  8.86 us
    pallas_call x4, Pallas kernels, unpack(): pl.pallas_call(functools.partial(kernel, rows), grid_spec=pltpu.PrefetchS...  4.99 us
    ppermute x2, starting transfers between devices, far_sums(): low = lax.ppermute(far[:half].astype(jnp.bfloat16), axis, PLUS)  4.43 us
  transfers between devices with their start and end apart: 32, of which 14 were waited for; matrix products, arithmetic and copies ran while one was open for 6% of the time, Pallas kernels for 8%

profile of v3, /device:TPU:102, one launch (start us, length us, event | category | flops | bytes accessed | tf_op | source)
XLA Modules:
  0.0 195.9 jit_solution(14876150561470647942)
XLA Ops:
  7.3 2.7 %copy_bitcast_fusion = bf16[64,2,8,768]{3,2,0,1:T(8,128)(2,1)} fusion(bf16[64,2,2,8,768]{4,3,2,1,0:T(8,128)(2,1)} %bitcast.169, s32[]{:T(128)S(6)} %select_n.268), kind=kLoop, calls=%fused_computation.16 | loop fusion | bytes 3145732 | tf_op jit(solution)/shard_map/jit(dynamic_index_in_dim)/squeeze | solution.py:259
  10.0 3.6 %collective-permute-done = bf16[64,2,8,768]{3,2,0,1:T(8,128)(2,1)S(1)} collective-permute-done((bf16[64,2,8,768]{3,2,0,1:T(8,128)(2,1)}, bf16[64,2,8,768]{3,2,0,1:T(8,128)(2,1)S(1)}, u32[]{:S(2)}, u32[]{:S(2)}) %collective-permute-start) | collective-permute-done | bytes 1572896 | tf_op jit(solution)/shard_map/ppermute | solution.py:29
  13.6 2.2 %fusion.5 = bf16[64,8,768]{2,1,0:T(8,128)(2,1)} fusion(bf16[64,2,8,768]{3,2,0,1:T(8,128)(2,1)S(1)} %collective-permute-done, s32[]{:T(128)S(6)} %select_n.264, bf16[64,2,2,8,768]{4,3,2,1,0:T(8,128)(2,1)} %bitcast.170, s32[]{:T(128)S(6)} %select_n.265, s32[]{:T(128)S(6)} %select_n.267), kind=kLoop, calls=%fused_computation.11 | loop fusion | flops 1572864 | bytes 2359308 | tf_op jit(solution)/shard_map/convert_element_type | solution.py:266
  15.9 0.2 fusion.35
  16.6 0.1 concatenate.52
  16.7 0.1 copy.61
  16.9 3.5 %fusion.2 = bf16[128,2048]{1,0:T(8,128)(2,1)S(1)} fusion(bf16[128,2048]{1,0:T(8,128)(2,1)S(1)} %bitcast.156, s32[2048]{0:T(1024)S(1)} %fusion.62), kind=kOutput, calls=%fused_computation.5 | convolution fusion | flops 1078198272 | bytes 1056768 | tf_op jit(solution)/shard_map/dot_general | solution.py:297
  20.4 0.9 fusion.13
  21.3 0.2 collective-permute-start.1
  21.5 19.7 %collective-permute-done.1 = bf16[64,8,768]{2,1,0:T(8,128)(2,1)S(1)} collective-permute-done((bf16[64,8,768]{2,1,0:T(8,128)(2,1)}, bf16[64,8,768]{2,1,0:T(8,128)(2,1)S(1)}, u32[]{:S(2)}, u32[]{:S(2)}) %collective-permute-start.1) | collective-permute-done | bytes 786464 | tf_op jit(solution)/shard_map/ppermute | solution.py:29
  41.1 4.0 %fusion.8 = (f32[64,1,1,8,768]{4,3,2,1,0:T(8,128)}, bf16[64,8,768]{2,1,0:T(8,128)(2,1)S(1)}) fusion(bf16[64,8,768]{2,1,0:T(8,128)(2,1)S(1)} %collective-permute-done.1, f32[64,1,1,8,768]{4,3,2,1,0:T(8,128)} %param.10, bf16[64,2,8,768]{3,2,0,1:T(8,128)(2,1)S(1)} %collective-permute-done, s32[]{:T(128)S(6)} %select_n.288, ...), kind=kLoop, calls=%fused_computation.21 | loop fusion | flops 5111808 | bytes 7864332
  45.1 18.7 %all_to_all.5 = bf16[16,8,3072]{2,1,0:T(8,128)(2,1)S(1)} all-to-all(bf16[16,8,3072]{2,1,0:T(8,128)(2,1)S(1)} %bitcast.167), channel_id=1, replica_groups=mesh['z_lo'=2,'core'=2,'y'=4,'x'=4,'z_hi'=4] {'y','x'}, dimensions={0} | all-to-all | bytes 1572864 | tf_op jit(solution)/shard_map/all_to_all | solution.py:311
  63.9 3.1 %collective-permute-start.2 = (bf16[128,3072]{1,0:T(8,128)(2,1)S(1)}, bf16[128,3072]{1,0:T(8,128)(2,1)S(1)}, u32[]{:S(2)}, u32[]{:S(2)}) collective-permute-start(bf16[128,3072]{1,0:T(8,128)(2,1)S(1)} %bitcast.161), channel_id=1, source_target_pairs={{0,128},{128,1},{1,129},{129,2},{2,130},{130,3},{3,131},{131,0},{4... | collective-permute-start | bytes 2359304 | tf_op jit(solution)/shard_map/ppermute | solution.py:315
  67.0 15.1 %collective-permute-done.2.refs_0_ = bf16[128,3072]{1,0:T(8,128)(2,1)S(1)} collective-permute-done((bf16[128,3072]{1,0:T(8,128)(2,1)S(1)}, bf16[128,3072]{1,0:T(8,128)(2,1)S(1)}, u32[]{:S(2)}, u32[]{:S(2)}) %collective-permute-start.2) | collective-permute-done | bytes 786464 | tf_op jit(solution)/shard_map/ppermute | solution.py:315
  82.2 3.7 %collective-permute-start.4 = (bf16[128,3072]{1,0:T(8,128)(2,1)S(1)}, bf16[128,3072]{1,0:T(8,128)(2,1)}, u32[]{:S(2)}, u32[]{:S(2)}) collective-permute-start(bf16[128,3072]{1,0:T(8,128)(2,1)S(1)} %collective-permute-done.2.refs_0_), channel_id=1, source_target_pairs={{0,128},{128,1},{1,129},{129,2},{2,130},{130,3},{3,131},{131,0},{4... | collective-permute-start | bytes 2359304 | tf_op jit(solution)/shard_map/ppermute | solution.py:315
  85.9 1.7 pad_maximum_fusion
  87.5 12.7 %collective-permute-done.4.refs_3_ = bf16[128,3072]{1,0:T(8,128)(2,1)} collective-permute-done((bf16[128,3072]{1,0:T(8,128)(2,1)S(1)}, bf16[128,3072]{1,0:T(8,128)(2,1)}, u32[]{:S(2)}, u32[]{:S(2)}) %collective-permute-start.4) | collective-permute-done | bytes 786464 | tf_op jit(solution)/shard_map/ppermute | solution.py:315
  100.2 3.8 %collective-permute-start.6 = (bf16[128,3072]{1,0:T(8,128)(2,1)}, bf16[128,3072]{1,0:T(8,128)(2,1)S(1)}, u32[]{:S(2)}, u32[]{:S(2)}) collective-permute-start(bf16[128,3072]{1,0:T(8,128)(2,1)} %collective-permute-done.4.refs_3_), channel_id=1, source_target_pairs={{0,128},{128,1},{1,129},{129,2},{2,130},{130,3},{3,131},{131,0},{4... | collective-permute-start | bytes 2359304 | tf_op jit(solution)/shard_map/ppermute | solution.py:315
  104.0 0.5 collective-permute-start.12
  104.5 13.5 %shard_map.103 = (bf16[4,384,2048]{2,1,0:T(8,128)(2,1)}, bf16[2048,384]{1,0:T(8,128)(2,1)S(1)}) custom-call(s32[1]{0:T(128)} %bitcast.1.where_ref, bf16[2048,2176]{1,0:T(8,128)(2,1)} %all-gather.2.cloned.1.call-done.row_ref), custom_call_target="tpu_custom_call" | custom-call | flops 1610612736 | bytes 15204352 | tf_op jit(solution)/shard_map/pallas_call | solution.py:104
  118.0 3.2 %collective-permute-done.7.refs_1_ = bf16[128,3072]{1,0:T(8,128)(2,1)} collective-permute-done((bf16[128,3072]{1,0:T(8,128)(2,1)}, bf16[128,3072]{1,0:T(8,128)(2,1)}, u32[]{:S(2)}, u32[]{:S(2)}) %collective-permute-start.7) | collective-permute-done | bytes 786464 | tf_op jit(solution)/shard_map/ppermute | solution.py:315
  121.2 0.3 collective-permute-start.8
  121.4 1.0 slice.135
  122.4 1.9 collective-permute-start.9
  124.4 0.5 collective-permute-start.14
  124.9 5.0 %collective-permute-done.8.refs_7_ = bf16[64,3072]{1,0:T(8,128)(2,1)S(1)} collective-permute-done((bf16[64,3072]{1,0:T(8,128)(2,1)S(1)}, bf16[64,3072]{1,0:T(8,128)(2,1)S(1)}, u32[]{:S(2)}, u32[]{:S(2)}) %collective-permute-start.8) | collective-permute-done | bytes 393248 | tf_op jit(solution)/shard_map/ppermute | solution.py:315
  129.9 4.6 %collective-permute-done.9.refs_8_ = bf16[64,3072]{1,0:T(8,128)(2,1)} collective-permute-done((bf16[64,3072]{1,0:T(8,128)(2,1)S(1)}, bf16[64,3072]{1,0:T(8,128)(2,1)}, u32[]{:S(2)}, u32[]{:S(2)}) %collective-permute-start.9) | collective-permute-done | bytes 393248 | tf_op jit(solution)/shard_map/ppermute | solution.py:315
  134.5 2.0 %collective-permute-done.16.refs_15_ = bf16[64,3072]{1,0:T(8,128)(2,1)} collective-permute-done((bf16[64,3072]{1,0:T(8,128)(2,1)}, bf16[64,3072]{1,0:T(8,128)(2,1)}, u32[]{:S(2)}, u32[]{:S(2)}) %collective-permute-start.16) | collective-permute-done | bytes 393248 | tf_op jit(solution)/shard_map/ppermute | solution.py:29
  136.6 1.1 copy-done.3
  137.7 1.1 copy-done.5
  138.8 8.9 %shard_map.105 = (bf16[4,384,768]{2,1,0:T(8,128)(2,1)S(1)}, bf16[2048,768]{1,0:T(8,128)(2,1)S(1)}) custom-call(s32[1]{0:T(128)} %bitcast.which_ref, bf16[4,384,2048]{2,1,0:T(8,128)(2,1)} %get-tuple-element.15.packed_ref, bf16[128,3072]{1,0:T(8,128)(2,1)S(1)} %copy-done.3, bf16[128,3072]{1,0:T(8,128)(2,1)S(1)} %bitcast.164, bf16[128,3072]{1,0:T(8,128)(2,1)S(1)} %copy-done.5, ...), custom_call_target="tpu_custom_call" | custom-call | flops 4831838208 | bytes 21233664 | tf_op jit(solution)/shard_map/pallas_call | solution.py:159
  147.7 0.4 shard_map.106.first_ref
  148.2 0.4 shard_map.107.first_ref
  148.7 1.9 shard_map.108.first_ref
  150.5 1.4 collective-permute-start.18
  151.9 1.9 collective-permute-start.20
  153.9 0.1 convert.61
  154.0 2.3 %shard_map.109 = f32[3,512,384]{2,1,0:T(8,128)S(1)} custom-call(s32[3]{0:T(128)S(1)} %get-tuple-element.57.where_ref, bf16[4,4,128,384]{3,2,1,0:T(8,128)(2,1)S(1)} %bitcast.158, bf16[4,4,2,48,768]{4,3,2,1,0:T(8,128)(2,1)S(1)} %bitcast.160, f32[3,512,384]{2,1,0:T(8,128)S(1)} %shard_map.108.first_ref), custom_call_target="tpu_custom_call" | custom-call | flops 452984832 | bytes 3538944 | tf_op jit(solution)/shard_map/pallas_call | solution.py:226
  156.3 0.1 convert.58
  156.5 0.3 collective-permute-start.17
  156.7 3.0 %collective-permute-start.25 = (bf16[256,384]{1,0:T(8,128)(2,1)S(1)}, bf16[256,384]{1,0:T(8,128)(2,1)S(1)}, u32[]{:S(2)}, u32[]{:S(2)}) collective-permute-start(bf16[256,384]{1,0:T(8,128)(2,1)S(1)} %get-tuple-element.50), channel_id=1, source_target_pairs={{0,4},{4,8},{8,12},{12,0},{1,5},{5,9},{9,13},{13,1},{2,6},{6,10},{... | collective-permute-start | bytes 589832 | tf_op jit(solution)/shard_map/ppermute | solution.py:49
  159.8 0.1 fusion.19
  160.0 0.2 collective-permute-start.19
  160.2 3.2 %collective-permute-start.21 = (bf16[512,384]{1,0:T(8,128)(2,1)S(1)}, bf16[512,384]{1,0:T(8,128)(2,1)S(1)}, u32[]{:S(2)}, u32[]{:S(2)}) collective-permute-start(bf16[512,384]{1,0:T(8,128)(2,1)S(1)} %pad_maximum_fusion.3), channel_id=1, source_target_pairs={{0,48},{16,0},{32,16},{48,32},{1,49},{17,1},{33,17},{49,33},{2,50}... | collective-permute-start | bytes 1179656 | tf_op jit(solution)/shard_map/ppermute | solution.py:58
  163.4 0.7 collective-permute-done.17
  164.3 3.0 %collective-permute-start.26 = (bf16[512,384]{1,0:T(8,128)(2,1)S(1)}, bf16[512,384]{1,0:T(8,128)(2,1)S(1)}, u32[]{:S(2)}, u32[]{:S(2)}) collective-permute-start(bf16[512,384]{1,0:T(8,128)(2,1)S(1)} %pad_maximum_fusion.4), channel_id=1, source_target_pairs={{0,4},{4,8},{8,12},{12,0},{1,5},{5,9},{9,13},{13,1},{2,6},{6,10},{... | collective-permute-start | bytes 1179656 | tf_op jit(solution)/shard_map/ppermute | solution.py:57
  167.4 0.2 fusion.87
  167.7 0.5 maximum_select_fusion
  168.7 0.2 dynamic-slice_bitcast_fusion
  168.9 2.0 %copy.63 = bf16[16,8,2,8,768]{4,3,2,1,0:T(8,128)(2,1)} copy(bf16[16,8,2,8,768]{4,3,0,1,2:T(8,128)(2,1)S(1)} %dynamic-slice_bitcast_fusion) | data formatting | bytes 6291456 | tf_op jit(solution)/shard_map/transpose | solution.py:366
  170.9 0.4 collective-permute-done.19
  171.3 0.1 fusion.12
  171.5 1.8 collective-permute-start.22
  173.3 1.2 collective-permute-start.23
  174.5 0.8 collective-permute-start.24
  175.3 2.1 %collective-permute-done.26 = bf16[512,384]{1,0:T(8,128)(2,1)S(1)} collective-permute-done((bf16[512,384]{1,0:T(8,128)(2,1)S(1)}, bf16[512,384]{1,0:T(8,128)(2,1)S(1)}, u32[]{:S(2)}, u32[]{:S(2)}) %collective-permute-start.26) | collective-permute-done | bytes 393248 | tf_op jit(solution)/shard_map/ppermute | solution.py:57
  177.4 3.5 %collective-permute-done.27 = bf16[512,384]{1,0:T(8,128)(2,1)S(1)} collective-permute-done((bf16[512,384]{1,0:T(8,128)(2,1)S(1)}, bf16[512,384]{1,0:T(8,128)(2,1)S(1)}, u32[]{:S(2)}, u32[]{:S(2)}) %collective-permute-start.27) | collective-permute-done | bytes 393248 | tf_op jit(solution)/shard_map/ppermute | solution.py:58
  180.9 0.1 fusion.10
  181.1 0.8 collective-permute-start.28
  181.9 0.6 collective-permute-start.29
  182.4 2.7 %collective-permute-start.30 = (bf16[128,384]{1,0:T(8,128)(2,1)S(1)}, bf16[128,384]{1,0:T(8,128)(2,1)S(1)}, u32[]{:S(2)}, u32[]{:S(2)}) collective-permute-start(bf16[128,384]{1,0:T(8,128)(2,1)S(1)} %get-tuple-element.46), channel_id=1, source_target_pairs={{0,48},{16,0},{32,16},{48,32},{1,49},{17,1},{33,17},{49,33},{2,50}... | collective-permute-start | bytes 294920 | tf_op jit(solution)/shard_map/ppermute | solution.py:339
  185.2 2.2 %collective-permute-done.28 = bf16[128,384]{1,0:T(8,128)(2,1)S(1)} collective-permute-done((bf16[128,384]{1,0:T(8,128)(2,1)S(1)}, bf16[128,384]{1,0:T(8,128)(2,1)S(1)}, u32[]{:S(2)}, u32[]{:S(2)}) %collective-permute-start.28) | collective-permute-done | bytes 98336 | tf_op jit(solution)/shard_map/ppermute | solution.py:337
  187.3 1.0 collective-permute-done.29
  188.4 0.7 pad_maximum_fusion.5
  (90 shorter events, 2.0 us)
Async XLA Ops:
  7.2 9.7 %copy-start = (bf16[4,32,2048]{2,1,0:T(8,128)(2,1)S(1)}, bf16[4,32,2048]{2,1,0:T(8,128)(2,1)}, u32[]{:S(2)}) copy-start(bf16[4,32,2048]{2,1,0:T(8,128)(2,1)} %param.11) | copy-start | bytes 1572868
  7.2 8.6 %copy-start.6 = (s32[4,32,8]{1,2,0:T(8,128)S(1)}, s32[4,32,8]{1,2,0:T(8,128)}, u32[]{:S(2)}) copy-start(s32[4,32,8]{1,2,0:T(8,128)} %param.12) | copy-start | bytes 12292
  7.2 9.3 %copy-start.7 = (f32[4,32,8]{1,2,0:T(8,128)S(1)}, f32[4,32,8]{1,2,0:T(8,128)}, u32[]{:S(2)}) copy-start(f32[4,32,8]{1,2,0:T(8,128)} %param.13) | copy-start | bytes 12292
  7.2 97.3 %all-gather.2.cloned.1.call-start = ((), (), s32[]{:S(2)}) async-start(), calls=%async_computation.1 | async-start | bytes 9469952 | tf_op jit(solution)/shard_map/all_gather | solution.py:303
  10.0 3.6 %collective-permute-start = (bf16[64,2,8,768]{3,2,0,1:T(8,128)(2,1)}, bf16[64,2,8,768]{3,2,0,1:T(8,128)(2,1)S(1)}, u32[]{:S(2)}, u32[]{:S(2)}) collective-permute-start(bf16[64,2,8,768]{3,2,0,1:T(8,128)(2,1)} %copy_bitcast_fusion), channel_id=1, source_target_pairs={{0,64},{64,0},{1,65},{65,1},{2,66},{66,2},{3,67},{67,3},{4,68},{68... | collective-permute-start | bytes 4718600 | tf_op jit(solution)/shard_map/ppermute | solution.py:29
  21.3 19.9 %collective-permute-start.1 = (bf16[64,8,768]{2,1,0:T(8,128)(2,1)}, bf16[64,8,768]{2,1,0:T(8,128)(2,1)S(1)}, u32[]{:S(2)}, u32[]{:S(2)}) collective-permute-start(bf16[64,8,768]{2,1,0:T(8,128)(2,1)} %fusion.5), channel_id=1, source_target_pairs={{0,128},{128,0},{1,129},{129,1},{2,130},{130,2},{3,131},{131,3},{4... | collective-permute-start | bytes 2359304 | tf_op jit(solution)/shard_map/ppermute | solution.py:29
  63.9 18.3 %collective-permute-start.2 = (bf16[128,3072]{1,0:T(8,128)(2,1)S(1)}, bf16[128,3072]{1,0:T(8,128)(2,1)S(1)}, u32[]{:S(2)}, u32[]{:S(2)}) collective-permute-start(bf16[128,3072]{1,0:T(8,128)(2,1)S(1)} %bitcast.161), channel_id=1, source_target_pairs={{0,128},{128,1},{1,129},{129,2},{2,130},{130,3},{3,131},{131,0},{4... | collective-permute-start | bytes 2359304 | tf_op jit(solution)/shard_map/ppermute | solution.py:315
  67.0 18.8 %collective-permute-start.3 = (bf16[128,3072]{1,0:T(8,128)(2,1)S(1)}, bf16[128,3072]{1,0:T(8,128)(2,1)S(1)}, u32[]{:S(2)}, u32[]{:S(2)}) collective-permute-start(bf16[128,3072]{1,0:T(8,128)(2,1)S(1)} %bitcast.162), channel_id=1, source_target_pairs={{128,0},{1,128},{129,1},{2,129},{130,2},{3,130},{131,3},{0,131},{1... | collective-permute-start | bytes 2359304 | tf_op jit(solution)/shard_map/ppermute | solution.py:315
  82.2 5.4 %copy-start.2 = (bf16[128,3072]{1,0:T(8,128)(2,1)}, bf16[128,3072]{1,0:T(8,128)(2,1)S(1)}, u32[]{:S(2)}) copy-start(bf16[128,3072]{1,0:T(8,128)(2,1)S(1)} %collective-permute-done.2.refs_0_) | copy-start | bytes 2359300
  82.2 18.0 %collective-permute-start.4 = (bf16[128,3072]{1,0:T(8,128)(2,1)S(1)}, bf16[128,3072]{1,0:T(8,128)(2,1)}, u32[]{:S(2)}, u32[]{:S(2)}) collective-permute-start(bf16[128,3072]{1,0:T(8,128)(2,1)S(1)} %collective-permute-done.2.refs_0_), channel_id=1, source_target_pairs={{0,128},{128,1},{1,129},{129,2},{2,130},{130,3},{3,131},{131,0},{4... | collective-permute-start | bytes 2359304 | tf_op jit(solution)/shard_map/ppermute | solution.py:315
  85.9 14.3 %copy-start.4 = (bf16[128,3072]{1,0:T(8,128)(2,1)}, bf16[128,3072]{1,0:T(8,128)(2,1)S(1)}, u32[]{:S(2)}) copy-start(bf16[128,3072]{1,0:T(8,128)(2,1)S(1)} %collective-permute-done.3.refs_2_) | copy-start | bytes 2359300
  85.9 18.1 %collective-permute-start.5 = (bf16[128,3072]{1,0:T(8,128)(2,1)S(1)}, bf16[128,3072]{1,0:T(8,128)(2,1)}, u32[]{:S(2)}, u32[]{:S(2)}) collective-permute-start(bf16[128,3072]{1,0:T(8,128)(2,1)S(1)} %collective-permute-done.3.refs_2_), channel_id=1, source_target_pairs={{128,0},{1,128},{129,1},{2,129},{130,2},{3,130},{131,3},{0,131},{1... | collective-permute-start | bytes 2359304 | tf_op jit(solution)/shard_map/ppermute | solution.py:315
  87.5 47.0 %collective-permute-start.10 = (bf16[384,3072]{1,0:T(8,128)(2,1)}, bf16[384,3072]{1,0:T(8,128)(2,1)}, u32[]{:S(2)}, u32[]{:S(2)}) collective-permute-start(bf16[384,3072]{1,0:T(8,128)(2,1)} %pad_maximum_fusion), channel_id=1, source_target_pairs={{0,64},{64,0},{1,65},{65,1},{2,66},{66,2},{3,67},{67,3},{4,68},{68... | collective-permute-start | bytes 7077896 | tf_op jit(solution)/shard_map/ppermute | solution.py:29
  100.2 17.8 %collective-permute-start.6 = (bf16[128,3072]{1,0:T(8,128)(2,1)}, bf16[128,3072]{1,0:T(8,128)(2,1)S(1)}, u32[]{:S(2)}, u32[]{:S(2)}) collective-permute-start(bf16[128,3072]{1,0:T(8,128)(2,1)} %collective-permute-done.4.refs_3_), channel_id=1, source_target_pairs={{0,128},{128,1},{1,129},{129,2},{2,130},{130,3},{3,131},{131,0},{4... | collective-permute-start | bytes 2359304 | tf_op jit(solution)/shard_map/ppermute | solution.py:315
  104.0 17.1 %collective-permute-start.7 = (bf16[128,3072]{1,0:T(8,128)(2,1)}, bf16[128,3072]{1,0:T(8,128)(2,1)}, u32[]{:S(2)}, u32[]{:S(2)}) collective-permute-start(bf16[128,3072]{1,0:T(8,128)(2,1)} %collective-permute-done.5.refs_4_), channel_id=1, source_target_pairs={{128,0},{1,128},{129,1},{2,129},{130,2},{3,130},{131,3},{0,131},{1... | collective-permute-start | bytes 2359304 | tf_op jit(solution)/shard_map/ppermute | solution.py:315
  104.0 20.4 %collective-permute-start.11 = (bf16[128,3072]{1,0:T(8,128)(2,1)}, bf16[128,3072]{1,0:T(8,128)(2,1)}, u32[]{:S(2)}, u32[]{:S(2)}) collective-permute-start(bf16[128,3072]{1,0:T(8,128)(2,1)} %collective-permute-done.4.refs_3_), channel_id=1, source_target_pairs={{0,64},{64,0},{1,65},{65,1},{2,66},{66,2},{3,67},{67,3},{4,68},{68... | collective-permute-start | bytes 2359304 | tf_op jit(solution)/shard_map/ppermute | solution.py:29
  104.0 20.4 %collective-permute-start.12 = (bf16[128,3072]{1,0:T(8,128)(2,1)}, bf16[128,3072]{1,0:T(8,128)(2,1)}, u32[]{:S(2)}, u32[]{:S(2)}) collective-permute-start(bf16[128,3072]{1,0:T(8,128)(2,1)} %collective-permute-done.5.refs_4_), channel_id=1, source_target_pairs={{0,64},{64,0},{1,65},{65,1},{2,66},{66,2},{3,67},{67,3},{4,68},{68... | collective-permute-start | bytes 2359304 | tf_op jit(solution)/shard_map/ppermute | solution.py:29
  118.0 16.5 %copy-start.8 = (s32[3]{0:T(128)S(1)}, s32[3]{0:T(128)}, u32[]{:S(2)}) copy-start(s32[3]{0:T(128)} %constant.362.clone) | copy-start | bytes 40
  121.2 8.7 %collective-permute-start.8 = (bf16[64,3072]{1,0:T(8,128)(2,1)S(1)}, bf16[64,3072]{1,0:T(8,128)(2,1)S(1)}, u32[]{:S(2)}, u32[]{:S(2)}) collective-permute-start(bf16[64,3072]{1,0:T(8,128)(2,1)S(1)} %slice.134), channel_id=1, source_target_pairs={{0,128},{128,1},{1,129},{129,2},{2,130},{130,3},{3,131},{131,0},{4... | collective-permute-start | bytes 1179656 | tf_op jit(solution)/shard_map/ppermute | solution.py:315
  122.4 12.1 %collective-permute-start.9 = (bf16[64,3072]{1,0:T(8,128)(2,1)S(1)}, bf16[64,3072]{1,0:T(8,128)(2,1)}, u32[]{:S(2)}, u32[]{:S(2)}) collective-permute-start(bf16[64,3072]{1,0:T(8,128)(2,1)S(1)} %slice.135), channel_id=1, source_target_pairs={{128,0},{1,128},{129,1},{2,129},{130,2},{3,130},{131,3},{0,131},{1... | collective-permute-start | bytes 1179656 | tf_op jit(solution)/shard_map/ppermute | solution.py:315
  124.4 12.2 %collective-permute-start.13 = (bf16[128,3072]{1,0:T(8,128)(2,1)S(1)}, bf16[128,3072]{1,0:T(8,128)(2,1)}, u32[]{:S(2)}, u32[]{:S(2)}) collective-permute-start(bf16[128,3072]{1,0:T(8,128)(2,1)S(1)} %get-tuple-element.17.refs_5_), channel_id=1, source_target_pairs={{0,64},{64,0},{1,65},{65,1},{2,66},{66,2},{3,67},{67,3},{4,68},{68... | collective-permute-start | bytes 2359304 | tf_op jit(solution)/shard_map/ppermute | solution.py:29
  124.4 12.2 %collective-permute-start.14 = (bf16[128,3072]{1,0:T(8,128)(2,1)}, bf16[128,3072]{1,0:T(8,128)(2,1)}, u32[]{:S(2)}, u32[]{:S(2)}) collective-permute-start(bf16[128,3072]{1,0:T(8,128)(2,1)} %get-tuple-element.18.refs_6_), channel_id=1, source_target_pairs={{0,64},{64,0},{1,65},{65,1},{2,66},{66,2},{3,67},{67,3},{4,68},{68... | collective-permute-start | bytes 2359304 | tf_op jit(solution)/shard_map/ppermute | solution.py:29
  129.9 4.6 %collective-permute-start.15 = (bf16[64,3072]{1,0:T(8,128)(2,1)S(1)}, bf16[64,3072]{1,0:T(8,128)(2,1)}, u32[]{:S(2)}, u32[]{:S(2)}) collective-permute-start(bf16[64,3072]{1,0:T(8,128)(2,1)S(1)} %collective-permute-done.8.refs_7_), channel_id=1, source_target_pairs={{0,64},{64,0},{1,65},{65,1},{2,66},{66,2},{3,67},{67,3},{4,68},{68... | collective-permute-start | bytes 1179656 | tf_op jit(solution)/shard_map/ppermute | solution.py:29
  134.5 2.1 %collective-permute-start.16 = (bf16[64,3072]{1,0:T(8,128)(2,1)}, bf16[64,3072]{1,0:T(8,128)(2,1)}, u32[]{:S(2)}, u32[]{:S(2)}) collective-permute-start(bf16[64,3072]{1,0:T(8,128)(2,1)} %collective-permute-done.9.refs_8_), channel_id=1, source_target_pairs={{0,64},{64,0},{1,65},{65,1},{2,66},{66,2},{3,67},{67,3},{4,68},{68... | collective-permute-start | bytes 1179656 | tf_op jit(solution)/shard_map/ppermute | solution.py:29
  136.6 1.1 copy-start.3
  137.7 1.1 copy-start.5
  150.5 9.3 %collective-permute-start.18 = (bf16[256,384]{1,0:T(8,128)(2,1)S(1)}, bf16[256,384]{1,0:T(8,128)(2,1)S(1)}, u32[]{:S(2)}, u32[]{:S(2)}) collective-permute-start(bf16[256,384]{1,0:T(8,128)(2,1)S(1)} %get-tuple-element.48), channel_id=1, source_target_pairs={{0,16},{16,32},{32,48},{48,0},{1,17},{17,33},{33,49},{49,1},{2,18}... | collective-permute-start | bytes 589832 | tf_op jit(solution)/shard_map/ppermute | solution.py:49
  151.9 7.9 %collective-permute-start.20 = (bf16[256,384]{1,0:T(8,128)(2,1)S(1)}, bf16[256,384]{1,0:T(8,128)(2,1)S(1)}, u32[]{:S(2)}, u32[]{:S(2)}) collective-permute-start(bf16[256,384]{1,0:T(8,128)(2,1)S(1)} %get-tuple-element.49), channel_id=1, source_target_pairs={{0,48},{16,0},{32,16},{48,32},{1,49},{17,1},{33,17},{49,33},{2,50}... | collective-permute-start | bytes 589832 | tf_op jit(solution)/shard_map/ppermute | solution.py:50
  156.5 7.7 %collective-permute-start.17 = (bf16[256,384]{1,0:T(8,128)(2,1)S(1)}, bf16[256,384]{1,0:T(8,128)(2,1)S(1)}, u32[]{:S(2)}, u32[]{:S(2)}) collective-permute-start(bf16[256,384]{1,0:T(8,128)(2,1)S(1)} %get-tuple-element.51), channel_id=1, source_target_pairs={{0,12},{4,0},{8,4},{12,8},{1,13},{5,1},{9,5},{13,9},{2,14},{6,2},{... | collective-permute-start | bytes 589832 | tf_op jit(solution)/shard_map/ppermute | solution.py:50
  156.7 7.4 %collective-permute-start.25 = (bf16[256,384]{1,0:T(8,128)(2,1)S(1)}, bf16[256,384]{1,0:T(8,128)(2,1)S(1)}, u32[]{:S(2)}, u32[]{:S(2)}) collective-permute-start(bf16[256,384]{1,0:T(8,128)(2,1)S(1)} %get-tuple-element.50), channel_id=1, source_target_pairs={{0,4},{4,8},{8,12},{12,0},{1,5},{5,9},{9,13},{13,1},{2,6},{6,10},{... | collective-permute-start | bytes 589832 | tf_op jit(solution)/shard_map/ppermute | solution.py:49
  160.0 11.3 %collective-permute-start.19 = (bf16[512,384]{1,0:T(8,128)(2,1)S(1)}, bf16[512,384]{1,0:T(8,128)(2,1)S(1)}, u32[]{:S(2)}, u32[]{:S(2)}) collective-permute-start(bf16[512,384]{1,0:T(8,128)(2,1)S(1)} %pad_maximum_fusion.2), channel_id=1, source_target_pairs={{0,16},{16,32},{32,48},{48,0},{1,17},{17,33},{33,49},{49,1},{2,18}... | collective-permute-start | bytes 1179656 | tf_op jit(solution)/shard_map/ppermute | solution.py:57
  160.2 11.1 %collective-permute-start.21 = (bf16[512,384]{1,0:T(8,128)(2,1)S(1)}, bf16[512,384]{1,0:T(8,128)(2,1)S(1)}, u32[]{:S(2)}, u32[]{:S(2)}) collective-permute-start(bf16[512,384]{1,0:T(8,128)(2,1)S(1)} %pad_maximum_fusion.3), channel_id=1, source_target_pairs={{0,48},{16,0},{32,16},{48,32},{1,49},{17,1},{33,17},{49,33},{2,50}... | collective-permute-start | bytes 1179656 | tf_op jit(solution)/shard_map/ppermute | solution.py:58
  164.3 13.1 %collective-permute-start.26 = (bf16[512,384]{1,0:T(8,128)(2,1)S(1)}, bf16[512,384]{1,0:T(8,128)(2,1)S(1)}, u32[]{:S(2)}, u32[]{:S(2)}) collective-permute-start(bf16[512,384]{1,0:T(8,128)(2,1)S(1)} %pad_maximum_fusion.4), channel_id=1, source_target_pairs={{0,4},{4,8},{8,12},{12,0},{1,5},{5,9},{9,13},{13,1},{2,6},{6,10},{... | collective-permute-start | bytes 1179656 | tf_op jit(solution)/shard_map/ppermute | solution.py:57
  167.3 13.6 %collective-permute-start.27 = (bf16[512,384]{1,0:T(8,128)(2,1)S(1)}, bf16[512,384]{1,0:T(8,128)(2,1)S(1)}, u32[]{:S(2)}, u32[]{:S(2)}) collective-permute-start(bf16[512,384]{1,0:T(8,128)(2,1)S(1)} %pad_maximum_fusion.1.refs_1_), channel_id=1, source_target_pairs={{0,12},{4,0},{8,4},{12,8},{1,13},{5,1},{9,5},{13,9},{2,14},{6,2},{... | collective-permute-start | bytes 1179656 | tf_op jit(solution)/shard_map/ppermute | solution.py:58
  171.3 17.8 %copy-start.1 = (bf16[4,32,2048]{2,1,0:T(8,128)(2,1)S(1)}, bf16[4,32,2048]{2,1,0:T(8,128)(2,1)}, u32[]{:S(2)}) copy-start(bf16[4,32,2048]{2,1,0:T(8,128)(2,1)} %param.11) | copy-start | bytes 1572868
  171.5 10.9 %collective-permute-start.22 = (bf16[128,384]{1,0:T(8,128)(2,1)S(1)}, bf16[128,384]{1,0:T(8,128)(2,1)S(1)}, u32[]{:S(2)}, u32[]{:S(2)}) collective-permute-start(bf16[128,384]{1,0:T(8,128)(2,1)S(1)} %get-tuple-element.42), channel_id=1, source_target_pairs={{0,8},{4,12},{8,0},{12,4},{1,9},{5,13},{9,1},{13,5},{2,10},{6,14},... | collective-permute-start | bytes 294920 | tf_op jit(solution)/shard_map/ppermute | solution.py:337
  173.3 11.8 %collective-permute-start.23 = (bf16[128,384]{1,0:T(8,128)(2,1)S(1)}, bf16[128,384]{1,0:T(8,128)(2,1)S(1)}, u32[]{:S(2)}, u32[]{:S(2)}) collective-permute-start(bf16[128,384]{1,0:T(8,128)(2,1)S(1)} %get-tuple-element.44), channel_id=1, source_target_pairs={{0,4},{4,8},{8,12},{12,0},{1,5},{5,9},{9,13},{13,1},{2,6},{6,10},{... | collective-permute-start | bytes 294920 | tf_op jit(solution)/shard_map/ppermute | solution.py:338
  174.5 10.6 %collective-permute-start.24 = (bf16[128,384]{1,0:T(8,128)(2,1)S(1)}, bf16[128,384]{1,0:T(8,128)(2,1)S(1)}, u32[]{:S(2)}, u32[]{:S(2)}) collective-permute-start(bf16[128,384]{1,0:T(8,128)(2,1)S(1)} %get-tuple-element.43), channel_id=1, source_target_pairs={{0,12},{4,0},{8,4},{12,8},{1,13},{5,1},{9,5},{13,9},{2,14},{6,2},{... | collective-permute-start | bytes 294920 | tf_op jit(solution)/shard_map/ppermute | solution.py:339
  181.1 6.3 %collective-permute-start.28 = (bf16[128,384]{1,0:T(8,128)(2,1)S(1)}, bf16[128,384]{1,0:T(8,128)(2,1)S(1)}, u32[]{:S(2)}, u32[]{:S(2)}) collective-permute-start(bf16[128,384]{1,0:T(8,128)(2,1)S(1)} %get-tuple-element.45), channel_id=1, source_target_pairs={{0,32},{16,48},{32,0},{48,16},{1,33},{17,49},{33,1},{49,17},{2,34}... | collective-permute-start | bytes 294920 | tf_op jit(solution)/shard_map/ppermute | solution.py:337
  181.9 6.5 %collective-permute-start.29 = (bf16[128,384]{1,0:T(8,128)(2,1)S(1)}, bf16[128,384]{1,0:T(8,128)(2,1)S(1)}, u32[]{:S(2)}, u32[]{:S(2)}) collective-permute-start(bf16[128,384]{1,0:T(8,128)(2,1)S(1)} %get-tuple-element.47), channel_id=1, source_target_pairs={{0,16},{16,32},{32,48},{48,0},{1,17},{17,33},{33,49},{49,1},{2,18}... | collective-permute-start | bytes 294920 | tf_op jit(solution)/shard_map/ppermute | solution.py:338
  182.4 5.9 %collective-permute-start.30 = (bf16[128,384]{1,0:T(8,128)(2,1)S(1)}, bf16[128,384]{1,0:T(8,128)(2,1)S(1)}, u32[]{:S(2)}, u32[]{:S(2)}) collective-permute-start(bf16[128,384]{1,0:T(8,128)(2,1)S(1)} %get-tuple-element.46), channel_id=1, source_target_pairs={{0,48},{16,0},{32,16},{48,32},{1,49},{17,1},{33,17},{49,33},{2,50}... | collective-permute-start | bytes 294920 | tf_op jit(solution)/shard_map/ppermute | solution.py:339
Sparse Core Ops, SparseCore 0:
  21.4 79.9 all-gather.1
